TPU v7x, 32 devices: a whole 2x2x4 slice. The times are simulated.
32 devices in a mesh: groups: 2 (over y), rep: 4 (over x, core), tp: 4 (over z).
Axes of the slice: x: 2, y: 2, z: 4, core: 2. Of those that a mesh axis runs over, the one named last changes fastest.
Arguments:
- features: bfloat16 [4096, 8192], P(('groups', 'rep'), 'tp'), parts along dimension 0, may hold values from -6 to 6
- query_weight: bfloat16 [8192, 8192], P(None, 'tp'), may hold values from -0.0625 to 0.0625
- adapter_down: bfloat16 [128, 16, 8192], P('rep', None, 'tp'), may hold values from -0.0625 to 0.0625
- adapter_up: bfloat16 [128, 16, 8192], P('rep', None, 'tp'), may hold values from -1.5 to 1.5
- block_owner: int32 [128, 1], P(('groups', 'rep')), parts along dimension 0, may hold values from 0 to 3; in each aligned block of 16 rows (0 to 15, 16 to 31, ...) at most 8 rows name the same one
- block_slot: int32 [128], P(('groups', 'rep')), parts along dimension 0, may hold values from 0 to 31
Outputs:
- queries: bfloat16 [4096, 8192], P(('groups', 'rep'), 'tp'), parts along dimension 0
There are 2 independent parts, one for each index of `groups`. A program takes and returns all parts, laid end to end along the dimension named above; an argument that names none is the same for every part. Nothing has to cross between parts.
Inputs may be any that keep to these rules, and one draw needn't show every extreme that they name: `block_owner`: among the 16 batches of one index of rep, no owner is named more than 8 times, a bound that some block reaches.
All inputs are finite; a program needn't handle non-finite values.
Results may differ from a plain program's by a relative error of at most 0.004.
Values may be sent and summed in bfloat16 or wider, within the bound.
No kernel may reach another device: no remote copies, remote signals or barrier semaphores. Data moves between devices by JAX's collectives and lax.ppermute only.
A program may use at most 192 MiB of HBM per device.

v0:
```python
import jax
import jax.numpy as jnp
from jax import lax
from jax.sharding import PartitionSpec as P


def on_device(features, query_weight, adapter_down, adapter_up, block_owner, block_slot):
    row_count = features.shape[0]
    out_cols = query_weight.shape[1]
    projected = jnp.dot(
        lax.all_gather(features, "tp", axis=1, tiled=True),
        query_weight,
        preferred_element_type=jnp.float32,
    )
    owners = block_owner[:, 0]
    blocks = owners.shape[0]
    held = adapter_down.shape[0]
    pool_down, pool_up = (
        lax.all_gather(adapter_down, "rep", axis=0, tiled=True),
        lax.all_gather(adapter_up, "rep", axis=0, tiled=True),
    )
    adapter_ids = owners * held + block_slot
    selected_down_weight = jnp.take(pool_down, adapter_ids, axis=0)
    chosen_up = jnp.take(pool_up, adapter_ids, axis=0)
    rows_by_adapter = features.reshape(blocks, row_count // blocks, features.shape[1])
    partial_value = jnp.einsum(
        "qlo,qfo->qlf", rows_by_adapter, selected_down_weight, preferred_element_type=jnp.float32
    )
    down_projected = lax.psum(partial_value, "tp").astype(jnp.bfloat16)
    adapter_term = jnp.einsum(
        "brk,bko->bro", down_projected, chosen_up, preferred_element_type=jnp.float32
    )
    total = projected.reshape(blocks, row_count // blocks, out_cols) + adapter_term
    return total.reshape(row_count, out_cols).astype(jnp.bfloat16)


def solution(mesh):
    placed = (
        P(("groups", "rep"), "tp"),
        P(None, "tp"),
        P("rep", None, "tp"),
        P("rep", None, "tp"),
        P(("groups", "rep"), None),
        P(("groups", "rep")),
    )
    return jax.shard_map(
        on_device, mesh=mesh, in_specs=placed, out_specs=P(("groups", "rep"), "tp"), check_vma=False
    )
```

profile of v0, /device:TPU:0, one launch (start us, length us, event | category | flops | bytes accessed | tf_op | source)
XLA Modules:
  0.0 316.2 jit_solution(14739216037797555919)
XLA Ops:
  6.5 0.0 copy-start.2
  6.5 0.0 copy-start.1
  6.5 0.0 all-gather.6.cloned.1.call-start
  6.5 0.7 all-gather.6.cloned.1.call-update
  7.3 0.0 copy-start
  7.3 0.0 all-gather.8.cloned.1.call-start
  7.3 0.7 all-gather.8.cloned.1.call-update
  8.0 0.0 all-gather.4.cloned.1.call-start
  8.1 0.7 all-gather.4.cloned.1.call-update
  8.8 0.0 copy-done.2
  8.8 0.0 copy-done.1
  8.8 61.1 %all-gather.6.cloned.1.call-done = bf16[128,16,2048]{2,1,0:T(8,128)(2,1)} async-done(((bf16[32,16,2048]{2,1,0:T(8,128)(2,1)}), bf16[128,16,2048]{2,1,0:T(8,128)(2,1)}) %all-gather.6.cloned.1.call-update) | async-done | bytes 8388624 | tf_op jit(solution)/shard_map/all_gather | solution.py:19
  69.9 5.0 %gather_fusion = bf16[16,16,2048]{2,1,0:T(8,128)(2,1)} fusion(bf16[128,16,2048]{2,1,0:T(8,128)(2,1)} %all-gather.6.cloned.1.call-done, s32[1024]{0:T(1024)S(1)} %pad_clamp_fusion), kind=kCustom, calls=%fused_computation.clone | custom fusion | bytes 2097216 | tf_op jit(solution)/shard_map/jit(_take)/gather | solution.py:23
  74.9 54.9 %all-gather.8.cloned.1.call-done = bf16[128,16,2048]{2,1,0:T(8,128)(2,1)} async-done(((bf16[32,16,2048]{2,1,0:T(8,128)(2,1)}), bf16[128,16,2048]{2,1,0:T(8,128)(2,1)}) %all-gather.8.cloned.1.call-update) | async-done | bytes 8388624 | tf_op jit(solution)/shard_map/all_gather | solution.py:20
  129.8 4.0 %gather_fusion.1 = bf16[16,16,2048]{2,1,0:T(8,128)(2,1)S(1)} fusion(bf16[128,16,2048]{2,1,0:T(8,128)(2,1)} %all-gather.8.cloned.1.call-done, s32[1024]{0:T(1024)S(1)} %pad_clamp_fusion), kind=kCustom, calls=%fused_computation.1.clone | custom fusion | bytes 2097216 | tf_op jit(solution)/shard_map/jit(_take)/gather | solution.py:24
  133.8 0.0 copy-done
  133.8 2.0 convolution_bitcast_fusion
  135.8 28.0 %psum.7 = bf16[16,32,16]{1,2,0:T(8,128)(2,1)S(1)} all-reduce(f32[16,32,16]{1,2,0:T(8,128)S(1)} %convolution_bitcast_fusion), channel_id=1, replica_groups=mesh['groups'=2,'rep'=4,'tp'=4] {'tp'}, use_global_device_ids=true, to_apply=%region_0.0 | all-reduce | flops 8192 | bytes 49152 | tf_op jit(solution)/shard_map/psum | solution.py:29
  163.8 120.0 %all-gather.4.cloned.1.call-done = bf16[512,8192]{1,0:T(8,128)(2,1)} async-done(((bf16[512,2048]{1,0:T(8,128)(2,1)}), bf16[512,8192]{1,0:T(8,128)(2,1)}) %all-gather.4.cloned.1.call-update) | async-done | bytes 8388624 | tf_op jit(solution)/shard_map/all_gather | solution.py:11
  283.8 23.8 %fusion.9 = f32[512,2048]{1,0:T(8,128)S(1)} fusion(bf16[512,8192]{1,0:T(8,128)(2,1)} %all-gather.4.cloned.1.call-done, bf16[8192,2048]{1,0:T(8,128)(2,1)} %param.9), kind=kOutput, calls=%fused_computation.17 | convolution fusion | flops 17179869184 | bytes 46137344 | tf_op jit(solution)/shard_map/dot_general | solution.py:10
  307.6 2.1 add_convert_fusion
  (2 shorter events, 0.0 us)
Async XLA Ops:
  6.5 2.2 copy-start.2
  6.5 2.2 copy-start.1
  6.5 63.4 %all-gather.6.cloned.1.call-start = ((), (), s32[]{:S(2)}) async-start(), calls=%async_computation.1 | async-start | bytes 10485760 | tf_op jit(solution)/shard_map/all_gather | solution.py:19
  7.3 126.6 %copy-start = (bf16[512,2048]{1,0:T(8,128)(2,1)S(1)}, bf16[512,2048]{1,0:T(8,128)(2,1)}, u32[]{:S(2)}) copy-start(bf16[512,2048]{1,0:T(8,128)(2,1)} %param.8) | copy-start | bytes 6291460
  7.3 122.5 %all-gather.8.cloned.1.call-start = ((), (), s32[]{:S(2)}) async-start(), calls=%async_computation.2 | async-start | bytes 10485760 | tf_op jit(solution)/shard_map/all_gather | solution.py:20
  8.0 275.8 %all-gather.4.cloned.1.call-start = ((), (), s32[]{:S(2)}) async-start(), calls=%async_computation | async-start | bytes 10485760 | tf_op jit(solution)/shard_map/all_gather | solution.py:11
Sparse Core Ops, SparseCore 0:
  8.9 60.9 all-gather.5
  71.5 58.2 all-gather.7
  131.4 152.3 all-gather.3
where the time goes:
time: 316 us
  waiting for transfers between devices  238 us (75%)
  blocking collectives  28 us (9%)
  matrix products  27.8 us (9%)
  between operations  13.2 us (4%)
  local copies, waits for them, and re-layouts  8.97 us (3%)
    all_gather x1, waiting for transfers between devices, on_device(): lax.all_gather(features, 'tp', axis=1, tiled=True)  120 us
    all_gather x1, waiting for transfers between devices, on_device(): lax.all_gather(adapter_down, 'rep', axis=0, tiled=True)  61.1 us
    all_gather x1, waiting for transfers between devices, on_device(): lax.all_gather(adapter_up, 'rep', axis=0, tiled=True)  54.9 us
    psum x1, blocking collectives, on_device(): down_projected = lax.psum(partial_value, 'tp').astype(jnp.bfloat16)  28 us
    dot_general x1, matrix products, on_device(): jnp.dot(lax.all_gather(features, 'tp', axis=1, tiled=True), query_weight,...  23.8 us
  transfers between devices with their start and end apart: 3, of which 3 were waited for; matrix products, arithmetic and copies ran while one was open for 3% of the time, Pallas kernels for 0%

commit v1 on v0

v1 whole, which is shorter than its diff:
```python
import functools

import jax
import jax.numpy as jnp
from jax import lax
from jax.experimental import pallas as pl
from jax.experimental.pallas import tpu as pltpu
from jax.sharding import PartitionSpec as P

F32 = jnp.float32
BF16 = jnp.bfloat16
PIECES = 2
ANY = pl.BlockSpec(memory_space=pl.ANY)
VMEM = pl.BlockSpec(memory_space=pltpu.VMEM)


def params(mib):
    return pltpu.CompilerParams(vmem_limit_bytes=mib << 20)


def dot(x, w):
    return jnp.dot(x, w, preferred_element_type=F32)


def wanted(block_owner, block_slot, rep):
    owners = block_owner[:, 0]
    blocks = owners.shape[0]
    cap = 2 * blocks // rep
    order = jnp.arange(blocks)
    earlier = (owners[None, :] == owners[:, None]) & (order[None, :] < order[:, None])
    rank = jnp.sum(earlier, axis=1, dtype=jnp.int32)
    source = jnp.bitwise_xor(owners, lax.axis_index("rep"))
    landing = source * cap + rank
    asked = jnp.sum(
        jnp.where(landing[None, :] == jnp.arange(rep * cap)[:, None], block_slot[None, :], 0), axis=1, dtype=jnp.int32
    ).reshape(rep, cap)
    lists = [lax.ppermute(asked[i], "rep", [(r, r ^ i) for r in range(rep)]) for i in range(1, rep)]
    return lists, source, jnp.where(source == 0, block_slot, rank)


def pack_kernel(count, cap, *refs):
    lists, (down, up), outs, sems = refs[:count], refs[count : count + 2], refs[count + 2 : -1], refs[-1]
    copies = []
    for i in range(count):
        for j in range(cap):
            slot = lists[i][j]
            for k, pool in enumerate((down, up)):
                at = k * cap + j
                copies.append(pltpu.make_async_copy(pool.at[slot], outs[i].at[at], sems.at[i, at]))
    for copy in copies:
        copy.start()
    for copy in copies:
        copy.wait()


def pack(lists, down, up):
    count, cap = len(lists), lists[0].shape[0]
    shape = jax.ShapeDtypeStruct((2 * cap,) + down.shape[1:], down.dtype)
    moved = count * 2 * cap * down.shape[1] * down.shape[2] * 4
    return pl.pallas_call(
        functools.partial(pack_kernel, count, cap),
        out_shape=[shape] * count,
        in_specs=[pl.BlockSpec(memory_space=pltpu.SMEM)] * count + [ANY] * 2,
        out_specs=[ANY] * count,
        scratch_shapes=[pltpu.SemaphoreType.DMA((count, 2 * cap))],
        cost_estimate=pl.CostEstimate(flops=0, bytes_accessed=moved, transcendentals=0),
        compiler_params=params(8),
        name="pack_blocks",
    )(*lists, down, up)


def shrink_kernel(rep, cap, source, place, features, down, up, *refs):
    held, (part, chosen_up), (chosen_down, sems) = refs[: rep - 1], refs[rep - 1 : rep + 1], refs[rep + 1 :]
    blocks = source.shape[0]
    rank = down.shape[1]

    def pair(b, i):
        at = place[b]
        one = down.at[at] if i == 0 else held[i - 1].at[at]
        two = up.at[at] if i == 0 else held[i - 1].at[cap + at]
        return (
            pltpu.make_async_copy(one, chosen_down.at[pl.ds(b * rank, rank)], sems.at[0, b]),
            pltpu.make_async_copy(two, chosen_up.at[pl.ds(b * rank, rank)], sems.at[1, b]),
        )

    for b in range(blocks):
        for i in range(rep):

            @pl.when(source[b] == i)
            def _():
                for copy in pair(b, i):
                    copy.start()

    for b in range(blocks):
        for i in range(rep):

            @pl.when(source[b] == i)
            def _():
                for copy in pair(b, i):
                    copy.wait()

    rows = features.shape[0]
    every = lax.dot_general(
        chosen_down[...], features[...], (((1,), (1,)), ((), ())), preferred_element_type=F32
    ).reshape(blocks, rank, rows)
    batch = lax.broadcasted_iota(jnp.int32, every.shape, 2) // (rows // blocks)
    own = batch == lax.broadcasted_iota(jnp.int32, every.shape, 0)
    part[...] = jnp.sum(jnp.where(own, every, 0.0), axis=0)


def shrink(source, place, features, down, up, held):
    blocks, rows = source.shape[0], features.shape[0]
    _, rank, depth = down.shape
    rep = len(held) + 1
    cap = held[0].shape[0] // 2
    return pl.pallas_call(
        functools.partial(shrink_kernel, rep, cap),
        out_shape=[
            jax.ShapeDtypeStruct((rank, rows), F32),
            jax.ShapeDtypeStruct((blocks * rank, depth), BF16),
        ],
        in_specs=[pl.BlockSpec(memory_space=pltpu.SMEM)] * 2 + [VMEM] + [ANY] * (2 + len(held)),
        out_specs=[VMEM, ANY],
        scratch_shapes=[pltpu.VMEM((blocks * rank, depth), BF16), pltpu.SemaphoreType.DMA((2, blocks))],
        cost_estimate=pl.CostEstimate(flops=2 * blocks * rank * rows * depth, bytes_accessed=rows * depth * 2, transcendentals=0),
        compiler_params=params(16),
        name="shrink",
    )(source, place, features, down, up, *held)


def spread(total, blocks):
    rank, rows = total.shape
    tall = jnp.concatenate([total] * blocks, axis=0)
    batch = lax.broadcasted_iota(jnp.int32, tall.shape, 1) // (rows // blocks)
    own = batch == lax.broadcasted_iota(jnp.int32, tall.shape, 0) // rank
    return jnp.where(own, tall, 0.0).astype(BF16)


def add_kernel(pieces, choices, tail, *refs):
    info = refs[0]
    cands = refs[1 : 1 + pieces * choices]
    rest = list(refs[1 + pieces * choices :])
    weight = rest.pop(0)
    acc = rest.pop(0) if tail["acc"] else None
    sums = [rest.pop(0) for _ in range(tail["sums"])]
    up = rest.pop(0) if tail["sums"] else None
    if tail["kept"]:
        rest.pop(0)
    out, x, sems = rest[0], rest[1], rest[2]
    wide = rest[3] if tail["sums"] else None
    step = x.shape[0] // pieces

    def copy(c, i):
        return pltpu.make_async_copy(cands[c * choices + i], x.at[pl.ds(c * step, step)], sems.at[c])

    @pl.when(pl.program_id(0) == 0)
    def _():
        for c in range(pieces):
            for i in range(choices):

                @pl.when(info[0] == i)
                def _():
                    copy(c, i).start()

        if tail["sums"]:
            total = sums[0][...]
            for more in sums[1:]:
                total = total + more[...]
            wide[...] = spread(total, tail["blocks"])
        for c in range(pieces):
            for i in range(choices):

                @pl.when(info[0] == i)
                def _():
                    copy(c, i).wait()

    total = dot(x[...], weight[...])
    if acc is not None:
        total = total + acc[...]
    if tail["sums"]:
        total = total + lax.dot_general(wide[...], up[...], (((0,), (0,)), ((), ())), preferred_element_type=F32)
    out[...] = total.astype(out.dtype)


def add_part(cands, which, part, weight, acc=None, sums=(), up=None, blocks=0, final=None, tile=512):
    pieces, choices = len(cands), len(cands[0])
    step, depth = cands[0][0].shape
    rows, cols = pieces * step, weight.shape[1]
    at = final[0] if final else 0
    out_rows = acc.shape[0] if final else rows
    tail = {"acc": acc is not None, "sums": len(sums), "blocks": blocks, "kept": bool(final and final[1] is not None)}
    args = [jnp.stack([which, part]).astype(jnp.int32)] + [x for piece in cands for x in piece] + [weight]
    specs = [ANY] * (pieces * choices) + [pl.BlockSpec((depth, tile), lambda j, info: (info[1], j))]
    block = pl.BlockSpec((rows, tile), lambda j, info: (at, j))
    aliases = {}
    if acc is not None:
        if not final:
            aliases[len(args)] = 0
        args.append(acc)
        specs.append(block)
    for s in sums:
        args.append(s)
        specs.append(pl.BlockSpec(s.shape, lambda j, info: (0, 0)))
    scratch = [pltpu.VMEM((rows, depth), BF16), pltpu.SemaphoreType.DMA((pieces,))]
    if sums:
        args.append(up)
        specs.append(pl.BlockSpec((up.shape[0], tile), lambda j, info: (0, j)))
        scratch.append(pltpu.VMEM((up.shape[0], rows), BF16))
    if tail["kept"]:
        aliases[len(args)] = 0
        args.append(final[1])
        specs.append(ANY)
    return pl.pallas_call(
        functools.partial(add_kernel, pieces, choices, tail),
        out_shape=jax.ShapeDtypeStruct((out_rows, cols), BF16 if final else F32),
        grid_spec=pltpu.PrefetchScalarGridSpec(
            num_scalar_prefetch=1, grid=(cols // tile,), in_specs=specs, out_specs=block, scratch_shapes=scratch
        ),
        input_output_aliases=aliases,
        cost_estimate=pl.CostEstimate(
            flops=2 * rows * depth * cols, bytes_accessed=2 * depth * cols + 8 * rows * cols, transcendentals=0
        ),
        compiler_params=params(32),
        name="add_part",
    )(*args)


def line_of_four(features, query_weight, part_of_shrink, blocks):
    z = lax.axis_index("tp")
    pick = lambda values: jnp.array(values, jnp.int32)[z]
    pieces = jnp.split(features, PIECES)
    right, left = [(0, 1), (1, 2), (2, 3)], [(1, 0), (2, 1), (3, 2)]
    r1, l1, r2, l2, far = [], [], [], [], []
    for p in pieces:
        r1.append(lax.ppermute(p, "tp", right))
        l1.append(lax.ppermute(p, "tp", left))
    for c in range(PIECES):
        r2.append(lax.ppermute(r1[c], "tp", right[1:]))
        l2.append(lax.ppermute(l1[c], "tp", left[:-1]))
    for c in range(PIECES):
        far.append(lax.ppermute(jnp.where(z == 1, l2[c], r2[c]), "tp", [(1, 0), (2, 3)]))
    acc = add_part([[features]], z * 0, z, query_weight)
    acc = add_part(list(zip(l1, r1)), pick([0, 1, 1, 1]), pick([1, 0, 1, 2]), query_weight, acc)
    mine, up = part_of_shrink
    sums = [mine] + [lax.ppermute(mine, "tp", [(i, (i + d) % 4) for i in range(4)]) for d in (1, 2, 3)]
    acc = add_part(
        list(zip(l1, r2, l2)), pick([2, 0, 0, 1]), pick([2, 2, 3, 1]), query_weight, acc, sums, up, blocks
    )
    out = None
    for c in range(PIECES):
        out = add_part(
            [[l2[c], r2[c], far[c]]], pick([2, 0, 1, 2]), pick([3, 3, 0, 0]), query_weight, acc, final=(c, out)
        )
    return out


def solution(mesh):
    tp, rep = mesh.shape["tp"], mesh.shape["rep"]

    def on_device(features, query_weight, adapter_down, adapter_up, block_owner, block_slot):
        lists, source, place = wanted(block_owner, block_slot, rep)
        packed = pack(lists, adapter_down, adapter_up)
        held = [lax.ppermute(p, "rep", [(r, r ^ (i + 1)) for r in range(rep)]) for i, p in enumerate(packed)]
        mine, up = shrink(source, place, features, adapter_down, adapter_up, held)
        blocks = block_slot.shape[0]
        if tp == 4:
            return line_of_four(features, query_weight, (mine, up), blocks)
        base = dot(lax.all_gather(features, "tp", axis=1, tiled=True), query_weight)
        extra = dot(spread(lax.psum(mine, "tp"), blocks).T, up)
        return (base + extra).astype(BF16)

    placed = (
        P(("groups", "rep"), "tp"),
        P(None, "tp"),
        P("rep", None, "tp"),
        P("rep", None, "tp"),
        P(("groups", "rep"), None),
        P(("groups", "rep")),
    )
    return jax.shard_map(
        on_device, mesh=mesh, in_specs=placed, out_specs=P(("groups", "rep"), "tp"), check_vma=False
    )
```

time: 316 us -> 176 us (0.56)
  waiting for transfers between devices: 238 us -> 71.8 us
  Pallas kernels: 0 us -> 52 us
  starting transfers between devices: 0.08 us -> 37.3 us
  blocking collectives: 28 us -> 0 us
  matrix products: 27.8 us -> 0 us
  between operations: 13.2 us -> 0.26 us
  other arithmetic: 0.02 us -> 7.04 us
    all_gather x3 -> x0, waiting for transfers between devices: 236 us -> none  [the longest x1 120 us: on_device(): lax.all_gather(features, 'tp', axis=1, tiled=True)]
    ppermute x0 -> x19, waiting for transfers between devices: none -> 71.8 us  [the longest x2 27.7 us: line_of_four(): l1.append(lax.ppermute(p, 'tp', left))]
    pallas_call x0 -> x7, Pallas kernels: none -> 52 us  [the longest x5 41.4 us: add_part(): pl.pallas_call(functools.partial(add_kernel, pieces, choices, tail), out_...]
    ppermute x0 -> x19, starting transfers between devices: none -> 37.3 us  [the longest x2 12.1 us: line_of_four(): r1.append(lax.ppermute(p, 'tp', right))]
    psum x1 -> x0, blocking collectives: 28 us -> none  [on_device(): down_projected = lax.psum(partial_value, 'tp').astype(jnp.bfloat16)]
    dot_general x3 -> x0, matrix products: 27.8 us -> none  [the longest x1 23.8 us: on_device(): jnp.dot(lax.all_gather(features, 'tp', axis=1, tiled=True), query_weight,...]
    gather x2 -> x0, local copies, waits for them, and re-layouts: 8.96 us -> none  [the longest x1 4.96 us: on_device(): selected_down_weight = jnp.take(pool_down, adapter_ids, axis=0)]
    another operation x0 -> x4, other arithmetic: none -> 4.08 us  [add_part(): jnp.stack([which, part]).astype(jnp.int32)]
  transfers between devices with their start and end apart: 3 -> 19, of which waited for: 3 -> 8; matrix products, arithmetic and copies ran while one was open for 3% -> 6% of each run, Pallas kernels for 0% -> 26%
where the time goes in v1:
time: 176 us
  waiting for transfers between devices  71.8 us (41%)
  Pallas kernels  52 us (30%)
  starting transfers between devices  37.3 us (21%)
  local copies, waits for them, and re-layouts  7.04 us (4%)
  other arithmetic  7.04 us (4%)
    pallas_call x5, Pallas kernels, add_part(): pl.pallas_call(functools.partial(add_kernel, pieces, choices, tail), out_...  41.4 us
    ppermute x2, waiting for transfers between devices, line_of_four(): l1.append(lax.ppermute(p, 'tp', left))  27.7 us
    ppermute x3, waiting for transfers between devices, on_device(): lax.ppermute(p, 'rep', [(r, r ^ i + 1) for r in range(rep)])  24.3 us
    ppermute x2, waiting for transfers between devices, line_of_four(): l2.append(lax.ppermute(l1[c], 'tp', left[:-1]))  15.8 us
    ppermute x2, starting transfers between devices, line_of_four(): r1.append(lax.ppermute(p, 'tp', right))  12.1 us
    ppermute x3, starting transfers between devices, line_of_four(): lax.ppermute(mine, 'tp', [(i, (i + d) % 4) for i in range(4)])  9.66 us
    pallas_call x1, Pallas kernels, pack(): pl.pallas_call(functools.partial(pack_kernel, count, cap), out_shape=[sha...  5.46 us
    pallas_call x1, Pallas kernels, shrink(): pl.pallas_call(functools.partial(shrink_kernel, rep, cap), out_shape=[jax...  5.16 us
  transfers between devices with their start and end apart: 19, of which 8 were waited for; matrix products, arithmetic and copies ran while one was open for 6% of the time, Pallas kernels for 26%

profile of v1, /device:TPU:0, one launch (start us, length us, event | category | flops | bytes accessed | tf_op | source)
XLA Modules:
  0.0 175.6 jit_solution(6476543996770233414)
XLA Ops:
  0.1 3.3 %fusion.1 = (bf16[256,2048]{1,0:T(8,128)(2,1)}, bf16[256,2048]{1,0:T(8,128)(2,1)}) fusion(bf16[512,2048]{1,0:T(8,128)(2,1)} %features.1), kind=kLoop, calls=%fused_computation.14 | loop fusion | bytes 4194304 | tf_op jit(solution)/shard_map/split | solution.py:231
  4.6 6.6 %collective-permute-start.6 = (bf16[256,2048]{1,0:T(8,128)(2,1)}, bf16[256,2048]{1,0:T(8,128)(2,1)}, u32[]{:S(2)}, u32[]{:S(2)}) collective-permute-start(bf16[256,2048]{1,0:T(8,128)(2,1)} %get-tuple-element.17), channel_id=1, source_target_pairs={{0,1},{1,2},{2,3},{4,5},{5,6},{6,7},{8,9},{9,10},{10,11},{12,13},{... | collective-permute-start | bytes 3145736 | tf_op jit(solution)/shard_map/ppermute | solution.py:235
  12.5 5.5 %collective-permute-start.2 = (bf16[256,2048]{1,0:T(8,128)(2,1)}, bf16[256,2048]{1,0:T(8,128)(2,1)}, u32[]{:S(2)}, u32[]{:S(2)}) collective-permute-start(bf16[256,2048]{1,0:T(8,128)(2,1)} %get-tuple-element.18), channel_id=1, source_target_pairs={{0,1},{1,2},{2,3},{4,5},{5,6},{6,7},{8,9},{9,10},{10,11},{12,13},{... | collective-permute-start | bytes 3145736 | tf_op jit(solution)/shard_map/ppermute | solution.py:235
  18.4 1.9 %collective-permute-start.10 = (s32[8]{0:T(128)S(1)}, s32[8]{0:T(128)S(1)}, u32[]{:S(2)}, u32[]{:S(2)}) collective-permute-start(s32[8]{0:T(128)S(1)} %get-tuple-element.20), channel_id=1, source_target_pairs={{0,8},{4,12},{8,0},{12,4},{1,9},{5,13},{9,1},{13,5},{2,10},{6,14},... | collective-permute-start | bytes 104 | tf_op jit(solution)/shard_map/ppermute | solution.py:37
  22.8 9.8 %collective-permute-done.5.refs_1_ = bf16[256,2048]{1,0:T(8,128)(2,1)} collective-permute-done((bf16[256,2048]{1,0:T(8,128)(2,1)}, bf16[256,2048]{1,0:T(8,128)(2,1)}, u32[]{:S(2)}, u32[]{:S(2)}) %collective-permute-start.5) | collective-permute-done | bytes 1048608 | tf_op jit(solution)/shard_map/ppermute | solution.py:236
  34.1 1.7 collective-permute-start.7
  37.1 17.9 %collective-permute-done.refs_3_.refs_4_ = bf16[256,2048]{1,0:T(8,128)(2,1)} collective-permute-done((bf16[256,2048]{1,0:T(8,128)(2,1)}, bf16[256,2048]{1,0:T(8,128)(2,1)}, u32[]{:S(2)}, u32[]{:S(2)}) %collective-permute-start) | collective-permute-done | bytes 1048608 | tf_op jit(solution)/shard_map/ppermute | solution.py:236
  56.3 1.7 collective-permute-start.3
  60.5 1.4 pad_add_fusion.refs_0_
  61.9 8.2 %add_part.5.refs_6_ = f32[512,2048]{1,0:T(8,128)S(1)} custom-call(s32[2]{0:T(128)S(1)} %pad_add_fusion.3.refs_0_, bf16[512,2048]{1,0:T(8,128)(2,1)S(1)} %copy-done, bf16[8192,2048]{1,0:T(8,128)(2,1)} %refs_4_.5), custom_call_target="tpu_custom_call" | custom-call | flops 4294967296 | bytes 16777216 | tf_op jit(solution)/shard_map/add_part/pallas_call | solution.py:213
  70.1 3.0 %collective-permute-done.11.refs_2_ = s32[8]{0:T(128)S(1)} collective-permute-done((s32[8]{0:T(128)S(1)}, s32[8]{0:T(128)S(1)}, u32[]{:S(2)}, u32[]{:S(2)}) %collective-permute-start.11) | collective-permute-done | bytes 64 | tf_op jit(solution)/shard_map/ppermute | solution.py:37
  74.6 5.5 %pack_blocks.1 = (bf16[16,16,2048]{2,1,0:T(8,128)(2,1)S(1)}, bf16[16,16,2048]{2,1,0:T(8,128)(2,1)S(1)}, bf16[16,16,2048]{2,1,0:T(8,128)(2,1)S(1)}) custom-call(s32[8]{0:T(128)S(1)} %collective-permute-done.9.refs_0_, s32[8]{0:T(128)S(1)} %collective-permute-done.10.refs_1_, s32[8]{0:T(128)S(1)} %collective-permute-done.11.refs_2_, ...), custom_call_target="tpu_custom_call" | custom-call | bytes 6291456 | tf_op jit(solution)/shard_map/pack_blocks/pallas_call | solution.py:60
  80.4 1.5 collective-permute-start.13
  83.3 15.8 %collective-permute-done.1.refs_6_.refs_1_ = bf16[256,2048]{1,0:T(8,128)(2,1)} collective-permute-done((bf16[256,2048]{1,0:T(8,128)(2,1)}, bf16[256,2048]{1,0:T(8,128)(2,1)}, u32[]{:S(2)}, u32[]{:S(2)}) %collective-permute-start.1) | collective-permute-done | bytes 1048608 | tf_op jit(solution)/shard_map/ppermute | solution.py:239
  100.4 1.4 broadcast_select_fusion.1
  103.1 3.3 %collective-permute-done.13.refs_1_ = bf16[16,16,2048]{2,1,0:T(8,128)(2,1)S(1)} collective-permute-done((bf16[16,16,2048]{2,1,0:T(8,128)(2,1)S(1)}, bf16[16,16,2048]{2,1,0:T(8,128)(2,1)S(1)}, u32[]{:S(2)}, u32[]{:S(2)}) %collective-permute-start.13) | collective-permute-done | bytes 1048608 | tf_op jit(solution)/shard_map/ppermute | solution.py:263
  106.4 21.0 %collective-permute-done.14.refs_2_ = bf16[16,16,2048]{2,1,0:T(8,128)(2,1)S(1)} collective-permute-done((bf16[16,16,2048]{2,1,0:T(8,128)(2,1)S(1)}, bf16[16,16,2048]{2,1,0:T(8,128)(2,1)S(1)}, u32[]{:S(2)}, u32[]{:S(2)}) %collective-permute-start.14) | collective-permute-done | bytes 1048608 | tf_op jit(solution)/shard_map/ppermute | solution.py:263
  127.4 5.2 %shrink.1 = (f32[16,512]{1,0:T(8,128)S(1)}, bf16[256,2048]{1,0:T(8,128)(2,1)S(1)}) custom-call(s32[16]{0:T(128)S(1)} %get-tuple-element.16.source, s32[16]{0:T(128)S(1)} %compare_select_fusion.place, bf16[512,2048]{1,0:T(8,128)(2,1)S(1)} %copy-done, bf16[32,16,2048]{2,1,0:T(8,128)(2,1)S(1)} %copy-done.1, bf16[32,16,2048]{2,1,0:T(8,128)(2,1)S(1)} %copy-done.2, ...), custom_call_target="tpu_custom_call" | custom-call | flops 536870912 | bytes 2097152 | tf_op jit(solution)/shard_map/shrink/pallas_call | solution.py:116
  132.6 6.6 %collective-permute-start.15 = (f32[16,512]{1,0:T(8,128)S(1)}, f32[16,512]{1,0:T(8,128)S(1)}, u32[]{:S(2)}, u32[]{:S(2)}) collective-permute-start(f32[16,512]{1,0:T(8,128)S(1)} %get-tuple-element.13.refs_9_), channel_id=1, source_target_pairs={{0,1},{1,2},{2,3},{3,0},{4,5},{5,6},{6,7},{7,4},{8,9},{9,10},{10,1... | collective-permute-start | bytes 98312 | tf_op jit(solution)/shard_map/ppermute | solution.py:245
  139.4 2.8 %collective-permute-start.17 = (f32[16,512]{1,0:T(8,128)S(1)}, f32[16,512]{1,0:T(8,128)S(1)}, u32[]{:S(2)}, u32[]{:S(2)}) collective-permute-start(f32[16,512]{1,0:T(8,128)S(1)} %get-tuple-element.13.refs_9_), channel_id=1, source_target_pairs={{0,3},{1,0},{2,1},{3,2},{4,7},{5,4},{6,5},{7,6},{8,11},{9,8},{10,9... | collective-permute-start | bytes 98312 | tf_op jit(solution)/shard_map/ppermute | solution.py:245
  142.2 9.6 %add_part.6.refs_8_ = f32[512,2048]{1,0:T(8,128)S(1)} custom-call(s32[2]{0:T(128)S(1)} %pad_add_fusion.2.refs_0_, bf16[256,2048]{1,0:T(8,128)(2,1)} %collective-permute-done.5.refs_1_, bf16[256,2048]{1,0:T(8,128)(2,1)} %collective-permute-done.6.refs_2_, bf16[256,2048]{1,0:T(8,128)(2,1)} %collective-permute-done.refs_3_.refs_4_, ...), custom_call_target="tpu_custom_call", output_to_operand_aliasing={{}: (6, {})} | custom-call | flops 4294967296 | bytes 16777216 | tf_op jit(solution)/shard_map/add_part/pallas_call | solution.py:213
  151.8 9.7 %add_part.7.refs_5_ = f32[512,2048]{1,0:T(8,128)S(1)} custom-call(s32[2]{0:T(128)S(1)} %pad_add_fusion.1.refs_0_, bf16[256,2048]{1,0:T(8,128)(2,1)} %collective-permute-done.5.refs_1_, bf16[256,2048]{1,0:T(8,128)(2,1)} %collective-permute-done.7.refs_2_, ...), custom_call_target="tpu_custom_call", output_to_operand_aliasing={{}: (8, {})} | custom-call | flops 4294967296 | bytes 16777216 | tf_op jit(solution)/shard_map/add_part/pallas_call | solution.py:213
  161.6 7.0 %add_part.8.refs_6_ = bf16[512,2048]{1,0:T(8,128)(2,1)} custom-call(s32[2]{0:T(128)S(1)} %pad_add_fusion.refs_0_, bf16[256,2048]{1,0:T(8,128)(2,1)S(1)} %collective-permute-done.8.refs_3_.refs_1_, bf16[256,2048]{1,0:T(8,128)(2,1)} %collective-permute-done.7.refs_2_, bf16[256,2048]{1,0:T(8,128)(2,1)S(1)} %collective-permute-done.18.refs_3_, ...), custom_call_target="tpu_custom_call" | custom-call | flops 2147483648 | bytes 12582912 | tf_op jit(solution)/shard_map/add_part/pallas_call | solution.py:213
  168.6 7.0 %add_part.9 = bf16[512,2048]{1,0:T(8,128)(2,1)} custom-call(s32[2]{0:T(128)S(1)} %pad_add_fusion.refs_0_, bf16[256,2048]{1,0:T(8,128)(2,1)} %collective-permute-done.1.refs_6_.refs_1_, bf16[256,2048]{1,0:T(8,128)(2,1)} %collective-permute-done.3.refs_5_.refs_2_, ...), custom_call_target="tpu_custom_call", output_to_operand_aliasing={{}: (6, {})} | custom-call | flops 2147483648 | bytes 12582912 | tf_op jit(solution)/shard_map/add_part/pallas_call | solution.py:213
  (61 shorter events, 18.2 us)
Async XLA Ops:
  0.0 21.5 %copy-start.8 = (s32[4]{0:T(128)S(1)}, s32[4]{0:T(128)}, u32[]{:S(2)}) copy-start(s32[4]{0:T(128)} %constant.32.clone) | copy-start | bytes 52
  0.0 22.1 %copy-start.7 = (s32[4]{0:T(128)S(1)}, s32[4]{0:T(128)}, u32[]{:S(2)}) copy-start(s32[4]{0:T(128)} %constant.33.clone) | copy-start | bytes 52
  0.0 59.3 %copy-start.6 = (s32[4]{0:T(128)S(1)}, s32[4]{0:T(128)}, u32[]{:S(2)}) copy-start(s32[4]{0:T(128)} %constant.34.clone) | copy-start | bytes 52
  0.0 59.9 %copy-start.5 = (s32[4]{0:T(128)S(1)}, s32[4]{0:T(128)}, u32[]{:S(2)}) copy-start(s32[4]{0:T(128)} %constant.35.clone) | copy-start | bytes 52
  0.0 61.8 %copy-start = (bf16[512,2048]{1,0:T(8,128)(2,1)S(1)}, bf16[512,2048]{1,0:T(8,128)(2,1)}, u32[]{:S(2)}) copy-start(bf16[512,2048]{1,0:T(8,128)(2,1)} %features.1) | copy-start | bytes 6291460
  3.3 29.2 %collective-permute-start.5 = (bf16[256,2048]{1,0:T(8,128)(2,1)}, bf16[256,2048]{1,0:T(8,128)(2,1)}, u32[]{:S(2)}, u32[]{:S(2)}) collective-permute-start(bf16[256,2048]{1,0:T(8,128)(2,1)} %get-tuple-element.17), channel_id=1, source_target_pairs={{1,0},{2,1},{3,2},{5,4},{6,5},{7,6},{9,8},{10,9},{11,10},{13,12},{... | collective-permute-start | bytes 3145736 | tf_op jit(solution)/shard_map/ppermute | solution.py:236
  4.6 29.4 %collective-permute-start.6 = (bf16[256,2048]{1,0:T(8,128)(2,1)}, bf16[256,2048]{1,0:T(8,128)(2,1)}, u32[]{:S(2)}, u32[]{:S(2)}) collective-permute-start(bf16[256,2048]{1,0:T(8,128)(2,1)} %get-tuple-element.17), channel_id=1, source_target_pairs={{0,1},{1,2},{2,3},{4,5},{5,6},{6,7},{8,9},{9,10},{10,11},{12,13},{... | collective-permute-start | bytes 3145736 | tf_op jit(solution)/shard_map/ppermute | solution.py:235
  11.2 43.8 %collective-permute-start = (bf16[256,2048]{1,0:T(8,128)(2,1)}, bf16[256,2048]{1,0:T(8,128)(2,1)}, u32[]{:S(2)}, u32[]{:S(2)}) collective-permute-start(bf16[256,2048]{1,0:T(8,128)(2,1)} %get-tuple-element.18), channel_id=1, source_target_pairs={{1,0},{2,1},{3,2},{5,4},{6,5},{7,6},{9,8},{10,9},{11,10},{13,12},{... | collective-permute-start | bytes 3145736 | tf_op jit(solution)/shard_map/ppermute | solution.py:236
  12.5 43.8 %collective-permute-start.2 = (bf16[256,2048]{1,0:T(8,128)(2,1)}, bf16[256,2048]{1,0:T(8,128)(2,1)}, u32[]{:S(2)}, u32[]{:S(2)}) collective-permute-start(bf16[256,2048]{1,0:T(8,128)(2,1)} %get-tuple-element.18), channel_id=1, source_target_pairs={{0,1},{1,2},{2,3},{4,5},{5,6},{6,7},{8,9},{9,10},{10,11},{12,13},{... | collective-permute-start | bytes 3145736 | tf_op jit(solution)/shard_map/ppermute | solution.py:235
  18.4 51.7 %collective-permute-start.10 = (s32[8]{0:T(128)S(1)}, s32[8]{0:T(128)S(1)}, u32[]{:S(2)}, u32[]{:S(2)}) collective-permute-start(s32[8]{0:T(128)S(1)} %get-tuple-element.20), channel_id=1, source_target_pairs={{0,8},{4,12},{8,0},{12,4},{1,9},{5,13},{9,1},{13,5},{2,10},{6,14},... | collective-permute-start | bytes 104 | tf_op jit(solution)/shard_map/ppermute | solution.py:37
  32.6 47.8 %collective-permute-start.8 = (bf16[256,2048]{1,0:T(8,128)(2,1)}, bf16[256,2048]{1,0:T(8,128)(2,1)S(1)}, u32[]{:S(2)}, u32[]{:S(2)}) collective-permute-start(bf16[256,2048]{1,0:T(8,128)(2,1)} %collective-permute-done.5.refs_1_), channel_id=1, source_target_pairs={{1,0},{2,1},{5,4},{6,5},{9,8},{10,9},{13,12},{14,13},{17,16},{18,1... | collective-permute-start | bytes 3145736 | tf_op jit(solution)/shard_map/ppermute | solution.py:239
  34.1 47.9 %collective-permute-start.7 = (bf16[256,2048]{1,0:T(8,128)(2,1)}, bf16[256,2048]{1,0:T(8,128)(2,1)}, u32[]{:S(2)}, u32[]{:S(2)}) collective-permute-start(bf16[256,2048]{1,0:T(8,128)(2,1)} %collective-permute-done.6.refs_2_), channel_id=1, source_target_pairs={{1,2},{2,3},{5,6},{6,7},{9,10},{10,11},{13,14},{14,15},{17,18},{18... | collective-permute-start | bytes 3145736 | tf_op jit(solution)/shard_map/ppermute | solution.py:238
  55.0 44.1 %collective-permute-start.1 = (bf16[256,2048]{1,0:T(8,128)(2,1)}, bf16[256,2048]{1,0:T(8,128)(2,1)}, u32[]{:S(2)}, u32[]{:S(2)}) collective-permute-start(bf16[256,2048]{1,0:T(8,128)(2,1)} %collective-permute-done.refs_3_.refs_4_), channel_id=1, source_target_pairs={{1,0},{2,1},{5,4},{6,5},{9,8},{10,9},{13,12},{14,13},{17,16},{18,1... | collective-permute-start | bytes 3145736 | tf_op jit(solution)/shard_map/ppermute | solution.py:239
  56.3 44.1 %collective-permute-start.3 = (bf16[256,2048]{1,0:T(8,128)(2,1)}, bf16[256,2048]{1,0:T(8,128)(2,1)}, u32[]{:S(2)}, u32[]{:S(2)}) collective-permute-start(bf16[256,2048]{1,0:T(8,128)(2,1)} %collective-permute-done.2.refs_4_), channel_id=1, source_target_pairs={{1,2},{2,3},{5,6},{6,7},{9,10},{10,11},{13,14},{14,15},{17,18},{18... | collective-permute-start | bytes 3145736 | tf_op jit(solution)/shard_map/ppermute | solution.py:238
  70.1 3.0 %collective-permute-start.11 = (s32[8]{0:T(128)S(1)}, s32[8]{0:T(128)S(1)}, u32[]{:S(2)}, u32[]{:S(2)}) collective-permute-start(s32[8]{0:T(128)S(1)} %get-tuple-element.19), channel_id=1, source_target_pairs={{0,12},{4,8},{8,4},{12,0},{1,13},{5,9},{9,5},{13,1},{2,14},{6,10},... | collective-permute-start | bytes 104 | tf_op jit(solution)/shard_map/ppermute | solution.py:37
  73.1 1.5 collective-permute-start.9
  80.0 23.1 %collective-permute-start.12 = (bf16[16,16,2048]{2,1,0:T(8,128)(2,1)S(1)}, bf16[16,16,2048]{2,1,0:T(8,128)(2,1)S(1)}, u32[]{:S(2)}, u32[]{:S(2)}) collective-permute-start(bf16[16,16,2048]{2,1,0:T(8,128)(2,1)S(1)} %get-tuple-element.10), channel_id=1, source_target_pairs={{0,4},{4,0},{8,12},{12,8},{1,5},{5,1},{9,13},{13,9},{2,6},{6,2},{1... | collective-permute-start | bytes 3145736 | tf_op jit(solution)/shard_map/ppermute | solution.py:263
  80.4 26.0 %collective-permute-start.13 = (bf16[16,16,2048]{2,1,0:T(8,128)(2,1)S(1)}, bf16[16,16,2048]{2,1,0:T(8,128)(2,1)S(1)}, u32[]{:S(2)}, u32[]{:S(2)}) collective-permute-start(bf16[16,16,2048]{2,1,0:T(8,128)(2,1)S(1)} %get-tuple-element.11), channel_id=1, source_target_pairs={{0,8},{4,12},{8,0},{12,4},{1,9},{5,13},{9,1},{13,5},{2,10},{6,14},... | collective-permute-start | bytes 3145736 | tf_op jit(solution)/shard_map/ppermute | solution.py:263
  81.9 45.5 %collective-permute-start.14 = (bf16[16,16,2048]{2,1,0:T(8,128)(2,1)S(1)}, bf16[16,16,2048]{2,1,0:T(8,128)(2,1)S(1)}, u32[]{:S(2)}, u32[]{:S(2)}) collective-permute-start(bf16[16,16,2048]{2,1,0:T(8,128)(2,1)S(1)} %get-tuple-element.12), channel_id=1, source_target_pairs={{0,12},{4,8},{8,4},{12,0},{1,13},{5,9},{9,5},{13,1},{2,14},{6,10},... | collective-permute-start | bytes 3145736 | tf_op jit(solution)/shard_map/ppermute | solution.py:263
  99.1 62.4 %collective-permute-start.18 = (bf16[256,2048]{1,0:T(8,128)(2,1)S(1)}, bf16[256,2048]{1,0:T(8,128)(2,1)S(1)}, u32[]{:S(2)}, u32[]{:S(2)}) collective-permute-start(bf16[256,2048]{1,0:T(8,128)(2,1)S(1)} %broadcast_select_fusion), channel_id=1, source_target_pairs={{1,0},{2,3},{5,4},{6,7},{9,8},{10,11},{13,12},{14,15},{17,16},{18,... | collective-permute-start | bytes 3145736 | tf_op jit(solution)/shard_map/ppermute | solution.py:241
  101.8 66.8 %collective-permute-start.4 = (bf16[256,2048]{1,0:T(8,128)(2,1)S(1)}, bf16[256,2048]{1,0:T(8,128)(2,1)S(1)}, u32[]{:S(2)}, u32[]{:S(2)}) collective-permute-start(bf16[256,2048]{1,0:T(8,128)(2,1)S(1)} %broadcast_select_fusion.1), channel_id=1, source_target_pairs={{1,0},{2,3},{5,4},{6,7},{9,8},{10,11},{13,12},{14,15},{17,16},{18,... | collective-permute-start | bytes 3145736 | tf_op jit(solution)/shard_map/ppermute | solution.py:241
  132.6 19.2 %collective-permute-start.15 = (f32[16,512]{1,0:T(8,128)S(1)}, f32[16,512]{1,0:T(8,128)S(1)}, u32[]{:S(2)}, u32[]{:S(2)}) collective-permute-start(f32[16,512]{1,0:T(8,128)S(1)} %get-tuple-element.13.refs_9_), channel_id=1, source_target_pairs={{0,1},{1,2},{2,3},{3,0},{4,5},{5,6},{6,7},{7,4},{8,9},{9,10},{10,1... | collective-permute-start | bytes 98312 | tf_op jit(solution)/shard_map/ppermute | solution.py:245
  139.2 12.6 %collective-permute-start.16 = (f32[16,512]{1,0:T(8,128)S(1)}, f32[16,512]{1,0:T(8,128)S(1)}, u32[]{:S(2)}, u32[]{:S(2)}) collective-permute-start(f32[16,512]{1,0:T(8,128)S(1)} %get-tuple-element.13.refs_9_), channel_id=1, source_target_pairs={{0,2},{1,3},{2,0},{3,1},{4,6},{5,7},{6,4},{7,5},{8,10},{9,11},{10,... | collective-permute-start | bytes 98312 | tf_op jit(solution)/shard_map/ppermute | solution.py:245
  139.4 12.4 %collective-permute-start.17 = (f32[16,512]{1,0:T(8,128)S(1)}, f32[16,512]{1,0:T(8,128)S(1)}, u32[]{:S(2)}, u32[]{:S(2)}) collective-permute-start(f32[16,512]{1,0:T(8,128)S(1)} %get-tuple-element.13.refs_9_), channel_id=1, source_target_pairs={{0,3},{1,0},{2,1},{3,2},{4,7},{5,4},{6,5},{7,6},{8,11},{9,8},{10,9... | collective-permute-start | bytes 98312 | tf_op jit(solution)/shard_map/ppermute | solution.py:245
  (6 other events, 102.6 us)

commit v2 on v0

v2 whole, which is shorter than its diff:
```python
import functools

import jax
import jax.numpy as jnp
from jax import lax
from jax.experimental import pallas as pl
from jax.experimental.pallas import tpu as pltpu
from jax.sharding import PartitionSpec as P

F32 = jnp.float32
BF16 = jnp.bfloat16
PIECE = (3, 4)
ANY = pl.BlockSpec(memory_space=pl.ANY)
VMEM = pl.BlockSpec(memory_space=pltpu.VMEM)


def params(mib):
    return pltpu.CompilerParams(vmem_limit_bytes=mib << 20)


def dot(x, w):
    return jnp.dot(x, w, preferred_element_type=F32)


def wanted(block_owner, block_slot, rep):
    owners = block_owner[:, 0]
    blocks = owners.shape[0]
    cap = 2 * blocks // rep
    order = jnp.arange(blocks)
    earlier = (owners[None, :] == owners[:, None]) & (order[None, :] < order[:, None])
    rank = jnp.sum(earlier, axis=1, dtype=jnp.int32)
    source = jnp.bitwise_xor(owners, lax.axis_index("rep"))
    landing = source * cap + rank
    asked = jnp.sum(
        jnp.where(landing[None, :] == jnp.arange(rep * cap)[:, None], block_slot[None, :], 0), axis=1, dtype=jnp.int32
    ).reshape(rep, cap)
    return asked, source, jnp.where(source == 0, block_slot, rank)


def swap(x, distance, rep):
    return lax.ppermute(x, "rep", [(r, r ^ distance) for r in range(rep)])


def after(x, *earlier):
    return lax.optimization_barrier((x,) + earlier)[0]


def in_turn(parts, rep):
    got = []
    for i, part in enumerate(parts):
        got.append(swap(after(part, *got[-1:]), i + 1, rep))
    return got


def pack_kernel(count, cap, *refs):
    lists, pool, outs, sems = refs[:count], refs[count], refs[count + 1 : -1], refs[-1]
    copies = []
    for i in range(count):
        for j in range(cap):
            copies.append(pltpu.make_async_copy(pool.at[lists[i][j]], outs[i].at[j], sems.at[i, j]))
    for copy in copies:
        copy.start()
    for copy in copies:
        copy.wait()


def pack(lists, pool):
    count, cap = len(lists), lists[0].shape[0]
    shape = jax.ShapeDtypeStruct((cap,) + pool.shape[1:], pool.dtype)
    moved = count * cap * pool.shape[1] * pool.shape[2] * 4
    return pl.pallas_call(
        functools.partial(pack_kernel, count, cap),
        out_shape=[shape] * count,
        in_specs=[pl.BlockSpec(memory_space=pltpu.SMEM)] * count + [ANY],
        out_specs=[ANY] * count,
        scratch_shapes=[pltpu.SemaphoreType.DMA((count, cap))],
        cost_estimate=pl.CostEstimate(flops=0, bytes_accessed=moved, transcendentals=0),
        compiler_params=params(8),
        name="pack_blocks",
    )(*lists, pool)


def choose(source, place, pool, held, chosen, sems):
    blocks, rank = source.shape[0], pool.shape[1]

    def each(act):
        for b in range(blocks):
            for i in range(len(held) + 1):

                @pl.when(source[b] == i)
                def _():
                    block = (pool if i == 0 else held[i - 1]).at[place[b]]
                    act(pltpu.make_async_copy(block, chosen.at[pl.ds(b * rank, rank)], sems.at[b]))

    each(lambda copy: copy.start())
    each(lambda copy: copy.wait())


def choose_kernel(source, place, pool, *refs):
    choose(source, place, pool, refs[:-2], refs[-2], refs[-1])


def chosen_blocks(source, place, pool, held):
    blocks = source.shape[0]
    _, rank, depth = pool.shape
    return pl.pallas_call(
        choose_kernel,
        out_shape=jax.ShapeDtypeStruct((blocks * rank, depth), pool.dtype),
        in_specs=[pl.BlockSpec(memory_space=pltpu.SMEM)] * 2 + [ANY] * (1 + len(held)),
        out_specs=ANY,
        scratch_shapes=[pltpu.SemaphoreType.DMA((blocks,))],
        cost_estimate=pl.CostEstimate(flops=0, bytes_accessed=blocks * rank * depth * 4, transcendentals=0),
        compiler_params=params(8),
        name="choose_blocks",
    )(source, place, pool, *held)


def shrink_kernel(source, place, features, pool, *refs):
    held, part, chosen, sems = refs[:-3], refs[-3], refs[-2], refs[-1]
    blocks, rank, rows = source.shape[0], pool.shape[1], features.shape[0]
    choose(source, place, pool, held, chosen, sems)
    every = lax.dot_general(
        chosen[...], features[...], (((1,), (1,)), ((), ())), preferred_element_type=F32
    ).reshape(blocks, rank, rows)
    batch = lax.broadcasted_iota(jnp.int32, every.shape, 2) // (rows // blocks)
    own = batch == lax.broadcasted_iota(jnp.int32, every.shape, 0)
    part[...] = jnp.sum(jnp.where(own, every, 0.0), axis=0)


def shrink(source, place, features, down, held):
    blocks, rows = source.shape[0], features.shape[0]
    _, rank, depth = down.shape
    return pl.pallas_call(
        shrink_kernel,
        out_shape=jax.ShapeDtypeStruct((rank, rows), F32),
        in_specs=[pl.BlockSpec(memory_space=pltpu.SMEM)] * 2 + [VMEM] + [ANY] * (1 + len(held)),
        out_specs=VMEM,
        scratch_shapes=[pltpu.VMEM((blocks * rank, depth), BF16), pltpu.SemaphoreType.DMA((blocks,))],
        cost_estimate=pl.CostEstimate(flops=2 * blocks * rank * rows * depth, bytes_accessed=rows * depth * 2, transcendentals=0),
        compiler_params=params(16),
        name="shrink",
    )(source, place, features, down, *held)


def spread(total, blocks):
    rank, rows = total.shape
    tall = jnp.concatenate([total] * blocks, axis=0)
    batch = lax.broadcasted_iota(jnp.int32, tall.shape, 1) // (rows // blocks)
    own = batch == lax.broadcasted_iota(jnp.int32, tall.shape, 0) // rank
    return jnp.where(own, tall, 0.0).astype(BF16)


def add_kernel(choices, tail, *refs):
    info, cands = refs[0], refs[1 : 1 + choices]
    rest = list(refs[1 + choices :])
    weight = rest.pop(0)
    acc = rest.pop(0) if tail["acc"] else None
    sums = [rest.pop(0) for _ in range(tail["sums"])]
    up = rest.pop(0) if sums else None
    if tail["kept"]:
        rest.pop(0)
    out, x, sem = rest[:3]
    wide = rest[3] if sums else None
    which = info[tail["which"]]

    def each(act):
        for i, cand in enumerate(cands):

            @pl.when(which == i)
            def _():
                rows = x.shape[0]
                first = 0 if cand.shape[0] == rows else tail["first"]
                act(pltpu.make_async_copy(cand.at[pl.ds(first, rows)], x, sem))

    @pl.when(pl.program_id(0) == 0)
    def _():
        each(lambda copy: copy.start())
        if sums:
            wide[...] = spread(sum(s[...] for s in sums), tail["blocks"])
        each(lambda copy: copy.wait())

    tile = out.shape[1]
    if weight.shape[1] == tile:
        total = dot(x[...], weight[...])
    else:
        total = dot(x[...], weight[:, pl.ds(pl.multiple_of(pl.program_id(0) * tile, tile), tile)])
    if acc is not None:
        total = total + acc[...]
    if sums:
        total = total + lax.dot_general(wide[...], up[...], (((0,), (0,)), ((), ())), preferred_element_type=F32)
    out[...] = total.astype(out.dtype)


def add_part(info, at, cands, weight, acc=None, sums=(), up=None, blocks=0, final=None, tile=512):
    whole, depth = cands[0].shape
    cols = weight.shape[1]
    first, end, kept = final if final else (0, whole, None)
    rows = end - first
    tail = {
        "acc": acc is not None,
        "blocks": blocks,
        "sums": len(sums),
        "kept": kept is not None,
        "which": at,
        "first": first,
    }
    args = [info, *cands, weight]
    specs = [ANY] * len(cands)
    if final:
        specs.append(VMEM)
    else:
        specs.append(pl.BlockSpec((depth, tile), lambda j, info: (info[at + 1], j)))
    block = pl.BlockSpec((rows, tile), lambda j, info: (first // rows, j))
    aliases = {}
    if acc is not None:
        if not final:
            aliases[len(args)] = 0
        args.append(acc)
        specs.append(block)
    scratch = [pltpu.VMEM((rows, depth), BF16), pltpu.SemaphoreType.DMA]
    if blocks:
        args += [*sums, up]
        specs += [pl.BlockSpec(s.shape, lambda j, info: (0, 0)) for s in sums]
        specs.append(pl.BlockSpec((up.shape[0], tile), lambda j, info: (0, j)))
        scratch.append(pltpu.VMEM((up.shape[0], rows), BF16))
    if kept is not None:
        aliases[len(args)] = 0
        args.append(kept)
        specs.append(ANY)
    return pl.pallas_call(
        functools.partial(add_kernel, len(cands), tail),
        out_shape=jax.ShapeDtypeStruct((whole, cols), BF16 if final else F32),
        grid_spec=pltpu.PrefetchScalarGridSpec(
            num_scalar_prefetch=1, grid=(cols // tile,), in_specs=specs, out_specs=block, scratch_shapes=scratch
        ),
        input_output_aliases=aliases,
        cost_estimate=pl.CostEstimate(
            flops=2 * rows * depth * cols, bytes_accessed=2 * depth * cols + 8 * rows * cols, transcendentals=0
        ),
        compiler_params=params(24),
        name="add_part",
    )(*args)


def fetch_kernel(at, info, weight, out, sem):
    depth = out.shape[0]
    copy = pltpu.make_async_copy(weight.at[pl.ds(pl.multiple_of(info[at] * depth, depth), depth)], out, sem)
    copy.start()
    copy.wait()


def fetch_part(info, at, weight, depth):
    return pl.pallas_call(
        functools.partial(fetch_kernel, at),
        out_shape=jax.ShapeDtypeStruct((depth, weight.shape[1]), weight.dtype),
        in_specs=[pl.BlockSpec(memory_space=pltpu.SMEM), ANY],
        out_specs=ANY,
        scratch_shapes=[pltpu.SemaphoreType.DMA],
        cost_estimate=pl.CostEstimate(flops=0, bytes_accessed=4 * depth * weight.shape[1], transcendentals=0),
        compiler_params=params(1),
        name="fetch_part",
    )(info, weight)


CHOICES = (
    (0, 0, 0, 1, 2, 2, 2, 3),
    (0, 1, 1, 0, 0, 2, 0, 3),
    (0, 2, 1, 1, 0, 3, 1, 0),
    (0, 3, 1, 2, 1, 1, 2, 0),
)


def on_line_of_four(features, query_weight, adapter_down, adapter_up, block_owner, block_slot, rep):
    z = lax.axis_index("tp")
    info = lax.dynamic_index_in_dim(jnp.array(CHOICES, jnp.int32), z, 0, keepdims=False)
    right, left = [(0, 1), (1, 2), (2, 3)], [(1, 0), (2, 1), (3, 2)]
    rows, blocks = features.shape[0], block_slot.shape[0]
    cut = rows * PIECE[0] // PIECE[1]

    asked, source, place = wanted(block_owner, block_slot, rep)
    r1, l1 = lax.ppermute(features, "tp", right), lax.ppermute(features, "tp", left)
    lists = in_turn(list(asked[1:]), rep)
    downs = in_turn(pack(lists, adapter_down), rep)
    acc = add_part(after(info, *lists), 0, [features], query_weight)
    packed = pack([after(lists[0], acc)] + lists[1:], adapter_up)
    r2, l2 = lax.ppermute(after(r1, acc, *downs), "tp", right[1:]), lax.ppermute(after(l1, acc, *downs), "tp", left[:-1])
    mine = shrink(after(source, acc, r1, l1), place, features, adapter_down, downs)
    acc = add_part(after(info, mine), 2, [l1, r1], query_weight, acc)
    ups = in_turn([after(packed[0], mine), *packed[1:]], rep)
    up = chosen_blocks(after(source, acc), place, adapter_up, ups)
    ready = after(mine, acc, up)
    shares = [mine] + [lax.ppermute(ready, "tp", [(i, i ^ d) for i in range(4)]) for d in (1, 2, 3)]

    bounds = (0, cut, rows)
    ends = [jnp.where(z == 1, l2[i:j], r2[i:j]) for i, j in zip(bounds, bounds[1:])]
    ends = lax.optimization_barrier((*ends, *shares))[: len(ends)]
    far = [lax.ppermute(end, "tp", [(1, 0), (2, 3)]) for end in ends]
    acc = add_part(info, 4, [l1, r2, l2], query_weight, acc, shares, up, blocks)
    weight = fetch_part(after(info, acc), 7, query_weight, features.shape[1])
    out = add_part(info, 6, [l2, r2, far[0]], weight, acc, final=(0, cut, None))
    return add_part(info, 6, [l2, r2, far[1]], weight, acc, final=(cut, rows, out))


def anywhere(features, query_weight, adapter_down, adapter_up, block_owner, block_slot, rep):
    asked, source, place = wanted(block_owner, block_slot, rep)
    lists = [swap(asked[i], i, rep) for i in range(1, rep)]
    downs = [swap(p, i + 1, rep) for i, p in enumerate(pack(lists, adapter_down))]
    ups = [swap(p, i + 1, rep) for i, p in enumerate(pack(lists, adapter_up))]
    total = lax.psum(shrink(source, place, features, adapter_down, downs), "tp")
    base = dot(lax.all_gather(features, "tp", axis=1, tiled=True), query_weight)
    up = chosen_blocks(source, place, adapter_up, ups)
    return (base + dot(spread(total, block_slot.shape[0]).T, up)).astype(BF16)


def solution(mesh):
    body = on_line_of_four if mesh.shape["tp"] == 4 else anywhere
    placed = (
        P(("groups", "rep"), "tp"),
        P(None, "tp"),
        P("rep", None, "tp"),
        P("rep", None, "tp"),
        P(("groups", "rep"), None),
        P(("groups", "rep")),
    )
    return jax.shard_map(
        functools.partial(body, rep=mesh.shape["rep"]),
        mesh=mesh,
        in_specs=placed,
        out_specs=P(("groups", "rep"), "tp"),
        check_vma=False,
    )
```

time: 316 us -> 160 us (0.51)
  waiting for transfers between devices: 238 us -> 58.1 us
  Pallas kernels: 0 us -> 49.2 us
  blocking collectives: 28 us -> 0 us
  matrix products: 27.8 us -> 0 us
  starting transfers between devices: 0.08 us -> 27.1 us
  between operations: 13.2 us -> 0.22 us
  local copies, waits for them, and re-layouts: 8.97 us -> 19.2 us
  other arithmetic: 0.02 us -> 5.01 us
    all_gather x3 -> x0, waiting for transfers between devices: 236 us -> none  [the longest x1 120 us: on_device(): lax.all_gather(features, 'tp', axis=1, tiled=True)]
    ppermute x0 -> x18, waiting for transfers between devices: none -> 58.1 us  [the longest x9 41.4 us: swap(): return lax.ppermute(x, 'rep', [(r, r ^ distance) for r in range(rep)])]
    pallas_call x0 -> x10, Pallas kernels: none -> 49.2 us  [the longest x5 35.4 us: add_part(): pl.pallas_call(functools.partial(add_kernel, len(cands), tail), out_shape...]
    psum x1 -> x0, blocking collectives: 28 us -> none  [on_device(): down_projected = lax.psum(partial_value, 'tp').astype(jnp.bfloat16)]
    dot_general x3 -> x0, matrix products: 27.8 us -> none  [the longest x1 23.8 us: on_device(): jnp.dot(lax.all_gather(features, 'tp', axis=1, tiled=True), query_weight,...]
    ppermute x0 -> x18, starting transfers between devices: none -> 27.1 us  [the longest x1 6.96 us: on_line_of_four(): lax.ppermute(features, 'tp', right)]
    unnamed x6 -> x22, local copies, waits for them, and re-layouts: 0.01 us -> 18.5 us
    gather x2 -> x0, local copies, waits for them, and re-layouts: 8.96 us -> none  [the longest x1 4.96 us: on_device(): selected_down_weight = jnp.take(pool_down, adapter_ids, axis=0)]
  transfers between devices with their start and end apart: 3 -> 18, of which waited for: 3 -> 13; matrix products, arithmetic and copies ran while one was open for 3% -> 4% of each run, Pallas kernels for 0% -> 29%
where the time goes in v2:
time: 160 us; the launch traced here: 159 us
  waiting for transfers between devices  58.1 us (36%)
  Pallas kernels  49.2 us (31%)
  starting transfers between devices  27.1 us (17%)
  local copies, waits for them, and re-layouts  19.2 us (12%)
  other arithmetic  5.01 us (3%)
    ppermute x9, waiting for transfers between devices, swap(): return lax.ppermute(x, 'rep', [(r, r ^ distance) for r in range(rep)])  41.4 us
    pallas_call x5, Pallas kernels, add_part(): pl.pallas_call(functools.partial(add_kernel, len(cands), tail), out_shape...  35.4 us
    unnamed x22, local copies, waits for them, and re-layouts  18.5 us
    ppermute x2, waiting for transfers between devices, on_line_of_four(): far = [lax.ppermute(end, 'tp', [(1, 0), (2, 3)]) for end in ends]  15.5 us
    ppermute x1, starting transfers between devices, on_line_of_four(): lax.ppermute(features, 'tp', right)  6.96 us
    ppermute x3, starting transfers between devices, on_line_of_four(): lax.ppermute(ready, 'tp', [(i, i ^ d) for i in range(4)])  6.56 us
    ppermute x9, starting transfers between devices, swap(): return lax.ppermute(x, 'rep', [(r, r ^ distance) for r in range(rep)])  6.36 us
    pallas_call x2, Pallas kernels, pack(): pl.pallas_call(functools.partial(pack_kernel, count, cap), out_shape=[sha...  5.85 us
  transfers between devices with their start and end apart: 18, of which 13 were waited for; matrix products, arithmetic and copies ran while one was open for 4% of the time, Pallas kernels for 29%

profile of v2, /device:TPU:0, one launch (start us, length us, event | category | flops | bytes accessed | tf_op | source)
XLA Modules:
  0.0 158.9 jit_solution(6637136633919571937)
XLA Ops:
  1.3 7.0 %collective-permute-start.8 = (bf16[512,2048]{1,0:T(8,128)(2,1)}, bf16[512,2048]{1,0:T(8,128)(2,1)}, u32[]{:S(2)}, u32[]{:S(2)}) collective-permute-start(bf16[512,2048]{1,0:T(8,128)(2,1)} %features.1), channel_id=1, source_target_pairs={{0,1},{1,2},{2,3},{4,5},{5,6},{6,7},{8,9},{9,10},{10,11},{12,13},{... | collective-permute-start | bytes 6291464 | tf_op jit(solution)/shard_map/ppermute | solution.py:281
  11.8 1.9 %collective-permute-start.2 = (s32[8]{0:T(128)S(1)}, s32[8]{0:T(128)S(1)}, u32[]{:S(2)}, u32[]{:S(2)}) collective-permute-start(s32[8]{0:T(128)S(1)} %get-tuple-element.29), channel_id=1, source_target_pairs={{0,8},{4,12},{8,0},{12,4},{1,9},{5,13},{9,1},{13,5},{2,10},{6,14},... | collective-permute-start | bytes 104 | tf_op jit(solution)/shard_map/ppermute | solution.py:41
  16.3 2.0 %collective-permute-done.3.refs_2_ = s32[8]{0:T(128)S(1)} collective-permute-done((s32[8]{0:T(128)S(1)}, s32[8]{0:T(128)S(1)}, u32[]{:S(2)}, u32[]{:S(2)}) %collective-permute-start.3) | collective-permute-done | bytes 64 | tf_op jit(solution)/shard_map/ppermute | solution.py:41
  19.9 2.9 %pack_blocks.2 = (bf16[8,16,2048]{2,1,0:T(8,128)(2,1)S(1)}, bf16[8,16,2048]{2,1,0:T(8,128)(2,1)S(1)}, bf16[8,16,2048]{2,1,0:T(8,128)(2,1)}) custom-call(s32[8]{0:T(128)S(1)} %collective-permute-done.1.refs_0_, s32[8]{0:T(128)S(1)} %collective-permute-done.2.refs_1_, s32[8]{0:T(128)S(1)} %collective-permute-done.3.refs_2_, bf16[32,16,2048]{2,1,0:T(8,128)(2,1)S(1)} %copy-done.5), custom_call_target="tpu_custom_call" | custom-call | bytes 3145728 | tf_op jit(solution)/shard_map/pack_blocks/pallas_call | solution.py:71
  26.7 12.6 %collective-permute-done.5.refs_1_ = bf16[8,16,2048]{2,1,0:T(8,128)(2,1)S(1)} collective-permute-done((bf16[8,16,2048]{2,1,0:T(8,128)(2,1)S(1)}, bf16[8,16,2048]{2,1,0:T(8,128)(2,1)S(1)}, u32[]{:S(2)}, u32[]{:S(2)}) %collective-permute-start.5) | collective-permute-done | bytes 524320 | tf_op jit(solution)/shard_map/ppermute | solution.py:41
  40.4 8.2 %add_part.5.refs_4_ = f32[512,2048]{1,0:T(8,128)S(1)} custom-call(s32[8]{0:T(128)S(1)} %dynamic-slice_bitcast_fusion.refs_0_.info, bf16[512,2048]{1,0:T(8,128)(2,1)S(1)} %copy-done.9, bf16[8192,2048]{1,0:T(8,128)(2,1)} %weight.1), custom_call_target="tpu_custom_call" | custom-call | flops 4294967296 | bytes 16777216 | tf_op jit(solution)/shard_map/add_part/pallas_call | solution.py:230
  48.6 5.2 %collective-permute-done.6.refs_2_ = bf16[8,16,2048]{2,1,0:T(8,128)(2,1)} collective-permute-done((bf16[8,16,2048]{2,1,0:T(8,128)(2,1)}, bf16[8,16,2048]{2,1,0:T(8,128)(2,1)}, u32[]{:S(2)}, u32[]{:S(2)}) %collective-permute-start.6) | collective-permute-done | bytes 524320 | tf_op jit(solution)/shard_map/ppermute | solution.py:41
  55.1 2.1 %collective-permute-start.9 = (bf16[512,2048]{1,0:T(8,128)(2,1)}, bf16[512,2048]{1,0:T(8,128)(2,1)}, u32[]{:S(2)}, u32[]{:S(2)}) collective-permute-start(bf16[512,2048]{1,0:T(8,128)(2,1)} %collective-permute-done.8.refs_2_), channel_id=1, source_target_pairs={{1,2},{2,3},{5,6},{6,7},{9,10},{10,11},{13,14},{14,15},{17,18},{18... | collective-permute-start | bytes 6291464 | tf_op jit(solution)/shard_map/ppermute | solution.py:286
  57.1 2.9 %pack_blocks.3 = (bf16[8,16,2048]{2,1,0:T(8,128)(2,1)S(1)}, bf16[8,16,2048]{2,1,0:T(8,128)(2,1)S(1)}, bf16[8,16,2048]{2,1,0:T(8,128)(2,1)}) custom-call(s32[8]{0:T(128)S(1)} %collective-permute-done.1.refs_0_, s32[8]{0:T(128)S(1)} %collective-permute-done.2.refs_1_, s32[8]{0:T(128)S(1)} %collective-permute-done.3.refs_2_, bf16[32,16,2048]{2,1,0:T(8,128)(2,1)S(1)} %copy-done.7), custom_call_target="tpu_custom_call" | custom-call | bytes 3145728 | tf_op jit(solution)/shard_map/pack_blocks/pallas_call | solution.py:71
  60.1 3.8 %shrink.1.refs_6_ = f32[16,512]{1,0:T(8,128)S(1)} custom-call(s32[16]{0:T(128)S(1)} %get-tuple-element.41.source, s32[16]{0:T(128)S(1)} %get-tuple-element.53.place, bf16[512,2048]{1,0:T(8,128)(2,1)S(1)} %copy-done.10, bf16[32,16,2048]{2,1,0:T(8,128)(2,1)S(1)} %copy-done.6, bf16[8,16,2048]{2,1,0:T(8,128)(2,1)S(1)} %collective-permute-done.4.refs_0_, ...), custom_call_target="tpu_custom_call" | custom-call | flops 536870912 | bytes 2097152 | tf_op jit(solution)/shard_map/shrink/pallas_call | solution.py:133
  66.5 13.4 %collective-permute-done.11.refs_1_ = bf16[8,16,2048]{2,1,0:T(8,128)(2,1)S(1)} collective-permute-done((bf16[8,16,2048]{2,1,0:T(8,128)(2,1)S(1)}, bf16[8,16,2048]{2,1,0:T(8,128)(2,1)S(1)}, u32[]{:S(2)}, u32[]{:S(2)}) %collective-permute-start.11) | collective-permute-done | bytes 524320 | tf_op jit(solution)/shard_map/ppermute | solution.py:41
  79.9 2.2 %copy-done.2 = f32[512,2048]{1,0:T(8,128)S(1)} copy-done((f32[512,2048]{1,0:T(8,128)S(1)}, f32[512,2048]{1,0:T(8,128)}, u32[]{:S(2)}) %copy-start.2) | copy-done | bytes 4194328
  82.1 9.7 %add_part.6.refs_5_ = f32[512,2048]{1,0:T(8,128)S(1)} custom-call(s32[8]{0:T(128)S(1)} %dynamic-slice_bitcast_fusion.refs_0_.info, bf16[512,2048]{1,0:T(8,128)(2,1)} %collective-permute-done.refs_1_, bf16[512,2048]{1,0:T(8,128)(2,1)} %collective-permute-done.8.refs_2_, bf16[8192,2048]{1,0:T(8,128)(2,1)} %weight.1, ...), custom_call_target="tpu_custom_call", output_to_operand_aliasing={{}: (4, {})} | custom-call | flops 4294967296 | bytes 16777216 | tf_op jit(solution)/shard_map/add_part/pallas_call | solution.py:230
  91.7 2.1 %collective-permute-done.12.refs_2_ = bf16[8,16,2048]{2,1,0:T(8,128)(2,1)} collective-permute-done((bf16[8,16,2048]{2,1,0:T(8,128)(2,1)}, bf16[8,16,2048]{2,1,0:T(8,128)(2,1)}, u32[]{:S(2)}, u32[]{:S(2)}) %collective-permute-start.12) | collective-permute-done | bytes 524320 | tf_op jit(solution)/shard_map/ppermute | solution.py:41
  93.9 3.1 %choose_blocks.1.refs_10_ = bf16[256,2048]{1,0:T(8,128)(2,1)S(1)} custom-call(s32[16]{0:T(128)S(1)} %get-tuple-element.41.source, s32[16]{0:T(128)S(1)} %get-tuple-element.53.place, bf16[32,16,2048]{2,1,0:T(8,128)(2,1)S(1)} %copy-done.8, bf16[8,16,2048]{2,1,0:T(8,128)(2,1)S(1)} %collective-permute-done.10.refs_0_, ...), custom_call_target="tpu_custom_call" | custom-call | bytes 2097152 | tf_op jit(solution)/shard_map/choose_blocks/pallas_call | solution.py:106
  97.0 3.2 %collective-permute-start.15 = (f32[16,512]{1,0:T(8,128)S(1)}, f32[16,512]{1,0:T(8,128)S(1)}, u32[]{:S(2)}, u32[]{:S(2)}) collective-permute-start(f32[16,512]{1,0:T(8,128)S(1)} %shrink.1.refs_6_), channel_id=1, source_target_pairs={{0,3},{1,2},{2,1},{3,0},{4,7},{5,6},{6,5},{7,4},{8,11},{9,10},{10,... | collective-permute-start | bytes 98312 | tf_op jit(solution)/shard_map/ppermute | solution.py:292
  100.2 3.4 %collective-permute-start.14 = (f32[16,512]{1,0:T(8,128)S(1)}, f32[16,512]{1,0:T(8,128)S(1)}, u32[]{:S(2)}, u32[]{:S(2)}) collective-permute-start(f32[16,512]{1,0:T(8,128)S(1)} %shrink.1.refs_6_), channel_id=1, source_target_pairs={{0,2},{1,3},{2,0},{3,1},{4,6},{5,7},{6,4},{7,5},{8,10},{9,11},{10,... | collective-permute-start | bytes 98312 | tf_op jit(solution)/shard_map/ppermute | solution.py:292
  110.0 8.4 %add_part.7.refs_5_ = f32[512,2048]{1,0:T(8,128)S(1)} custom-call(s32[8]{0:T(128)S(1)} %dynamic-slice_bitcast_fusion.refs_0_.info, bf16[512,2048]{1,0:T(8,128)(2,1)} %collective-permute-done.refs_1_, bf16[512,2048]{1,0:T(8,128)(2,1)} %collective-permute-done.9.refs_2_, ...), custom_call_target="tpu_custom_call", output_to_operand_aliasing={{}: (5, {})} | custom-call | flops 4294967296 | bytes 16777216 | tf_op jit(solution)/shard_map/add_part/pallas_call | solution.py:230
  118.5 1.9 %copy-done.3 = f32[512,2048]{1,0:T(8,128)} copy-done((f32[512,2048]{1,0:T(8,128)}, f32[512,2048]{1,0:T(8,128)S(1)}, u32[]{:S(2)}) %copy-start.3) | copy-done | bytes 4194328
  120.4 10.5 %copy-done = bf16[8192,2048]{1,0:T(8,128)(2,1)S(1)} copy-done((bf16[8192,2048]{1,0:T(8,128)(2,1)S(1)}, bf16[8192,2048]{1,0:T(8,128)(2,1)}, u32[]{:S(2)}) %copy-start) | copy-done | bytes 33554456
  132.1 14.9 %collective-permute-done.17.refs_3_ = bf16[384,2048]{1,0:T(8,128)(2,1)S(1)} collective-permute-done((bf16[384,2048]{1,0:T(8,128)(2,1)S(1)}, bf16[384,2048]{1,0:T(8,128)(2,1)S(1)}, u32[]{:S(2)}, u32[]{:S(2)}) %collective-permute-start.17) | collective-permute-done | bytes 1572896 | tf_op jit(solution)/shard_map/ppermute | solution.py:297
  147.0 2.2 %copy-done.4 = f32[512,2048]{1,0:T(8,128)S(1)} copy-done((f32[512,2048]{1,0:T(8,128)S(1)}, f32[512,2048]{1,0:T(8,128)}, u32[]{:S(2)}) %copy-start.4) | copy-done | bytes 4194328
  149.2 5.7 %add_part.8.refs_6_ = bf16[512,2048]{1,0:T(8,128)(2,1)} custom-call(s32[8]{0:T(128)S(1)} %dynamic-slice_bitcast_fusion.refs_0_.info, bf16[512,2048]{1,0:T(8,128)(2,1)S(1)} %collective-permute-done.7.refs_3_.refs_1_, bf16[512,2048]{1,0:T(8,128)(2,1)} %collective-permute-done.9.refs_2_, bf16[384,2048]{1,0:T(8,128)(2,1)S(1)} %collective-permute-done.17.refs_3_, ...), custom_call_target="tpu_custom_call" | custom-call | flops 3221225472 | bytes 14680064 | tf_op jit(solution)/shard_map/add_part/pallas_call | solution.py:230
  155.5 3.4 %add_part.9 = bf16[512,2048]{1,0:T(8,128)(2,1)} custom-call(s32[8]{0:T(128)S(1)} %dynamic-slice_bitcast_fusion.refs_0_.info, bf16[512,2048]{1,0:T(8,128)(2,1)S(1)} %collective-permute-done.7.refs_3_.refs_1_, bf16[512,2048]{1,0:T(8,128)(2,1)} %collective-permute-done.9.refs_2_, ...), custom_call_target="tpu_custom_call", output_to_operand_aliasing={{}: (6, {})} | custom-call | flops 1073741824 | bytes 10485760 | tf_op jit(solution)/shard_map/add_part/pallas_call | solution.py:230
  (52 shorter events, 26.0 us)
Async XLA Ops:
  0.0 53.8 %collective-permute-start = (bf16[512,2048]{1,0:T(8,128)(2,1)}, bf16[512,2048]{1,0:T(8,128)(2,1)}, u32[]{:S(2)}, u32[]{:S(2)}) collective-permute-start(bf16[512,2048]{1,0:T(8,128)(2,1)} %features.1), channel_id=1, source_target_pairs={{1,0},{2,1},{3,2},{5,4},{6,5},{7,6},{9,8},{10,9},{11,10},{13,12},{... | collective-permute-start | bytes 6291464 | tf_op jit(solution)/shard_map/ppermute | solution.py:281
  1.3 52.5 %collective-permute-start.8 = (bf16[512,2048]{1,0:T(8,128)(2,1)}, bf16[512,2048]{1,0:T(8,128)(2,1)}, u32[]{:S(2)}, u32[]{:S(2)}) collective-permute-start(bf16[512,2048]{1,0:T(8,128)(2,1)} %features.1), channel_id=1, source_target_pairs={{0,1},{1,2},{2,3},{4,5},{5,6},{6,7},{8,9},{9,10},{10,11},{12,13},{... | collective-permute-start | bytes 6291464 | tf_op jit(solution)/shard_map/ppermute | solution.py:281
  10.7 1.1 collective-permute-start.1
  11.8 3.5 %collective-permute-start.2 = (s32[8]{0:T(128)S(1)}, s32[8]{0:T(128)S(1)}, u32[]{:S(2)}, u32[]{:S(2)}) collective-permute-start(s32[8]{0:T(128)S(1)} %get-tuple-element.29), channel_id=1, source_target_pairs={{0,8},{4,12},{8,0},{12,4},{1,9},{5,13},{9,1},{13,5},{2,10},{6,14},... | collective-permute-start | bytes 104 | tf_op jit(solution)/shard_map/ppermute | solution.py:41
  15.3 3.0 %collective-permute-start.3 = (s32[8]{0:T(128)S(1)}, s32[8]{0:T(128)S(1)}, u32[]{:S(2)}, u32[]{:S(2)}) collective-permute-start(s32[8]{0:T(128)S(1)} %get-tuple-element.30), channel_id=1, source_target_pairs={{0,12},{4,8},{8,4},{12,0},{1,13},{5,9},{9,5},{13,1},{2,14},{6,10},... | collective-permute-start | bytes 104 | tf_op jit(solution)/shard_map/ppermute | solution.py:41
  19.9 20.5 %copy-start.9 = (bf16[512,2048]{1,0:T(8,128)(2,1)S(1)}, bf16[512,2048]{1,0:T(8,128)(2,1)}, u32[]{:S(2)}) copy-start(bf16[512,2048]{1,0:T(8,128)(2,1)} %features.1) | copy-start | bytes 6291460
  22.8 2.3 %collective-permute-start.4 = (bf16[8,16,2048]{2,1,0:T(8,128)(2,1)S(1)}, bf16[8,16,2048]{2,1,0:T(8,128)(2,1)S(1)}, u32[]{:S(2)}, u32[]{:S(2)}) collective-permute-start(bf16[8,16,2048]{2,1,0:T(8,128)(2,1)S(1)} %get-tuple-element.32), channel_id=1, source_target_pairs={{0,4},{4,0},{8,12},{12,8},{1,5},{5,1},{9,13},{13,9},{2,6},{6,2},{1... | collective-permute-start | bytes 1572872 | tf_op jit(solution)/shard_map/ppermute | solution.py:41
  25.1 14.2 %collective-permute-start.5 = (bf16[8,16,2048]{2,1,0:T(8,128)(2,1)S(1)}, bf16[8,16,2048]{2,1,0:T(8,128)(2,1)S(1)}, u32[]{:S(2)}, u32[]{:S(2)}) collective-permute-start(bf16[8,16,2048]{2,1,0:T(8,128)(2,1)S(1)} %get-tuple-element.34), channel_id=1, source_target_pairs={{0,8},{4,12},{8,0},{12,4},{1,9},{5,13},{9,1},{13,5},{2,10},{6,14},... | collective-permute-start | bytes 1572872 | tf_op jit(solution)/shard_map/ppermute | solution.py:41
  39.3 14.5 %collective-permute-start.6 = (bf16[8,16,2048]{2,1,0:T(8,128)(2,1)}, bf16[8,16,2048]{2,1,0:T(8,128)(2,1)}, u32[]{:S(2)}, u32[]{:S(2)}) collective-permute-start(bf16[8,16,2048]{2,1,0:T(8,128)(2,1)} %get-tuple-element.36), channel_id=1, source_target_pairs={{0,12},{4,8},{8,4},{12,0},{1,13},{5,9},{9,5},{13,1},{2,14},{6,10},... | collective-permute-start | bytes 1572872 | tf_op jit(solution)/shard_map/ppermute | solution.py:41
  40.4 16.7 %copy-start.7 = (bf16[32,16,2048]{2,1,0:T(8,128)(2,1)S(1)}, bf16[32,16,2048]{2,1,0:T(8,128)(2,1)}, u32[]{:S(2)}) copy-start(bf16[32,16,2048]{2,1,0:T(8,128)(2,1)} %pool.3) | copy-start | bytes 6291460
  40.4 19.7 %copy-start.10 = (bf16[512,2048]{1,0:T(8,128)(2,1)S(1)}, bf16[512,2048]{1,0:T(8,128)(2,1)}, u32[]{:S(2)}) copy-start(bf16[512,2048]{1,0:T(8,128)(2,1)} %features.1) | copy-start | bytes 6291460
  48.6 15.3 %copy-start.1 = (f32[512,2048]{1,0:T(8,128)}, f32[512,2048]{1,0:T(8,128)S(1)}, u32[]{:S(2)}) copy-start(f32[512,2048]{1,0:T(8,128)S(1)} %add_part.5.refs_4_) | copy-start | bytes 12582916
  48.6 11.5 %copy-start.6 = (bf16[32,16,2048]{2,1,0:T(8,128)(2,1)S(1)}, bf16[32,16,2048]{2,1,0:T(8,128)(2,1)}, u32[]{:S(2)}) copy-start(bf16[32,16,2048]{2,1,0:T(8,128)(2,1)} %pool.2) | copy-start | bytes 6291460
  53.8 50.4 %collective-permute-start.7 = (bf16[512,2048]{1,0:T(8,128)(2,1)}, bf16[512,2048]{1,0:T(8,128)(2,1)S(1)}, u32[]{:S(2)}, u32[]{:S(2)}) collective-permute-start(bf16[512,2048]{1,0:T(8,128)(2,1)} %collective-permute-done.refs_1_), channel_id=1, source_target_pairs={{1,0},{2,1},{5,4},{6,5},{9,8},{10,9},{13,12},{14,13},{17,16},{18,1... | collective-permute-start | bytes 6291464 | tf_op jit(solution)/shard_map/ppermute | solution.py:286
  55.1 49.1 %collective-permute-start.9 = (bf16[512,2048]{1,0:T(8,128)(2,1)}, bf16[512,2048]{1,0:T(8,128)(2,1)}, u32[]{:S(2)}, u32[]{:S(2)}) collective-permute-start(bf16[512,2048]{1,0:T(8,128)(2,1)} %collective-permute-done.8.refs_2_), channel_id=1, source_target_pairs={{1,2},{2,3},{5,6},{6,7},{9,10},{10,11},{13,14},{14,15},{17,18},{18... | collective-permute-start | bytes 6291464 | tf_op jit(solution)/shard_map/ppermute | solution.py:286
  63.9 2.0 %collective-permute-start.10 = (bf16[8,16,2048]{2,1,0:T(8,128)(2,1)S(1)}, bf16[8,16,2048]{2,1,0:T(8,128)(2,1)S(1)}, u32[]{:S(2)}, u32[]{:S(2)}) collective-permute-start(bf16[8,16,2048]{2,1,0:T(8,128)(2,1)S(1)} %get-tuple-element.44), channel_id=1, source_target_pairs={{0,4},{4,0},{8,12},{12,8},{1,5},{5,1},{9,13},{13,9},{2,6},{6,2},{1... | collective-permute-start | bytes 1572872 | tf_op jit(solution)/shard_map/ppermute | solution.py:41
  65.9 14.0 %collective-permute-start.11 = (bf16[8,16,2048]{2,1,0:T(8,128)(2,1)S(1)}, bf16[8,16,2048]{2,1,0:T(8,128)(2,1)S(1)}, u32[]{:S(2)}, u32[]{:S(2)}) collective-permute-start(bf16[8,16,2048]{2,1,0:T(8,128)(2,1)S(1)} %get-tuple-element.46), channel_id=1, source_target_pairs={{0,8},{4,12},{8,0},{12,4},{1,9},{5,13},{9,1},{13,5},{2,10},{6,14},... | collective-permute-start | bytes 1572872 | tf_op jit(solution)/shard_map/ppermute | solution.py:41
  79.9 14.0 %collective-permute-start.12 = (bf16[8,16,2048]{2,1,0:T(8,128)(2,1)}, bf16[8,16,2048]{2,1,0:T(8,128)(2,1)}, u32[]{:S(2)}, u32[]{:S(2)}) collective-permute-start(bf16[8,16,2048]{2,1,0:T(8,128)(2,1)} %get-tuple-element.48), channel_id=1, source_target_pairs={{0,12},{4,8},{8,4},{12,0},{1,13},{5,9},{9,5},{13,1},{2,14},{6,10},... | collective-permute-start | bytes 1572872 | tf_op jit(solution)/shard_map/ppermute | solution.py:41
  82.0 11.8 %copy-start.8 = (bf16[32,16,2048]{2,1,0:T(8,128)(2,1)S(1)}, bf16[32,16,2048]{2,1,0:T(8,128)(2,1)}, u32[]{:S(2)}) copy-start(bf16[32,16,2048]{2,1,0:T(8,128)(2,1)} %pool.3) | copy-start | bytes 6291460
  97.0 9.9 %collective-permute-start.15 = (f32[16,512]{1,0:T(8,128)S(1)}, f32[16,512]{1,0:T(8,128)S(1)}, u32[]{:S(2)}, u32[]{:S(2)}) collective-permute-start(f32[16,512]{1,0:T(8,128)S(1)} %shrink.1.refs_6_), channel_id=1, source_target_pairs={{0,3},{1,2},{2,1},{3,0},{4,7},{5,6},{6,5},{7,4},{8,11},{9,10},{10,... | collective-permute-start | bytes 98312 | tf_op jit(solution)/shard_map/ppermute | solution.py:292
  100.2 6.7 %collective-permute-start.14 = (f32[16,512]{1,0:T(8,128)S(1)}, f32[16,512]{1,0:T(8,128)S(1)}, u32[]{:S(2)}, u32[]{:S(2)}) collective-permute-start(f32[16,512]{1,0:T(8,128)S(1)} %shrink.1.refs_6_), channel_id=1, source_target_pairs={{0,2},{1,3},{2,0},{3,1},{4,6},{5,7},{6,4},{7,5},{8,10},{9,11},{10,... | collective-permute-start | bytes 98312 | tf_op jit(solution)/shard_map/ppermute | solution.py:292
  103.5 3.9 %collective-permute-start.13 = (f32[16,512]{1,0:T(8,128)S(1)}, f32[16,512]{1,0:T(8,128)S(1)}, u32[]{:S(2)}, u32[]{:S(2)}) collective-permute-start(f32[16,512]{1,0:T(8,128)S(1)} %shrink.1.refs_6_), channel_id=1, source_target_pairs={{0,1},{1,0},{2,3},{3,2},{4,5},{5,4},{6,7},{7,6},{8,9},{9,8},{10,11... | collective-permute-start | bytes 98312 | tf_op jit(solution)/shard_map/ppermute | solution.py:292
  107.4 39.6 %collective-permute-start.17 = (bf16[384,2048]{1,0:T(8,128)(2,1)S(1)}, bf16[384,2048]{1,0:T(8,128)(2,1)S(1)}, u32[]{:S(2)}, u32[]{:S(2)}) collective-permute-start(bf16[384,2048]{1,0:T(8,128)(2,1)S(1)} %slice_select_fusion), channel_id=1, source_target_pairs={{1,0},{2,3},{5,4},{6,7},{9,8},{10,11},{13,12},{14,15},{17,16},{18,... | collective-permute-start | bytes 4718600 | tf_op jit(solution)/shard_map/ppermute | solution.py:297
  108.7 46.8 %collective-permute-start.16 = (bf16[128,2048]{1,0:T(8,128)(2,1)S(1)}, bf16[128,2048]{1,0:T(8,128)(2,1)S(1)}, u32[]{:S(2)}, u32[]{:S(2)}) collective-permute-start(bf16[128,2048]{1,0:T(8,128)(2,1)S(1)} %slice_select_fusion.1), channel_id=1, source_target_pairs={{1,0},{2,3},{5,4},{6,7},{9,8},{10,11},{13,12},{14,15},{17,16},{18,... | collective-permute-start | bytes 1572872 | tf_op jit(solution)/shard_map/ppermute | solution.py:297
  (5 other events, 18.5 us)

commit v3 on v2

--- a/solution.py
+++ b/solution.py
@@ -279,26 +279,26 @@
 
     asked, source, place = wanted(block_owner, block_slot, rep)
     r1, l1 = lax.ppermute(features, "tp", right), lax.ppermute(features, "tp", left)
-    lists = in_turn(list(asked[1:]), rep)
+    lists = [swap(asked[i], i, rep) for i in range(1, rep)]
     downs = in_turn(pack(lists, adapter_down), rep)
     acc = add_part(after(info, *lists), 0, [features], query_weight)
     packed = pack([after(lists[0], acc)] + lists[1:], adapter_up)
-    r2, l2 = lax.ppermute(after(r1, acc, *downs), "tp", right[1:]), lax.ppermute(after(l1, acc, *downs), "tp", left[:-1])
+    r2, l2 = lax.ppermute(after(r1, acc, packed[0], *downs), "tp", right[1:]), lax.ppermute(after(l1, acc, packed[0], *downs), "tp", left[:-1])
     mine = shrink(after(source, acc, r1, l1), place, features, adapter_down, downs)
     acc = add_part(after(info, mine), 2, [l1, r1], query_weight, acc)
-    ups = in_turn([after(packed[0], mine), *packed[1:]], rep)
+    ups = in_turn([after(packed[0], downs[-1]), *packed[1:]], rep)
     up = chosen_blocks(after(source, acc), place, adapter_up, ups)
-    ready = after(mine, acc, up)
+    ready = after(mine, acc, ups[-1])
     shares = [mine] + [lax.ppermute(ready, "tp", [(i, i ^ d) for i in range(4)]) for d in (1, 2, 3)]
 
     bounds = (0, cut, rows)
     ends = [jnp.where(z == 1, l2[i:j], r2[i:j]) for i, j in zip(bounds, bounds[1:])]
-    ends = lax.optimization_barrier((*ends, *shares))[: len(ends)]
+    ends[0] = after(ends[0], *shares)
     far = [lax.ppermute(end, "tp", [(1, 0), (2, 3)]) for end in ends]
     acc = add_part(info, 4, [l1, r2, l2], query_weight, acc, shares, up, blocks)
     weight = fetch_part(after(info, acc), 7, query_weight, features.shape[1])
-    out = add_part(info, 6, [l2, r2, far[0]], weight, acc, final=(0, cut, None))
-    return add_part(info, 6, [l2, r2, far[1]], weight, acc, final=(cut, rows, out))
+    out = add_part(info, 6, [l2, r2, far[0]], weight, acc, final=(0, cut, None), tile=1024)
+    return add_part(info, 6, [l2, r2, far[1]], weight, acc, final=(cut, rows, out), tile=1024)
 
 
 def anywhere(features, query_weight, adapter_down, adapter_up, block_owner, block_slot, rep):

time: 160 us -> 156 us (0.975)
  waiting for transfers between devices: 58.1 us -> 54.5 us
    ppermute x9, waiting for transfers between devices: 41.4 us -> 32 us  [swap(): return lax.ppermute(x, 'rep', [(r, r ^ distance) for r in range(rep)])]
    ppermute x2, waiting for transfers between devices: 0.64 us -> 4.46 us  [the longest x1 4.46 us: on_line_of_four(): lax.ppermute(after(l1, acc, packed[0], *downs), 'tp', left[:-1])]
    ppermute x1, waiting for transfers between devices: 0.01 us -> 1.81 us  [on_line_of_four(): lax.ppermute(features, 'tp', right)]
    unnamed x22 -> x26, local copies, waits for them, and re-layouts: 18.5 us -> 18.9 us
  transfers between devices with their start and end apart: 18 -> 18, of which waited for: 13 -> 12; matrix products, arithmetic and copies ran while one was open for 4% -> 4% of each run, Pallas kernels for 29% -> 29%
where the time goes in v3:
time: 156 us; the launch traced here: 155 us
  waiting for transfers between devices  54.5 us (35%)
  Pallas kernels  48 us (31%)
  starting transfers between devices  28.1 us (18%)
  local copies, waits for them, and re-layouts  19.6 us (13%)
  other arithmetic  5.01 us (3%)
    pallas_call x5, Pallas kernels, add_part(): pl.pallas_call(functools.partial(add_kernel, len(cands), tail), out_shape...  34.4 us
    ppermute x9, waiting for transfers between devices, swap(): return lax.ppermute(x, 'rep', [(r, r ^ distance) for r in range(rep)])  32 us
    unnamed x26, local copies, waits for them, and re-layouts  18.9 us
    ppermute x2, waiting for transfers between devices, on_line_of_four(): far = [lax.ppermute(end, 'tp', [(1, 0), (2, 3)]) for end in ends]  14.9 us
    ppermute x3, starting transfers between devices, on_line_of_four(): lax.ppermute(ready, 'tp', [(i, i ^ d) for i in range(4)])  8.03 us
    ppermute x1, starting transfers between devices, on_line_of_four(): lax.ppermute(features, 'tp', right)  6.97 us
    ppermute x9, starting transfers between devices, swap(): return lax.ppermute(x, 'rep', [(r, r ^ distance) for r in range(rep)])  5.9 us
    pallas_call x2, Pallas kernels, pack(): pl.pallas_call(functools.partial(pack_kernel, count, cap), out_shape=[sha...  5.86 us
  transfers between devices with their start and end apart: 18, of which 12 were waited for; matrix products, arithmetic and copies ran while one was open for 4% of the time, Pallas kernels for 29%

profile of v3, /device:TPU:0, one launch (start us, length us, event | category | flops | bytes accessed | tf_op | source)
XLA Modules:
  0.0 155.5 jit_solution(15773953713543055575)
XLA Ops:
  1.3 7.0 %collective-permute-start.8 = (bf16[512,2048]{1,0:T(8,128)(2,1)}, bf16[512,2048]{1,0:T(8,128)(2,1)}, u32[]{:S(2)}, u32[]{:S(2)}) collective-permute-start(bf16[512,2048]{1,0:T(8,128)(2,1)} %features.1), channel_id=1, source_target_pairs={{0,1},{1,2},{2,3},{4,5},{5,6},{6,7},{8,9},{9,10},{10,11},{12,13},{... | collective-permute-start | bytes 6291464 | tf_op jit(solution)/shard_map/ppermute | solution.py:281
  15.0 1.6 %copy-done.3 = bf16[32,16,2048]{2,1,0:T(8,128)(2,1)S(1)} copy-done((bf16[32,16,2048]{2,1,0:T(8,128)(2,1)S(1)}, bf16[32,16,2048]{2,1,0:T(8,128)(2,1)}, u32[]{:S(2)}) %copy-start.3) | copy-done | bytes 2097176
  16.6 2.9 %pack_blocks.3 = (bf16[8,16,2048]{2,1,0:T(8,128)(2,1)S(1)}, bf16[8,16,2048]{2,1,0:T(8,128)(2,1)S(1)}, bf16[8,16,2048]{2,1,0:T(8,128)(2,1)}) custom-call(s32[8]{0:T(128)S(1)} %collective-permute-done.1.refs_0_, s32[8]{0:T(128)S(1)} %collective-permute-done.2.refs_1_, s32[8]{0:T(128)S(1)} %collective-permute-done.3.refs_2_, bf16[32,16,2048]{2,1,0:T(8,128)(2,1)S(1)} %copy-done.3), custom_call_target="tpu_custom_call" | custom-call | bytes 3145728 | tf_op jit(solution)/shard_map/pack_blocks/pallas_call | solution.py:71
  22.7 13.1 %collective-permute-done.5.refs_1_ = bf16[8,16,2048]{2,1,0:T(8,128)(2,1)S(1)} collective-permute-done((bf16[8,16,2048]{2,1,0:T(8,128)(2,1)S(1)}, bf16[8,16,2048]{2,1,0:T(8,128)(2,1)S(1)}, u32[]{:S(2)}, u32[]{:S(2)}) %collective-permute-start.5) | collective-permute-done | bytes 524320 | tf_op jit(solution)/shard_map/ppermute | solution.py:41
  36.5 8.0 %add_part.5.refs_4_ = f32[512,2048]{1,0:T(8,128)S(1)} custom-call(s32[8]{0:T(128)S(1)} %dynamic-slice_bitcast_fusion.refs_0_.info, bf16[512,2048]{1,0:T(8,128)(2,1)S(1)} %copy-done.7, bf16[8192,2048]{1,0:T(8,128)(2,1)} %weight.1), custom_call_target="tpu_custom_call" | custom-call | flops 4294967296 | bytes 16777216 | tf_op jit(solution)/shard_map/add_part/pallas_call | solution.py:230
  44.5 1.9 %copy-done.1 = f32[512,2048]{1,0:T(8,128)} copy-done((f32[512,2048]{1,0:T(8,128)}, f32[512,2048]{1,0:T(8,128)S(1)}, u32[]{:S(2)}) %copy-start.1) | copy-done | bytes 4194328
  46.5 2.9 %pack_blocks.2 = (bf16[8,16,2048]{2,1,0:T(8,128)(2,1)S(1)}, bf16[8,16,2048]{2,1,0:T(8,128)(2,1)S(1)}, bf16[8,16,2048]{2,1,0:T(8,128)(2,1)}) custom-call(s32[8]{0:T(128)S(1)} %collective-permute-done.1.refs_0_, s32[8]{0:T(128)S(1)} %collective-permute-done.2.refs_1_, s32[8]{0:T(128)S(1)} %collective-permute-done.3.refs_2_, bf16[32,16,2048]{2,1,0:T(8,128)(2,1)S(1)} %copy-done.5), custom_call_target="tpu_custom_call" | custom-call | bytes 3145728 | tf_op jit(solution)/shard_map/pack_blocks/pallas_call | solution.py:71
  50.2 1.8 %collective-permute-done.8.refs_2_ = bf16[512,2048]{1,0:T(8,128)(2,1)} collective-permute-done((bf16[512,2048]{1,0:T(8,128)(2,1)}, bf16[512,2048]{1,0:T(8,128)(2,1)}, u32[]{:S(2)}, u32[]{:S(2)}) %collective-permute-start.8) | collective-permute-done | bytes 2097184 | tf_op jit(solution)/shard_map/ppermute | solution.py:281
  53.3 2.0 %collective-permute-start.9 = (bf16[512,2048]{1,0:T(8,128)(2,1)}, bf16[512,2048]{1,0:T(8,128)(2,1)}, u32[]{:S(2)}, u32[]{:S(2)}) collective-permute-start(bf16[512,2048]{1,0:T(8,128)(2,1)} %collective-permute-done.8.refs_2_), channel_id=1, source_target_pairs={{1,2},{2,3},{5,6},{6,7},{9,10},{10,11},{13,14},{14,15},{17,18},{18... | collective-permute-start | bytes 6291464 | tf_op jit(solution)/shard_map/ppermute | solution.py:286
  55.4 1.9 %collective-permute-done.11.refs_0_ = bf16[8,16,2048]{2,1,0:T(8,128)(2,1)S(1)} collective-permute-done((bf16[8,16,2048]{2,1,0:T(8,128)(2,1)S(1)}, bf16[8,16,2048]{2,1,0:T(8,128)(2,1)S(1)}, u32[]{:S(2)}, u32[]{:S(2)}) %collective-permute-start.11) | collective-permute-done | bytes 524320 | tf_op jit(solution)/shard_map/ppermute | solution.py:41
  58.1 1.6 %collective-permute-start.12 = (bf16[8,16,2048]{2,1,0:T(8,128)(2,1)S(1)}, bf16[8,16,2048]{2,1,0:T(8,128)(2,1)S(1)}, u32[]{:S(2)}, u32[]{:S(2)}) collective-permute-start(bf16[8,16,2048]{2,1,0:T(8,128)(2,1)S(1)} %get-tuple-element.41), channel_id=1, source_target_pairs={{0,8},{4,12},{8,0},{12,4},{1,9},{5,13},{9,1},{13,5},{2,10},{6,14},... | collective-permute-start | bytes 1572872 | tf_op jit(solution)/shard_map/ppermute | solution.py:41
  59.7 12.3 %collective-permute-done.12.refs_1_ = bf16[8,16,2048]{2,1,0:T(8,128)(2,1)S(1)} collective-permute-done((bf16[8,16,2048]{2,1,0:T(8,128)(2,1)S(1)}, bf16[8,16,2048]{2,1,0:T(8,128)(2,1)S(1)}, u32[]{:S(2)}, u32[]{:S(2)}) %collective-permute-start.12) | collective-permute-done | bytes 524320 | tf_op jit(solution)/shard_map/ppermute | solution.py:41
  76.6 3.7 %shrink.1.refs_6_ = f32[16,512]{1,0:T(8,128)S(1)} custom-call(s32[16]{0:T(128)S(1)} %get-tuple-element.44.source, s32[16]{0:T(128)S(1)} %get-tuple-element.47.place, bf16[512,2048]{1,0:T(8,128)(2,1)S(1)} %copy-done.8, bf16[32,16,2048]{2,1,0:T(8,128)(2,1)S(1)} %copy-done.4, bf16[8,16,2048]{2,1,0:T(8,128)(2,1)S(1)} %collective-permute-done.4.refs_0_, ...), custom_call_target="tpu_custom_call" | custom-call | flops 536870912 | bytes 2097152 | tf_op jit(solution)/shard_map/shrink/pallas_call | solution.py:133
  80.3 9.6 %add_part.6.refs_5_ = f32[512,2048]{1,0:T(8,128)S(1)} custom-call(s32[8]{0:T(128)S(1)} %dynamic-slice_bitcast_fusion.refs_0_.info, bf16[512,2048]{1,0:T(8,128)(2,1)} %collective-permute-done.refs_1_, bf16[512,2048]{1,0:T(8,128)(2,1)} %collective-permute-done.8.refs_2_, bf16[8192,2048]{1,0:T(8,128)(2,1)} %weight.1, ...), custom_call_target="tpu_custom_call", output_to_operand_aliasing={{}: (4, {})} | custom-call | flops 4294967296 | bytes 16777216 | tf_op jit(solution)/shard_map/add_part/pallas_call | solution.py:230
  90.0 4.9 %collective-permute-start.16 = (f32[16,512]{1,0:T(8,128)S(1)}, f32[16,512]{1,0:T(8,128)S(1)}, u32[]{:S(2)}, u32[]{:S(2)}) collective-permute-start(f32[16,512]{1,0:T(8,128)S(1)} %shrink.1.refs_6_), channel_id=1, source_target_pairs={{0,3},{1,2},{2,1},{3,0},{4,7},{5,6},{6,5},{7,4},{8,11},{9,10},{10,... | collective-permute-start | bytes 98312 | tf_op jit(solution)/shard_map/ppermute | solution.py:292
  94.8 3.2 %collective-permute-start.15 = (f32[16,512]{1,0:T(8,128)S(1)}, f32[16,512]{1,0:T(8,128)S(1)}, u32[]{:S(2)}, u32[]{:S(2)}) collective-permute-start(f32[16,512]{1,0:T(8,128)S(1)} %shrink.1.refs_6_), channel_id=1, source_target_pairs={{0,2},{1,3},{2,0},{3,1},{4,6},{5,7},{6,4},{7,5},{8,10},{9,11},{10,... | collective-permute-start | bytes 98312 | tf_op jit(solution)/shard_map/ppermute | solution.py:292
  98.0 4.5 %collective-permute-done.7.refs_3_.refs_1_ = bf16[512,2048]{1,0:T(8,128)(2,1)S(1)} collective-permute-done((bf16[512,2048]{1,0:T(8,128)(2,1)}, bf16[512,2048]{1,0:T(8,128)(2,1)S(1)}, u32[]{:S(2)}, u32[]{:S(2)}) %collective-permute-start.7) | collective-permute-done | bytes 2097184 | tf_op jit(solution)/shard_map/ppermute | solution.py:286
  106.7 3.0 %choose_blocks.1.refs_10_ = bf16[256,2048]{1,0:T(8,128)(2,1)S(1)} custom-call(s32[16]{0:T(128)S(1)} %get-tuple-element.44.source, s32[16]{0:T(128)S(1)} %get-tuple-element.47.place, bf16[32,16,2048]{2,1,0:T(8,128)(2,1)S(1)} %copy-done.6, bf16[8,16,2048]{2,1,0:T(8,128)(2,1)S(1)} %copy-done.10, bf16[8,16,2048]{2,1,0:T(8,128)(2,1)S(1)} %copy-done.12, ...), custom_call_target="tpu_custom_call" | custom-call | bytes 2097152 | tf_op jit(solution)/shard_map/choose_blocks/pallas_call | solution.py:106
  112.1 8.4 %add_part.7.refs_5_ = f32[512,2048]{1,0:T(8,128)S(1)} custom-call(s32[8]{0:T(128)S(1)} %dynamic-slice_bitcast_fusion.refs_0_.info, bf16[512,2048]{1,0:T(8,128)(2,1)} %collective-permute-done.refs_1_, bf16[512,2048]{1,0:T(8,128)(2,1)} %collective-permute-done.9.refs_2_, ...), custom_call_target="tpu_custom_call", output_to_operand_aliasing={{}: (5, {})} | custom-call | flops 4294967296 | bytes 16777216 | tf_op jit(solution)/shard_map/add_part/pallas_call | solution.py:230
  120.5 10.5 %copy-done = bf16[8192,2048]{1,0:T(8,128)(2,1)S(1)} copy-done((bf16[8192,2048]{1,0:T(8,128)(2,1)S(1)}, bf16[8192,2048]{1,0:T(8,128)(2,1)}, u32[]{:S(2)}) %copy-start) | copy-done | bytes 33554456
  132.2 12.7 %collective-permute-done.17.refs_3_ = bf16[384,2048]{1,0:T(8,128)(2,1)S(1)} collective-permute-done((bf16[384,2048]{1,0:T(8,128)(2,1)S(1)}, bf16[384,2048]{1,0:T(8,128)(2,1)S(1)}, u32[]{:S(2)}, u32[]{:S(2)}) %collective-permute-start.17) | collective-permute-done | bytes 1572896 | tf_op jit(solution)/shard_map/ppermute | solution.py:297
  144.8 5.4 %add_part.8.refs_6_ = bf16[512,2048]{1,0:T(8,128)(2,1)} custom-call(s32[8]{0:T(128)S(1)} %dynamic-slice_bitcast_fusion.refs_0_.info, bf16[512,2048]{1,0:T(8,128)(2,1)S(1)} %collective-permute-done.7.refs_3_.refs_1_, bf16[512,2048]{1,0:T(8,128)(2,1)} %collective-permute-done.9.refs_2_, bf16[384,2048]{1,0:T(8,128)(2,1)S(1)} %collective-permute-done.17.refs_3_, ...), custom_call_target="tpu_custom_call" | custom-call | flops 3221225472 | bytes 14680064 | tf_op jit(solution)/shard_map/add_part/pallas_call | solution.py:230
  150.3 2.2 %collective-permute-done.10.refs_3_ = bf16[128,2048]{1,0:T(8,128)(2,1)S(1)} collective-permute-done((bf16[128,2048]{1,0:T(8,128)(2,1)S(1)}, bf16[128,2048]{1,0:T(8,128)(2,1)S(1)}, u32[]{:S(2)}, u32[]{:S(2)}) %collective-permute-start.10) | collective-permute-done | bytes 524320 | tf_op jit(solution)/shard_map/ppermute | solution.py:297
  152.5 2.9 %add_part.9 = bf16[512,2048]{1,0:T(8,128)(2,1)} custom-call(s32[8]{0:T(128)S(1)} %dynamic-slice_bitcast_fusion.refs_0_.info, bf16[512,2048]{1,0:T(8,128)(2,1)S(1)} %collective-permute-done.7.refs_3_.refs_1_, bf16[512,2048]{1,0:T(8,128)(2,1)} %collective-permute-done.9.refs_2_, ...), custom_call_target="tpu_custom_call", output_to_operand_aliasing={{}: (6, {})} | custom-call | flops 1073741824 | bytes 10485760 | tf_op jit(solution)/shard_map/add_part/pallas_call | solution.py:230
  (56 shorter events, 27.1 us)
Async XLA Ops:
  0.0 52.0 %collective-permute-start = (bf16[512,2048]{1,0:T(8,128)(2,1)}, bf16[512,2048]{1,0:T(8,128)(2,1)}, u32[]{:S(2)}, u32[]{:S(2)}) collective-permute-start(bf16[512,2048]{1,0:T(8,128)(2,1)} %features.1), channel_id=1, source_target_pairs={{1,0},{2,1},{3,2},{5,4},{6,5},{7,6},{9,8},{10,9},{11,10},{13,12},{... | collective-permute-start | bytes 6291464 | tf_op jit(solution)/shard_map/ppermute | solution.py:281
  1.3 50.8 %collective-permute-start.8 = (bf16[512,2048]{1,0:T(8,128)(2,1)}, bf16[512,2048]{1,0:T(8,128)(2,1)}, u32[]{:S(2)}, u32[]{:S(2)}) collective-permute-start(bf16[512,2048]{1,0:T(8,128)(2,1)} %features.1), channel_id=1, source_target_pairs={{0,1},{1,2},{2,3},{4,5},{5,6},{6,7},{8,9},{9,10},{10,11},{12,13},{... | collective-permute-start | bytes 6291464 | tf_op jit(solution)/shard_map/ppermute | solution.py:281
  10.7 3.0 %collective-permute-start.3 = (s32[8]{0:T(128)S(1)}, s32[8]{0:T(128)S(1)}, u32[]{:S(2)}, u32[]{:S(2)}) collective-permute-start(s32[8]{0:T(128)S(1)} %get-tuple-element.49), channel_id=1, source_target_pairs={{0,12},{4,8},{8,4},{12,0},{1,13},{5,9},{9,5},{13,1},{2,14},{6,10},... | collective-permute-start | bytes 104 | tf_op jit(solution)/shard_map/ppermute | solution.py:41
  11.5 3.5 %collective-permute-start.2 = (s32[8]{0:T(128)S(1)}, s32[8]{0:T(128)S(1)}, u32[]{:S(2)}, u32[]{:S(2)}) collective-permute-start(s32[8]{0:T(128)S(1)} %get-tuple-element.50), channel_id=1, source_target_pairs={{0,8},{4,12},{8,0},{12,4},{1,9},{5,13},{9,1},{13,5},{2,10},{6,14},... | collective-permute-start | bytes 104 | tf_op jit(solution)/shard_map/ppermute | solution.py:41
  12.7 2.3 %collective-permute-start.1 = (s32[8]{0:T(128)S(1)}, s32[8]{0:T(128)S(1)}, u32[]{:S(2)}, u32[]{:S(2)}) collective-permute-start(s32[8]{0:T(128)S(1)} %get-tuple-element.51), channel_id=1, source_target_pairs={{0,4},{4,0},{8,12},{12,8},{1,5},{5,1},{9,13},{13,9},{2,6},{6,2},{1... | collective-permute-start | bytes 104 | tf_op jit(solution)/shard_map/ppermute | solution.py:41
  16.6 19.9 %copy-start.7 = (bf16[512,2048]{1,0:T(8,128)(2,1)S(1)}, bf16[512,2048]{1,0:T(8,128)(2,1)}, u32[]{:S(2)}) copy-start(bf16[512,2048]{1,0:T(8,128)(2,1)} %features.1) | copy-start | bytes 6291460
  19.6 2.1 %collective-permute-start.4 = (bf16[8,16,2048]{2,1,0:T(8,128)(2,1)S(1)}, bf16[8,16,2048]{2,1,0:T(8,128)(2,1)S(1)}, u32[]{:S(2)}, u32[]{:S(2)}) collective-permute-start(bf16[8,16,2048]{2,1,0:T(8,128)(2,1)S(1)} %get-tuple-element.29), channel_id=1, source_target_pairs={{0,4},{4,0},{8,12},{12,8},{1,5},{5,1},{9,13},{13,9},{2,6},{6,2},{1... | collective-permute-start | bytes 1572872 | tf_op jit(solution)/shard_map/ppermute | solution.py:41
  21.6 14.2 %collective-permute-start.5 = (bf16[8,16,2048]{2,1,0:T(8,128)(2,1)S(1)}, bf16[8,16,2048]{2,1,0:T(8,128)(2,1)S(1)}, u32[]{:S(2)}, u32[]{:S(2)}) collective-permute-start(bf16[8,16,2048]{2,1,0:T(8,128)(2,1)S(1)} %get-tuple-element.31), channel_id=1, source_target_pairs={{0,8},{4,12},{8,0},{12,4},{1,9},{5,13},{9,1},{13,5},{2,10},{6,14},... | collective-permute-start | bytes 1572872 | tf_op jit(solution)/shard_map/ppermute | solution.py:41
  35.8 14.4 %collective-permute-start.6 = (bf16[8,16,2048]{2,1,0:T(8,128)(2,1)}, bf16[8,16,2048]{2,1,0:T(8,128)(2,1)}, u32[]{:S(2)}, u32[]{:S(2)}) collective-permute-start(bf16[8,16,2048]{2,1,0:T(8,128)(2,1)} %get-tuple-element.33), channel_id=1, source_target_pairs={{0,12},{4,8},{8,4},{12,0},{1,13},{5,9},{9,5},{13,1},{2,14},{6,10},... | collective-permute-start | bytes 1572872 | tf_op jit(solution)/shard_map/ppermute | solution.py:41
  36.5 9.9 %copy-start.5 = (bf16[32,16,2048]{2,1,0:T(8,128)(2,1)S(1)}, bf16[32,16,2048]{2,1,0:T(8,128)(2,1)}, u32[]{:S(2)}) copy-start(bf16[32,16,2048]{2,1,0:T(8,128)(2,1)} %pool.3) | copy-start | bytes 6291460
  52.0 50.4 %collective-permute-start.7 = (bf16[512,2048]{1,0:T(8,128)(2,1)}, bf16[512,2048]{1,0:T(8,128)(2,1)S(1)}, u32[]{:S(2)}, u32[]{:S(2)}) collective-permute-start(bf16[512,2048]{1,0:T(8,128)(2,1)} %collective-permute-done.refs_1_), channel_id=1, source_target_pairs={{1,0},{2,1},{5,4},{6,5},{9,8},{10,9},{13,12},{14,13},{17,16},{18,1... | collective-permute-start | bytes 6291464 | tf_op jit(solution)/shard_map/ppermute | solution.py:286
  53.3 49.1 %collective-permute-start.9 = (bf16[512,2048]{1,0:T(8,128)(2,1)}, bf16[512,2048]{1,0:T(8,128)(2,1)}, u32[]{:S(2)}, u32[]{:S(2)}) collective-permute-start(bf16[512,2048]{1,0:T(8,128)(2,1)} %collective-permute-done.8.refs_2_), channel_id=1, source_target_pairs={{1,2},{2,3},{5,6},{6,7},{9,10},{10,11},{13,14},{14,15},{17,18},{18... | collective-permute-start | bytes 6291464 | tf_op jit(solution)/shard_map/ppermute | solution.py:286
  55.4 1.9 %collective-permute-start.11 = (bf16[8,16,2048]{2,1,0:T(8,128)(2,1)S(1)}, bf16[8,16,2048]{2,1,0:T(8,128)(2,1)S(1)}, u32[]{:S(2)}, u32[]{:S(2)}) collective-permute-start(bf16[8,16,2048]{2,1,0:T(8,128)(2,1)S(1)} %get-tuple-element.40), channel_id=1, source_target_pairs={{0,4},{4,0},{8,12},{12,8},{1,5},{5,1},{9,13},{13,9},{2,6},{6,2},{1... | collective-permute-start | bytes 1572872 | tf_op jit(solution)/shard_map/ppermute | solution.py:41
  58.1 14.0 %collective-permute-start.12 = (bf16[8,16,2048]{2,1,0:T(8,128)(2,1)S(1)}, bf16[8,16,2048]{2,1,0:T(8,128)(2,1)S(1)}, u32[]{:S(2)}, u32[]{:S(2)}) collective-permute-start(bf16[8,16,2048]{2,1,0:T(8,128)(2,1)S(1)} %get-tuple-element.41), channel_id=1, source_target_pairs={{0,8},{4,12},{8,0},{12,4},{1,9},{5,13},{9,1},{13,5},{2,10},{6,14},... | collective-permute-start | bytes 1572872 | tf_op jit(solution)/shard_map/ppermute | solution.py:41
  72.8 17.1 %collective-permute-start.13 = (bf16[8,16,2048]{2,1,0:T(8,128)(2,1)}, bf16[8,16,2048]{2,1,0:T(8,128)(2,1)}, u32[]{:S(2)}, u32[]{:S(2)}) collective-permute-start(bf16[8,16,2048]{2,1,0:T(8,128)(2,1)} %get-tuple-element.42), channel_id=1, source_target_pairs={{0,12},{4,8},{8,4},{12,0},{1,13},{5,9},{9,5},{13,1},{2,14},{6,10},... | collective-permute-start | bytes 1572872 | tf_op jit(solution)/shard_map/ppermute | solution.py:41
  89.9 16.7 %copy-start.6 = (bf16[32,16,2048]{2,1,0:T(8,128)(2,1)S(1)}, bf16[32,16,2048]{2,1,0:T(8,128)(2,1)}, u32[]{:S(2)}) copy-start(bf16[32,16,2048]{2,1,0:T(8,128)(2,1)} %pool.3) | copy-start | bytes 6291460
  89.9 16.7 %copy-start.10 = (bf16[8,16,2048]{2,1,0:T(8,128)(2,1)S(1)}, bf16[8,16,2048]{2,1,0:T(8,128)(2,1)}, u32[]{:S(2)}) copy-start(bf16[8,16,2048]{2,1,0:T(8,128)(2,1)} %copy-done.9) | copy-start | bytes 1572868
  89.9 16.7 %copy-start.12 = (bf16[8,16,2048]{2,1,0:T(8,128)(2,1)S(1)}, bf16[8,16,2048]{2,1,0:T(8,128)(2,1)}, u32[]{:S(2)}) copy-start(bf16[8,16,2048]{2,1,0:T(8,128)(2,1)} %copy-done.11) | copy-start | bytes 1572868
  90.0 14.1 %collective-permute-start.16 = (f32[16,512]{1,0:T(8,128)S(1)}, f32[16,512]{1,0:T(8,128)S(1)}, u32[]{:S(2)}, u32[]{:S(2)}) collective-permute-start(f32[16,512]{1,0:T(8,128)S(1)} %shrink.1.refs_6_), channel_id=1, source_target_pairs={{0,3},{1,2},{2,1},{3,0},{4,7},{5,6},{6,5},{7,4},{8,11},{9,10},{10,... | collective-permute-start | bytes 98312 | tf_op jit(solution)/shard_map/ppermute | solution.py:292
  94.8 10.6 %collective-permute-start.15 = (f32[16,512]{1,0:T(8,128)S(1)}, f32[16,512]{1,0:T(8,128)S(1)}, u32[]{:S(2)}, u32[]{:S(2)}) collective-permute-start(f32[16,512]{1,0:T(8,128)S(1)} %shrink.1.refs_6_), channel_id=1, source_target_pairs={{0,2},{1,3},{2,0},{3,1},{4,6},{5,7},{6,4},{7,5},{8,10},{9,11},{10,... | collective-permute-start | bytes 98312 | tf_op jit(solution)/shard_map/ppermute | solution.py:292
  98.0 7.4 %collective-permute-start.14 = (f32[16,512]{1,0:T(8,128)S(1)}, f32[16,512]{1,0:T(8,128)S(1)}, u32[]{:S(2)}, u32[]{:S(2)}) collective-permute-start(f32[16,512]{1,0:T(8,128)S(1)} %shrink.1.refs_6_), channel_id=1, source_target_pairs={{0,1},{1,0},{2,3},{3,2},{4,5},{5,4},{6,7},{7,6},{8,9},{9,8},{10,11... | collective-permute-start | bytes 98312 | tf_op jit(solution)/shard_map/ppermute | solution.py:292
  105.4 39.5 %collective-permute-start.17 = (bf16[384,2048]{1,0:T(8,128)(2,1)S(1)}, bf16[384,2048]{1,0:T(8,128)(2,1)S(1)}, u32[]{:S(2)}, u32[]{:S(2)}) collective-permute-start(bf16[384,2048]{1,0:T(8,128)(2,1)S(1)} %slice_select_fusion), channel_id=1, source_target_pairs={{1,0},{2,3},{5,4},{6,7},{9,8},{10,11},{13,12},{14,15},{17,16},{18,... | collective-permute-start | bytes 4718600 | tf_op jit(solution)/shard_map/ppermute | solution.py:297
  110.8 41.8 %collective-permute-start.10 = (bf16[128,2048]{1,0:T(8,128)(2,1)S(1)}, bf16[128,2048]{1,0:T(8,128)(2,1)S(1)}, u32[]{:S(2)}, u32[]{:S(2)}) collective-permute-start(bf16[128,2048]{1,0:T(8,128)(2,1)S(1)} %slice_select_fusion.1), channel_id=1, source_target_pairs={{1,0},{2,3},{5,4},{6,7},{9,8},{10,11},{13,12},{14,15},{17,16},{18,... | collective-permute-start | bytes 1572872 | tf_op jit(solution)/shard_map/ppermute | solution.py:297
  120.5 10.5 %copy-start = (bf16[8192,2048]{1,0:T(8,128)(2,1)S(1)}, bf16[8192,2048]{1,0:T(8,128)(2,1)}, u32[]{:S(2)}) copy-start(bf16[8192,2048]{1,0:T(8,128)(2,1)} %weight.1) | copy-start | bytes 100663296
  (7 other events, 12.0 us)

commit v4 on v3

--- a/solution.py
+++ b/solution.py
@@ -195,6 +195,7 @@
     whole, depth = cands[0].shape
     cols = weight.shape[1]
     first, end, kept = final if final else (0, whole, None)
+    whole = acc.shape[0] if final else whole
     rows = end - first
     tail = {
         "acc": acc is not None,
@@ -263,10 +264,10 @@
 
 
 CHOICES = (
-    (0, 0, 0, 1, 2, 2, 2, 3),
+    (0, 0, 0, 1, 1, 2, 1, 3),
     (0, 1, 1, 0, 0, 2, 0, 3),
-    (0, 2, 1, 1, 0, 3, 1, 0),
-    (0, 3, 1, 2, 1, 1, 2, 0),
+    (0, 2, 1, 1, 0, 3, 0, 0),
+    (0, 3, 1, 2, 2, 1, 1, 0),
 )
 
 
@@ -280,25 +281,27 @@
     asked, source, place = wanted(block_owner, block_slot, rep)
     r1, l1 = lax.ppermute(features, "tp", right), lax.ppermute(features, "tp", left)
     lists = [swap(asked[i], i, rep) for i in range(1, rep)]
-    downs = in_turn(pack(lists, adapter_down), rep)
+    downs = [swap(p, i + 1, rep) for i, p in enumerate(pack(lists, adapter_down))]
     acc = add_part(after(info, *lists), 0, [features], query_weight)
     packed = pack([after(lists[0], acc)] + lists[1:], adapter_up)
-    r2, l2 = lax.ppermute(after(r1, acc, packed[0], *downs), "tp", right[1:]), lax.ppermute(after(l1, acc, packed[0], *downs), "tp", left[:-1])
-    mine = shrink(after(source, acc, r1, l1), place, features, adapter_down, downs)
-    acc = add_part(after(info, mine), 2, [l1, r1], query_weight, acc)
-    ups = in_turn([after(packed[0], downs[-1]), *packed[1:]], rep)
+    mine = shrink(after(source, acc, packed[0]), place, features, adapter_down, downs)
+    pair = mine + lax.ppermute(mine, "tp", [(i, i ^ 1) for i in range(4)])
+
+    l2, r2 = lax.ppermute(after(l1, pair), "tp", [(1, 0)]), lax.ppermute(after(r1, pair), "tp", [(2, 3)])
+    inner, bounds = after(z, pair), (0, cut, rows)
+    cross = [
+        lax.ppermute(jnp.where(inner == 1, r1[i:j], l1[i:j]), "tp", [(1, 2), (2, 1)]) for i, j in zip(bounds, bounds[1:])
+    ]
+    far = [lax.ppermute(c, "tp", [(1, 0), (2, 3)]) for c in cross]
+
+    ups = in_turn([after(packed[0], pair), *packed[1:]], rep)
+    shares = [pair, lax.ppermute(after(pair, ups[-1]), "tp", [(i, i ^ 2) for i in range(4)])]
+    acc = add_part(after(info, pair), 2, [l1, r1], query_weight, acc)
     up = chosen_blocks(after(source, acc), place, adapter_up, ups)
-    ready = after(mine, acc, ups[-1])
-    shares = [mine] + [lax.ppermute(ready, "tp", [(i, i ^ d) for i in range(4)]) for d in (1, 2, 3)]
-
-    bounds = (0, cut, rows)
-    ends = [jnp.where(z == 1, l2[i:j], r2[i:j]) for i, j in zip(bounds, bounds[1:])]
-    ends[0] = after(ends[0], *shares)
-    far = [lax.ppermute(end, "tp", [(1, 0), (2, 3)]) for end in ends]
-    acc = add_part(info, 4, [l1, r2, l2], query_weight, acc, shares, up, blocks)
+    acc = add_part(info, 4, [l1, l2, r2], query_weight, acc, shares, up, blocks)
     weight = fetch_part(after(info, acc), 7, query_weight, features.shape[1])
-    out = add_part(info, 6, [l2, r2, far[0]], weight, acc, final=(0, cut, None), tile=1024)
-    return add_part(info, 6, [l2, r2, far[1]], weight, acc, final=(cut, rows, out), tile=1024)
+    out = add_part(info, 6, [cross[0], far[0]], weight, acc, final=(0, cut, None), tile=1024)
+    return add_part(info, 6, [cross[1], far[1]], weight, acc, final=(cut, rows, out), tile=1024)
 
 
 def anywhere(features, query_weight, adapter_down, adapter_up, block_owner, block_slot, rep):

time: 156 us -> 155 us (level)
  starting transfers between devices: 28.1 us -> 43.4 us
  waiting for transfers between devices: 54.5 us -> 44.5 us
  local copies, waits for them, and re-layouts: 19.6 us -> 15.3 us
  Pallas kernels: 48 us -> 45.2 us
    ppermute x7 -> x8, starting transfers between devices: 13.9 us -> 28.9 us  [the longest x1 22.1 us: on_line_of_four(): lax.ppermute(after(pair, ups[-1]), 'tp', [(i, i ^ 2) for i in range(4)])]
    ppermute x7 -> x8, waiting for transfers between devices: 20.7 us -> 7.78 us  [the longest x1 4.47 us: on_line_of_four(): pair = mine + lax.ppermute(mine, 'tp', [(i, i ^ 1) for i in range(4)])]
    ppermute x9, waiting for transfers between devices: 32 us -> 36.8 us  [swap(): return lax.ppermute(x, 'rep', [(r, r ^ distance) for r in range(rep)])]
    unnamed x26 -> x24, local copies, waits for them, and re-layouts: 18.9 us -> 14.6 us
    ppermute x1, waiting for transfers between devices: 1.81 us -> 0.01 us  [on_line_of_four(): lax.ppermute(features, 'tp', right)]
    pallas_call x5, Pallas kernels: 34.4 us -> 32.8 us  [add_part(): pl.pallas_call(functools.partial(add_kernel, len(cands), tail), out_shape...]
  transfers between devices with their start and end apart: 18 -> 19, of which waited for: 12 -> 8; matrix products, arithmetic and copies ran while one was open for 4% -> 3% of each run, Pallas kernels for 29% -> 27%
where the time goes in v4:
time: 155 us; the launch traced here: 154 us
  Pallas kernels  45.2 us (29%)
  waiting for transfers between devices  44.5 us (29%)
  starting transfers between devices  43.4 us (28%)
  local copies, waits for them, and re-layouts  15.3 us (10%)
  other arithmetic  5.17 us (3%)
    ppermute x9, waiting for transfers between devices, swap(): return lax.ppermute(x, 'rep', [(r, r ^ distance) for r in range(rep)])  36.8 us
    pallas_call x5, Pallas kernels, add_part(): pl.pallas_call(functools.partial(add_kernel, len(cands), tail), out_shape...  32.8 us
    ppermute x1, starting transfers between devices, on_line_of_four(): lax.ppermute(after(pair, ups[-1]), 'tp', [(i, i ^ 2) for i in range(4)])  22.1 us
    unnamed x24, local copies, waits for them, and re-layouts  14.6 us
    ppermute x1, starting transfers between devices, on_line_of_four(): lax.ppermute(features, 'tp', right)  6.93 us
    ppermute x9, starting transfers between devices, swap(): return lax.ppermute(x, 'rep', [(r, r ^ distance) for r in range(rep)])  6.31 us
    pallas_call x2, Pallas kernels, pack(): pl.pallas_call(functools.partial(pack_kernel, count, cap), out_shape=[sha...  4.91 us
    ppermute x1, waiting for transfers between devices, on_line_of_four(): pair = mine + lax.ppermute(mine, 'tp', [(i, i ^ 1) for i in range(4)])  4.47 us
  transfers between devices with their start and end apart: 19, of which 8 were waited for; matrix products, arithmetic and copies ran while one was open for 3% of the time, Pallas kernels for 27%

profile of v4, /device:TPU:0, one launch (start us, length us, event | category | flops | bytes accessed | tf_op | source)
XLA Modules:
  0.0 153.9 jit_solution(9636822446800052465)
XLA Ops:
  1.3 6.9 %collective-permute-start.7 = (bf16[512,2048]{1,0:T(8,128)(2,1)}, bf16[512,2048]{1,0:T(8,128)(2,1)}, u32[]{:S(2)}, u32[]{:S(2)}) collective-permute-start(bf16[512,2048]{1,0:T(8,128)(2,1)} %features.1), channel_id=1, source_target_pairs={{0,1},{1,2},{2,3},{4,5},{5,6},{6,7},{8,9},{9,10},{10,11},{12,13},{... | collective-permute-start | bytes 6291464 | tf_op jit(solution)/shard_map/ppermute | solution.py:282
  10.7 2.0 %collective-permute-start.1 = (s32[8]{0:T(128)S(1)}, s32[8]{0:T(128)S(1)}, u32[]{:S(2)}, u32[]{:S(2)}) collective-permute-start(s32[8]{0:T(128)S(1)} %get-tuple-element.46), channel_id=1, source_target_pairs={{0,8},{4,12},{8,0},{12,4},{1,9},{5,13},{9,1},{13,5},{2,10},{6,14},... | collective-permute-start | bytes 104 | tf_op jit(solution)/shard_map/ppermute | solution.py:41
  12.7 1.5 collective-permute-done.1.refs_1_
  15.6 1.6 %copy-done.3 = bf16[32,16,2048]{2,1,0:T(8,128)(2,1)S(1)} copy-done((bf16[32,16,2048]{2,1,0:T(8,128)(2,1)S(1)}, bf16[32,16,2048]{2,1,0:T(8,128)(2,1)}, u32[]{:S(2)}) %copy-start.3) | copy-done | bytes 2097176
  17.2 1.9 %pack_blocks.3 = (bf16[8,16,2048]{2,1,0:T(8,128)(2,1)}, bf16[8,16,2048]{2,1,0:T(8,128)(2,1)}, bf16[8,16,2048]{2,1,0:T(8,128)(2,1)}) custom-call(s32[8]{0:T(128)S(1)} %collective-permute-done.refs_0_, s32[8]{0:T(128)S(1)} %collective-permute-done.1.refs_1_, s32[8]{0:T(128)S(1)} %collective-permute-done.2.refs_2_, bf16[32,16,2048]{2,1,0:T(8,128)(2,1)S(1)} %copy-done.3), custom_call_target="tpu_custom_call" | custom-call | bytes 3145728 | tf_op jit(solution)/shard_map/pack_blocks/pallas_call | solution.py:71
  21.7 1.6 %copy-done.7 = bf16[512,2048]{1,0:T(8,128)(2,1)S(1)} copy-done((bf16[512,2048]{1,0:T(8,128)(2,1)S(1)}, bf16[512,2048]{1,0:T(8,128)(2,1)}, u32[]{:S(2)}) %copy-start.7) | copy-done | bytes 2097176
  23.3 8.0 %add_part.5.refs_4_ = f32[512,2048]{1,0:T(8,128)S(1)} custom-call(s32[8]{0:T(128)S(1)} %dynamic-slice_bitcast_fusion.refs_0_.info, bf16[512,2048]{1,0:T(8,128)(2,1)S(1)} %copy-done.7, bf16[8192,2048]{1,0:T(8,128)(2,1)} %weight.1), custom_call_target="tpu_custom_call" | custom-call | flops 4294967296 | bytes 16777216 | tf_op jit(solution)/shard_map/add_part/pallas_call | solution.py:231
  31.3 3.0 %pack_blocks.2 = (bf16[8,16,2048]{2,1,0:T(8,128)(2,1)S(1)}, bf16[8,16,2048]{2,1,0:T(8,128)(2,1)S(1)}, bf16[8,16,2048]{2,1,0:T(8,128)(2,1)S(1)}) custom-call(s32[8]{0:T(128)S(1)} %collective-permute-done.refs_0_, s32[8]{0:T(128)S(1)} %collective-permute-done.1.refs_1_, s32[8]{0:T(128)S(1)} %collective-permute-done.2.refs_2_, bf16[32,16,2048]{2,1,0:T(8,128)(2,1)S(1)} %copy-done.5), custom_call_target="tpu_custom_call" | custom-call | bytes 3145728 | tf_op jit(solution)/shard_map/pack_blocks/pallas_call | solution.py:71
  35.2 9.0 %collective-permute-done.5.refs_2_ = bf16[8,16,2048]{2,1,0:T(8,128)(2,1)} collective-permute-done((bf16[8,16,2048]{2,1,0:T(8,128)(2,1)}, bf16[8,16,2048]{2,1,0:T(8,128)(2,1)}, u32[]{:S(2)}, u32[]{:S(2)}) %collective-permute-start.5) | collective-permute-done | bytes 524320 | tf_op jit(solution)/shard_map/ppermute | solution.py:41
  44.2 3.5 %shrink.1 = f32[16,512]{1,0:T(8,128)S(1)} custom-call(s32[16]{0:T(128)S(1)} %get-tuple-element.41.source, s32[16]{0:T(128)S(1)} %get-tuple-element.43.place, bf16[512,2048]{1,0:T(8,128)(2,1)S(1)} %copy-done.7, bf16[32,16,2048]{2,1,0:T(8,128)(2,1)S(1)} %copy-done.4, bf16[8,16,2048]{2,1,0:T(8,128)(2,1)S(1)} %collective-permute-done.3.refs_0_, ...), custom_call_target="tpu_custom_call" | custom-call | flops 536870912 | bytes 2097152 | tf_op jit(solution)/shard_map/shrink/pallas_call | solution.py:133
  48.2 4.5 %collective-permute-done.6 = f32[16,512]{1,0:T(8,128)S(1)} collective-permute-done((f32[16,512]{1,0:T(8,128)S(1)}, f32[16,512]{1,0:T(8,128)S(1)}, u32[]{:S(2)}, u32[]{:S(2)}) %collective-permute-start.6) | collective-permute-done | bytes 32800 | tf_op jit(solution)/shard_map/ppermute | solution.py:288
  52.7 1.7 %slice_select_fusion = bf16[384,2048]{1,0:T(8,128)(2,1)S(1)} fusion(bf16[512,2048]{1,0:T(8,128)(2,1)S(1)} %collective-permute-done.8.refs_1_, bf16[512,2048]{1,0:T(8,128)(2,1)} %collective-permute-done.7.refs_2_, pred[]{:T(512)S(6)} %eq.40), kind=kLoop, calls=%fused_computation | loop fusion | flops 786432 | bytes 4718593 | tf_op jit(solution)/shard_map/jit(_where)/select_n | solution.py:293
  57.5 2.1 %collective-permute-done.13.refs_0_ = bf16[8,16,2048]{2,1,0:T(8,128)(2,1)S(1)} collective-permute-done((bf16[8,16,2048]{2,1,0:T(8,128)(2,1)}, bf16[8,16,2048]{2,1,0:T(8,128)(2,1)S(1)}, u32[]{:S(2)}, u32[]{:S(2)}) %collective-permute-start.13) | collective-permute-done | bytes 524320 | tf_op jit(solution)/shard_map/ppermute | solution.py:41
  59.6 1.6 %collective-permute-start.14 = (bf16[8,16,2048]{2,1,0:T(8,128)(2,1)}, bf16[8,16,2048]{2,1,0:T(8,128)(2,1)S(1)}, u32[]{:S(2)}, u32[]{:S(2)}) collective-permute-start(bf16[8,16,2048]{2,1,0:T(8,128)(2,1)} %copy-done.10), channel_id=1, source_target_pairs={{0,8},{4,12},{8,0},{12,4},{1,9},{5,13},{9,1},{13,5},{2,10},{6,14},... | collective-permute-start | bytes 1572872 | tf_op jit(solution)/shard_map/ppermute | solution.py:41
  62.5 11.2 %collective-permute-done.14.refs_1_ = bf16[8,16,2048]{2,1,0:T(8,128)(2,1)S(1)} collective-permute-done((bf16[8,16,2048]{2,1,0:T(8,128)(2,1)}, bf16[8,16,2048]{2,1,0:T(8,128)(2,1)S(1)}, u32[]{:S(2)}, u32[]{:S(2)}) %collective-permute-start.14) | collective-permute-done | bytes 524320 | tf_op jit(solution)/shard_map/ppermute | solution.py:41
  76.3 11.5 %collective-permute-done.15.refs_2_ = bf16[8,16,2048]{2,1,0:T(8,128)(2,1)S(1)} collective-permute-done((bf16[8,16,2048]{2,1,0:T(8,128)(2,1)S(1)}, bf16[8,16,2048]{2,1,0:T(8,128)(2,1)S(1)}, u32[]{:S(2)}, u32[]{:S(2)}) %collective-permute-start.15) | collective-permute-done | bytes 524320 | tf_op jit(solution)/shard_map/ppermute | solution.py:41
  87.8 22.1 %collective-permute-start.16 = (f32[16,512]{1,0:T(8,128)S(1)}, f32[16,512]{1,0:T(8,128)S(1)}, u32[]{:S(2)}, u32[]{:S(2)}) collective-permute-start(f32[16,512]{1,0:T(8,128)S(1)} %add.16.refs_6_), channel_id=1, source_target_pairs={{0,2},{1,3},{2,0},{3,1},{4,6},{5,7},{6,4},{7,5},{8,10},{9,11},{10,... | collective-permute-start | bytes 98312 | tf_op jit(solution)/shard_map/ppermute | solution.py:298
  109.9 8.0 %add_part.6.refs_5_ = f32[512,2048]{1,0:T(8,128)S(1)} custom-call(s32[8]{0:T(128)S(1)} %dynamic-slice_bitcast_fusion.refs_0_.info, bf16[512,2048]{1,0:T(8,128)(2,1)S(1)} %collective-permute-done.8.refs_1_, bf16[512,2048]{1,0:T(8,128)(2,1)} %collective-permute-done.7.refs_2_, bf16[8192,2048]{1,0:T(8,128)(2,1)} %weight.1, ...), custom_call_target="tpu_custom_call", output_to_operand_aliasing={{}: (4, {})} | custom-call | flops 4294967296 | bytes 16777216 | tf_op jit(solution)/shard_map/add_part/pallas_call | solution.py:231
  117.9 2.8 %choose_blocks.1.refs_8_ = bf16[256,2048]{1,0:T(8,128)(2,1)S(1)} custom-call(s32[16]{0:T(128)S(1)} %get-tuple-element.41.source, s32[16]{0:T(128)S(1)} %get-tuple-element.43.place, bf16[32,16,2048]{2,1,0:T(8,128)(2,1)S(1)} %copy-done.6, bf16[8,16,2048]{2,1,0:T(8,128)(2,1)S(1)} %collective-permute-done.13.refs_0_, ...), custom_call_target="tpu_custom_call" | custom-call | bytes 2097152 | tf_op jit(solution)/shard_map/choose_blocks/pallas_call | solution.py:106
  122.1 8.4 %add_part.7.refs_4_ = f32[512,2048]{1,0:T(8,128)S(1)} custom-call(s32[8]{0:T(128)S(1)} %dynamic-slice_bitcast_fusion.refs_0_.info, bf16[512,2048]{1,0:T(8,128)(2,1)S(1)} %collective-permute-done.8.refs_1_, bf16[512,2048]{1,0:T(8,128)(2,1)S(1)} %collective-permute-done.11.refs_2_, ...), custom_call_target="tpu_custom_call", output_to_operand_aliasing={{}: (5, {})} | custom-call | flops 4294967296 | bytes 16777216 | tf_op jit(solution)/shard_map/add_part/pallas_call | solution.py:231
  130.6 10.5 %copy-done = bf16[8192,2048]{1,0:T(8,128)(2,1)S(1)} copy-done((bf16[8192,2048]{1,0:T(8,128)(2,1)S(1)}, bf16[8192,2048]{1,0:T(8,128)(2,1)}, u32[]{:S(2)}) %copy-start) | copy-done | bytes 33554456
  142.2 5.4 %add_part.8.refs_5_ = bf16[512,2048]{1,0:T(8,128)(2,1)} custom-call(s32[8]{0:T(128)S(1)} %dynamic-slice_bitcast_fusion.refs_0_.info, bf16[384,2048]{1,0:T(8,128)(2,1)S(1)} %collective-permute-done.17.refs_1_, bf16[384,2048]{1,0:T(8,128)(2,1)S(1)} %collective-permute-done.18.refs_2_, bf16[2048,2048]{1,0:T(8,128)(2,1)S(1)} %fetch_part.1.refs_3_, ...), custom_call_target="tpu_custom_call" | custom-call | flops 3221225472 | bytes 14680064 | tf_op jit(solution)/shard_map/add_part/pallas_call | solution.py:231
  147.7 3.3 %collective-permute-done.10.refs_2_ = bf16[128,2048]{1,0:T(8,128)(2,1)S(1)} collective-permute-done((bf16[128,2048]{1,0:T(8,128)(2,1)S(1)}, bf16[128,2048]{1,0:T(8,128)(2,1)S(1)}, u32[]{:S(2)}, u32[]{:S(2)}) %collective-permute-start.10) | collective-permute-done | bytes 524320 | tf_op jit(solution)/shard_map/ppermute | solution.py:295
  151.0 2.9 %add_part.9 = bf16[512,2048]{1,0:T(8,128)(2,1)} custom-call(s32[8]{0:T(128)S(1)} %dynamic-slice_bitcast_fusion.refs_0_.info, bf16[128,2048]{1,0:T(8,128)(2,1)S(1)} %collective-permute-done.9.refs_1_, bf16[128,2048]{1,0:T(8,128)(2,1)S(1)} %collective-permute-done.10.refs_2_, ...), custom_call_target="tpu_custom_call", output_to_operand_aliasing={{}: (5, {})} | custom-call | flops 1073741824 | bytes 10485760 | tf_op jit(solution)/shard_map/add_part/pallas_call | solution.py:231
  (57 shorter events, 18.3 us)
Async XLA Ops:
  0.0 52.7 %collective-permute-start.8 = (bf16[512,2048]{1,0:T(8,128)(2,1)}, bf16[512,2048]{1,0:T(8,128)(2,1)S(1)}, u32[]{:S(2)}, u32[]{:S(2)}) collective-permute-start(bf16[512,2048]{1,0:T(8,128)(2,1)} %features.1), channel_id=1, source_target_pairs={{1,0},{2,1},{3,2},{5,4},{6,5},{7,6},{9,8},{10,9},{11,10},{13,12},{... | collective-permute-start | bytes 6291464 | tf_op jit(solution)/shard_map/ppermute | solution.py:282
  1.3 51.4 %collective-permute-start.7 = (bf16[512,2048]{1,0:T(8,128)(2,1)}, bf16[512,2048]{1,0:T(8,128)(2,1)}, u32[]{:S(2)}, u32[]{:S(2)}) collective-permute-start(bf16[512,2048]{1,0:T(8,128)(2,1)} %features.1), channel_id=1, source_target_pairs={{0,1},{1,2},{2,3},{4,5},{5,6},{6,7},{8,9},{9,10},{10,11},{12,13},{... | collective-permute-start | bytes 6291464 | tf_op jit(solution)/shard_map/ppermute | solution.py:282
  10.6 2.1 %collective-permute-start = (s32[8]{0:T(128)S(1)}, s32[8]{0:T(128)S(1)}, u32[]{:S(2)}, u32[]{:S(2)}) collective-permute-start(s32[8]{0:T(128)S(1)} %get-tuple-element.47), channel_id=1, source_target_pairs={{0,4},{4,0},{8,12},{12,8},{1,5},{5,1},{9,13},{13,9},{2,6},{6,2},{1... | collective-permute-start | bytes 104 | tf_op jit(solution)/shard_map/ppermute | solution.py:41
  10.7 3.6 %collective-permute-start.1 = (s32[8]{0:T(128)S(1)}, s32[8]{0:T(128)S(1)}, u32[]{:S(2)}, u32[]{:S(2)}) collective-permute-start(s32[8]{0:T(128)S(1)} %get-tuple-element.46), channel_id=1, source_target_pairs={{0,8},{4,12},{8,0},{12,4},{1,9},{5,13},{9,1},{13,5},{2,10},{6,14},... | collective-permute-start | bytes 104 | tf_op jit(solution)/shard_map/ppermute | solution.py:41
  12.6 3.0 %collective-permute-start.2 = (s32[8]{0:T(128)S(1)}, s32[8]{0:T(128)S(1)}, u32[]{:S(2)}, u32[]{:S(2)}) collective-permute-start(s32[8]{0:T(128)S(1)} %get-tuple-element.45), channel_id=1, source_target_pairs={{0,12},{4,8},{8,4},{12,0},{1,13},{5,9},{9,5},{13,1},{2,14},{6,10},... | collective-permute-start | bytes 104 | tf_op jit(solution)/shard_map/ppermute | solution.py:41
  19.1 16.1 %collective-permute-start.3 = (bf16[8,16,2048]{2,1,0:T(8,128)(2,1)}, bf16[8,16,2048]{2,1,0:T(8,128)(2,1)S(1)}, u32[]{:S(2)}, u32[]{:S(2)}) collective-permute-start(bf16[8,16,2048]{2,1,0:T(8,128)(2,1)} %get-tuple-element.28), channel_id=1, source_target_pairs={{0,4},{4,0},{8,12},{12,8},{1,5},{5,1},{9,13},{13,9},{2,6},{6,2},{1... | collective-permute-start | bytes 1572872 | tf_op jit(solution)/shard_map/ppermute | solution.py:41
  19.6 15.6 %collective-permute-start.4 = (bf16[8,16,2048]{2,1,0:T(8,128)(2,1)}, bf16[8,16,2048]{2,1,0:T(8,128)(2,1)S(1)}, u32[]{:S(2)}, u32[]{:S(2)}) collective-permute-start(bf16[8,16,2048]{2,1,0:T(8,128)(2,1)} %get-tuple-element.29), channel_id=1, source_target_pairs={{0,8},{4,12},{8,0},{12,4},{1,9},{5,13},{9,1},{13,5},{2,10},{6,14},... | collective-permute-start | bytes 1572872 | tf_op jit(solution)/shard_map/ppermute | solution.py:41
  19.9 24.3 %collective-permute-start.5 = (bf16[8,16,2048]{2,1,0:T(8,128)(2,1)}, bf16[8,16,2048]{2,1,0:T(8,128)(2,1)}, u32[]{:S(2)}, u32[]{:S(2)}) collective-permute-start(bf16[8,16,2048]{2,1,0:T(8,128)(2,1)} %get-tuple-element.30), channel_id=1, source_target_pairs={{0,12},{4,8},{8,4},{12,0},{1,13},{5,9},{9,5},{13,1},{2,14},{6,10},... | collective-permute-start | bytes 1572872 | tf_op jit(solution)/shard_map/ppermute | solution.py:41
  31.3 16.4 %copy-start.1 = (f32[512,2048]{1,0:T(8,128)}, f32[512,2048]{1,0:T(8,128)S(1)}, u32[]{:S(2)}) copy-start(f32[512,2048]{1,0:T(8,128)S(1)} %add_part.5.refs_4_) | copy-start | bytes 12582916
  31.3 12.9 %copy-start.4 = (bf16[32,16,2048]{2,1,0:T(8,128)(2,1)S(1)}, bf16[32,16,2048]{2,1,0:T(8,128)(2,1)}, u32[]{:S(2)}) copy-start(bf16[32,16,2048]{2,1,0:T(8,128)(2,1)} %pool.2) | copy-start | bytes 6291460
  47.8 4.9 %collective-permute-start.6 = (f32[16,512]{1,0:T(8,128)S(1)}, f32[16,512]{1,0:T(8,128)S(1)}, u32[]{:S(2)}, u32[]{:S(2)}) collective-permute-start(f32[16,512]{1,0:T(8,128)S(1)} %shrink.1), channel_id=1, source_target_pairs={{0,1},{1,0},{2,3},{3,2},{4,5},{5,4},{6,7},{7,6},{8,9},{9,8},{10,11... | collective-permute-start | bytes 98312 | tf_op jit(solution)/shard_map/ppermute | solution.py:288
  52.6 21.1 %copy-start.9 = (bf16[8,16,2048]{2,1,0:T(8,128)(2,1)S(1)}, bf16[8,16,2048]{2,1,0:T(8,128)(2,1)}, u32[]{:S(2)}) copy-start(bf16[8,16,2048]{2,1,0:T(8,128)(2,1)} %copy-done.8) | copy-start | bytes 1572868
  52.7 57.3 %copy-start.2 = (f32[512,2048]{1,0:T(8,128)S(1)}, f32[512,2048]{1,0:T(8,128)}, u32[]{:S(2)}) copy-start(f32[512,2048]{1,0:T(8,128)} %copy-done.1) | copy-start | bytes 12582916
  54.4 6.8 %collective-permute-start.17 = (bf16[384,2048]{1,0:T(8,128)(2,1)S(1)}, bf16[384,2048]{1,0:T(8,128)(2,1)S(1)}, u32[]{:S(2)}, u32[]{:S(2)}) collective-permute-start(bf16[384,2048]{1,0:T(8,128)(2,1)S(1)} %slice_select_fusion), channel_id=1, source_target_pairs={{1,2},{2,1},{5,6},{6,5},{9,10},{10,9},{13,14},{14,13},{17,18},{18,... | collective-permute-start | bytes 4718600 | tf_op jit(solution)/shard_map/ppermute | solution.py:293
  55.3 66.8 %collective-permute-start.11 = (bf16[512,2048]{1,0:T(8,128)(2,1)S(1)}, bf16[512,2048]{1,0:T(8,128)(2,1)S(1)}, u32[]{:S(2)}, u32[]{:S(2)}) collective-permute-start(bf16[512,2048]{1,0:T(8,128)(2,1)S(1)} %collective-permute-done.8.refs_1_), channel_id=1, source_target_pairs={{1,0},{5,4},{9,8},{13,12},{17,16},{21,20},{25,24},{29,28}} | collective-permute-start | bytes 6291464 | tf_op jit(solution)/shard_map/ppermute | solution.py:290
  56.6 65.5 %collective-permute-start.12 = (bf16[512,2048]{1,0:T(8,128)(2,1)}, bf16[512,2048]{1,0:T(8,128)(2,1)S(1)}, u32[]{:S(2)}, u32[]{:S(2)}) collective-permute-start(bf16[512,2048]{1,0:T(8,128)(2,1)} %collective-permute-done.7.refs_2_), channel_id=1, source_target_pairs={{2,3},{6,7},{10,11},{14,15},{18,19},{22,23},{26,27},{30,31}} | collective-permute-start | bytes 6291464 | tf_op jit(solution)/shard_map/ppermute | solution.py:290
  57.4 2.2 %collective-permute-start.13 = (bf16[8,16,2048]{2,1,0:T(8,128)(2,1)}, bf16[8,16,2048]{2,1,0:T(8,128)(2,1)S(1)}, u32[]{:S(2)}, u32[]{:S(2)}) collective-permute-start(bf16[8,16,2048]{2,1,0:T(8,128)(2,1)} %copy-done.11), channel_id=1, source_target_pairs={{0,4},{4,0},{8,12},{12,8},{1,5},{5,1},{9,13},{13,9},{2,6},{6,2},{1... | collective-permute-start | bytes 1572872 | tf_op jit(solution)/shard_map/ppermute | solution.py:41
  59.6 14.2 %collective-permute-start.14 = (bf16[8,16,2048]{2,1,0:T(8,128)(2,1)}, bf16[8,16,2048]{2,1,0:T(8,128)(2,1)S(1)}, u32[]{:S(2)}, u32[]{:S(2)}) collective-permute-start(bf16[8,16,2048]{2,1,0:T(8,128)(2,1)} %copy-done.10), channel_id=1, source_target_pairs={{0,8},{4,12},{8,0},{12,4},{1,9},{5,13},{9,1},{13,5},{2,10},{6,14},... | collective-permute-start | bytes 1572872 | tf_op jit(solution)/shard_map/ppermute | solution.py:41
  61.2 81.0 %collective-permute-start.18 = (bf16[384,2048]{1,0:T(8,128)(2,1)S(1)}, bf16[384,2048]{1,0:T(8,128)(2,1)S(1)}, u32[]{:S(2)}, u32[]{:S(2)}) collective-permute-start(bf16[384,2048]{1,0:T(8,128)(2,1)S(1)} %collective-permute-done.17.refs_1_), channel_id=1, source_target_pairs={{1,0},{2,3},{5,4},{6,7},{9,8},{10,11},{13,12},{14,15},{17,16},{18,... | collective-permute-start | bytes 4718600 | tf_op jit(solution)/shard_map/ppermute | solution.py:295
  73.8 14.0 %collective-permute-start.15 = (bf16[8,16,2048]{2,1,0:T(8,128)(2,1)S(1)}, bf16[8,16,2048]{2,1,0:T(8,128)(2,1)S(1)}, u32[]{:S(2)}, u32[]{:S(2)}) collective-permute-start(bf16[8,16,2048]{2,1,0:T(8,128)(2,1)S(1)} %copy-done.9), channel_id=1, source_target_pairs={{0,12},{4,8},{8,4},{12,0},{1,13},{5,9},{9,5},{13,1},{2,14},{6,10},... | collective-permute-start | bytes 1572872 | tf_op jit(solution)/shard_map/ppermute | solution.py:41
  75.4 42.5 %copy-start.6 = (bf16[32,16,2048]{2,1,0:T(8,128)(2,1)S(1)}, bf16[32,16,2048]{2,1,0:T(8,128)(2,1)}, u32[]{:S(2)}) copy-start(bf16[32,16,2048]{2,1,0:T(8,128)(2,1)} %pool.3) | copy-start | bytes 6291460
  75.5 45.3 %collective-permute-start.9 = (bf16[128,2048]{1,0:T(8,128)(2,1)S(1)}, bf16[128,2048]{1,0:T(8,128)(2,1)S(1)}, u32[]{:S(2)}, u32[]{:S(2)}) collective-permute-start(bf16[128,2048]{1,0:T(8,128)(2,1)S(1)} %slice_select_fusion.1), channel_id=1, source_target_pairs={{1,2},{2,1},{5,6},{6,5},{9,10},{10,9},{13,14},{14,13},{17,18},{18,... | collective-permute-start | bytes 1572872 | tf_op jit(solution)/shard_map/ppermute | solution.py:293
  87.8 34.3 %collective-permute-start.16 = (f32[16,512]{1,0:T(8,128)S(1)}, f32[16,512]{1,0:T(8,128)S(1)}, u32[]{:S(2)}, u32[]{:S(2)}) collective-permute-start(f32[16,512]{1,0:T(8,128)S(1)} %add.16.refs_6_), channel_id=1, source_target_pairs={{0,2},{1,3},{2,0},{3,1},{4,6},{5,7},{6,4},{7,5},{8,10},{9,11},{10,... | collective-permute-start | bytes 98312 | tf_op jit(solution)/shard_map/ppermute | solution.py:298
  120.8 30.2 %collective-permute-start.10 = (bf16[128,2048]{1,0:T(8,128)(2,1)S(1)}, bf16[128,2048]{1,0:T(8,128)(2,1)S(1)}, u32[]{:S(2)}, u32[]{:S(2)}) collective-permute-start(bf16[128,2048]{1,0:T(8,128)(2,1)S(1)} %collective-permute-done.9.refs_1_), channel_id=1, source_target_pairs={{1,0},{2,3},{5,4},{6,7},{9,8},{10,11},{13,12},{14,15},{17,16},{18,... | collective-permute-start | bytes 1572872 | tf_op jit(solution)/shard_map/ppermute | solution.py:295
  (7 other events, 40.6 us)

commit v5 on v4

--- a/solution.py
+++ b/solution.py
@@ -150,16 +150,16 @@
     return jnp.where(own, tall, 0.0).astype(BF16)
 
 
-def add_kernel(choices, tail, *refs):
-    info, cands = refs[0], refs[1 : 1 + choices]
-    rest = list(refs[1 + choices :])
+def add_kernel(tail, *refs):
+    info, rest = refs[0], list(refs[1:])
+    cands = [[rest.pop(0) for _ in range(n)] for n in tail["cands"]]
     weight = rest.pop(0)
     acc = rest.pop(0) if tail["acc"] else None
     sums = [rest.pop(0) for _ in range(tail["sums"])]
     up = rest.pop(0) if sums else None
     if tail["kept"]:
         rest.pop(0)
-    out, x, sem = rest[:3]
+    out, x, sems = rest[:3]
     wide = rest[3] if sums else None
     which = info[tail["which"]]
 
@@ -168,9 +168,11 @@
 
             @pl.when(which == i)
             def _():
-                rows = x.shape[0]
-                first = 0 if cand.shape[0] == rows else tail["first"]
-                act(pltpu.make_async_copy(cand.at[pl.ds(first, rows)], x, sem))
+                first = 0
+                for c, piece in enumerate(cand):
+                    rows = piece.shape[0]
+                    act(pltpu.make_async_copy(piece, x.at[pl.ds(first, rows)], sems.at[c]))
+                    first += rows
 
     @pl.when(pl.program_id(0) == 0)
     def _():
@@ -192,21 +194,19 @@
 
 
 def add_part(info, at, cands, weight, acc=None, sums=(), up=None, blocks=0, final=None, tile=512):
-    whole, depth = cands[0].shape
+    rows, depth = sum(p.shape[0] for p in cands[0]), cands[0][0].shape[1]
     cols = weight.shape[1]
-    first, end, kept = final if final else (0, whole, None)
-    whole = acc.shape[0] if final else whole
-    rows = end - first
+    first, kept = final if final else (0, None)
     tail = {
+        "cands": [len(c) for c in cands],
         "acc": acc is not None,
         "blocks": blocks,
         "sums": len(sums),
         "kept": kept is not None,
         "which": at,
-        "first": first,
     }
-    args = [info, *cands, weight]
-    specs = [ANY] * len(cands)
+    args = [info] + [p for cand in cands for p in cand] + [weight]
+    specs = [ANY] * (len(args) - 2)
     if final:
         specs.append(VMEM)
     else:
@@ -218,8 +218,9 @@
             aliases[len(args)] = 0
         args.append(acc)
         specs.append(block)
-    scratch = [pltpu.VMEM((rows, depth), BF16), pltpu.SemaphoreType.DMA]
-    if blocks:
+    most = max(tail["cands"])
+    scratch = [pltpu.VMEM((rows, depth), BF16), pltpu.SemaphoreType.DMA((most,))]
+    if sums:
         args += [*sums, up]
         specs += [pl.BlockSpec(s.shape, lambda j, info: (0, 0)) for s in sums]
         specs.append(pl.BlockSpec((up.shape[0], tile), lambda j, info: (0, j)))
@@ -229,8 +230,8 @@
         args.append(kept)
         specs.append(ANY)
     return pl.pallas_call(
-        functools.partial(add_kernel, len(cands), tail),
-        out_shape=jax.ShapeDtypeStruct((whole, cols), BF16 if final else F32),
+        functools.partial(add_kernel, tail),
+        out_shape=jax.ShapeDtypeStruct((acc.shape[0] if final else rows, cols), BF16 if final else F32),
         grid_spec=pltpu.PrefetchScalarGridSpec(
             num_scalar_prefetch=1, grid=(cols // tile,), in_specs=specs, out_specs=block, scratch_shapes=scratch
         ),
@@ -243,6 +244,33 @@
     )(*args)
 
 
+def split_kernel(starts, count, *refs):
+    arrays, outs, sems = refs[:count], refs[count:-1], refs[-1]
+    copies = []
+    for c, (first, end) in enumerate(zip(starts, starts[1:])):
+        for k, x in enumerate(arrays):
+            at = c * count + k
+            copies.append(pltpu.make_async_copy(x.at[pl.ds(first, end - first)], outs[at], sems.at[at]))
+    for copy in copies:
+        copy.start()
+    for copy in copies:
+        copy.wait()
+
+
+def split_rows(arrays, starts):
+    shapes = [jax.ShapeDtypeStruct((b - a, x.shape[1]), x.dtype) for a, b in zip(starts, starts[1:]) for x in arrays]
+    return pl.pallas_call(
+        functools.partial(split_kernel, starts, len(arrays)),
+        out_shape=shapes,
+        in_specs=[ANY] * len(arrays),
+        out_specs=[ANY] * len(shapes),
+        scratch_shapes=[pltpu.SemaphoreType.DMA((len(shapes),))],
+        cost_estimate=pl.CostEstimate(flops=0, bytes_accessed=sum(4 * x.size for x in arrays), transcendentals=0),
+        compiler_params=params(1),
+        name="split_rows",
+    )(*arrays)
+
+
 def fetch_kernel(at, info, weight, out, sem):
     depth = out.shape[0]
     copy = pltpu.make_async_copy(weight.at[pl.ds(pl.multiple_of(info[at] * depth, depth), depth)], out, sem)
@@ -265,43 +293,43 @@
 
 CHOICES = (
     (0, 0, 0, 1, 1, 2, 1, 3),
-    (0, 1, 1, 0, 0, 2, 0, 3),
-    (0, 2, 1, 1, 0, 3, 0, 0),
-    (0, 3, 1, 2, 2, 1, 1, 0),
+    (0, 1, 0, 0, 0, 2, 0, 3),
+    (0, 2, 0, 3, 0, 1, 0, 0),
+    (0, 3, 0, 2, 1, 1, 1, 0),
 )
 
 
 def on_line_of_four(features, query_weight, adapter_down, adapter_up, block_owner, block_slot, rep):
     z = lax.axis_index("tp")
     info = lax.dynamic_index_in_dim(jnp.array(CHOICES, jnp.int32), z, 0, keepdims=False)
-    right, left = [(0, 1), (1, 2), (2, 3)], [(1, 0), (2, 1), (3, 2)]
+    outer, middle, outward = [(i, i ^ 1) for i in range(4)], [(1, 2), (2, 1)], [(1, 0), (2, 3)]
     rows, blocks = features.shape[0], block_slot.shape[0]
     cut = rows * PIECE[0] // PIECE[1]
 
     asked, source, place = wanted(block_owner, block_slot, rep)
-    r1, l1 = lax.ppermute(features, "tp", right), lax.ppermute(features, "tp", left)
+    near = lax.ppermute(features, "tp", outer)
+    across = lax.ppermute(features, "tp", middle)
     lists = [swap(asked[i], i, rep) for i in range(1, rep)]
     downs = [swap(p, i + 1, rep) for i, p in enumerate(pack(lists, adapter_down))]
-    acc = add_part(after(info, *lists), 0, [features], query_weight)
+    acc = add_part(after(info, *lists), 0, [[features]], query_weight)
     packed = pack([after(lists[0], acc)] + lists[1:], adapter_up)
     mine = shrink(after(source, acc, packed[0]), place, features, adapter_down, downs)
-    pair = mine + lax.ppermute(mine, "tp", [(i, i ^ 1) for i in range(4)])
-
-    l2, r2 = lax.ppermute(after(l1, pair), "tp", [(1, 0)]), lax.ppermute(after(r1, pair), "tp", [(2, 3)])
-    inner, bounds = after(z, pair), (0, cut, rows)
-    cross = [
-        lax.ppermute(jnp.where(inner == 1, r1[i:j], l1[i:j]), "tp", [(1, 2), (2, 1)]) for i, j in zip(bounds, bounds[1:])
-    ]
-    far = [lax.ppermute(c, "tp", [(1, 0), (2, 3)]) for c in cross]
-
-    ups = in_turn([after(packed[0], pair), *packed[1:]], rep)
-    shares = [pair, lax.ppermute(after(pair, ups[-1]), "tp", [(i, i ^ 2) for i in range(4)])]
-    acc = add_part(after(info, pair), 2, [l1, r1], query_weight, acc)
+    pair = mine + lax.ppermute(mine, "tp", outer)
+    shares = [pair, lax.ppermute(pair, "tp", [(i, i ^ 2) for i in range(4)])]
+    held = after(near, *shares[:1])
+    halves = held[:cut], held[cut:]
+    passed = lax.ppermute(after(across, *shares[:1]), "tp", outward)
+    inner = [lax.ppermute(p, "tp", middle) for p in halves]
+    last = [lax.ppermute(p, "tp", outward) for p in inner]
+
+    ups = in_turn([after(packed[0], *shares[:1]), *packed[1:]], rep)
+    acc = add_part(after(info, *shares[:1]), 2, [[near]], query_weight, acc)
+    base = acc
     up = chosen_blocks(after(source, acc), place, adapter_up, ups)
-    acc = add_part(info, 4, [l1, l2, r2], query_weight, acc, shares, up, blocks)
-    weight = fetch_part(after(info, acc), 7, query_weight, features.shape[1])
-    out = add_part(info, 6, [cross[0], far[0]], weight, acc, final=(0, cut, None), tile=1024)
-    return add_part(info, 6, [cross[1], far[1]], weight, acc, final=(cut, rows, out), tile=1024)
+    acc = add_part(info, 4, [[across], [passed]], query_weight, acc, shares, up, blocks)
+    weight = fetch_part(after(info, base), 7, query_weight, features.shape[1])
+    out = add_part(info, 6, [inner[:1], last[:1]], weight, acc, final=(0, None), tile=1024)
+    return add_part(info, 6, [inner[1:], last[1:]], weight, acc, final=(cut, out), tile=1024)
 
 
 def anywhere(features, query_weight, adapter_down, adapter_up, block_owner, block_slot, rep):

time: 155 us -> 150 us (0.968)
  waiting for transfers between devices: 44.5 us -> 30.6 us
  starting transfers between devices: 43.4 us -> 56.7 us
  other arithmetic: 5.17 us -> 2.34 us
    ppermute x10 -> x9, starting transfers between devices: 37.1 us -> 50.6 us  [the longest x1 37.7 us: on_line_of_four(): shares = [pair, lax.ppermute(pair, 'tp', [(i, i ^ 2) for i in range(4)])]]
    ppermute x9, waiting for transfers between devices: 36.8 us -> 25.4 us  [swap(): return lax.ppermute(x, 'rep', [(r, r ^ distance) for r in range(rep)])]
    select_n x2 -> x0, other arithmetic: 2.82 us -> none  [on_line_of_four(): jnp.where(inner == 1, r1[i:j], l1[i:j])]
    ppermute x10 -> x9, waiting for transfers between devices: 7.79 us -> 5.1 us  [the longest x1 2.97 us: on_line_of_four(): pair = mine + lax.ppermute(mine, 'tp', outer)]
    unnamed x24 -> x10, local copies, waits for them, and re-layouts: 14.6 us -> 13.7 us
  transfers between devices with their start and end apart: 19 -> 18, of which waited for: 8 -> 7; matrix products, arithmetic and copies ran while one was open for 3% -> 2% of each run, Pallas kernels for 27% -> 28%
where the time goes in v5:
time: 150 us
  starting transfers between devices  56.7 us (38%)
  Pallas kernels  45.1 us (30%)
  waiting for transfers between devices  30.6 us (20%)
  local copies, waits for them, and re-layouts  14.6 us (10%)
  other arithmetic  2.34 us (2%)
    ppermute x1, starting transfers between devices, on_line_of_four(): shares = [pair, lax.ppermute(pair, 'tp', [(i, i ^ 2) for i in range(4)])]  37.7 us
    pallas_call x5, Pallas kernels, add_part(): pl.pallas_call(functools.partial(add_kernel, tail), out_shape=jax.ShapeDt...  32.8 us
    ppermute x9, waiting for transfers between devices, swap(): return lax.ppermute(x, 'rep', [(r, r ^ distance) for r in range(rep)])  25.4 us
    unnamed x10, local copies, waits for them, and re-layouts  13.7 us
    ppermute x9, starting transfers between devices, swap(): return lax.ppermute(x, 'rep', [(r, r ^ distance) for r in range(rep)])  6.11 us
    pallas_call x2, Pallas kernels, pack(): pl.pallas_call(functools.partial(pack_kernel, count, cap), out_shape=[sha...  4.9 us
    pallas_call x1, Pallas kernels, shrink(): pl.pallas_call(shrink_kernel, out_shape=jax.ShapeDtypeStruct((rank, rows)...  3.49 us
    ppermute x1, starting transfers between devices, on_line_of_four(): near = lax.ppermute(features, 'tp', outer)  3.02 us
  transfers between devices with their start and end apart: 18, of which 7 were waited for; matrix products, arithmetic and copies ran while one was open for 2% of the time, Pallas kernels for 28%

profile of v5, /device:TPU:0, one launch (start us, length us, event | category | flops | bytes accessed | tf_op | source)
XLA Modules:
  0.0 149.6 jit_solution(1961441835539088847)
XLA Ops:
  0.0 3.0 %collective-permute-start = (bf16[512,2048]{1,0:T(8,128)(2,1)}, bf16[512,2048]{1,0:T(8,128)(2,1)S(1)}, u32[]{:S(2)}, u32[]{:S(2)}) collective-permute-start(bf16[512,2048]{1,0:T(8,128)(2,1)} %features.1), channel_id=1, source_target_pairs={{0,1},{1,0},{2,3},{3,2},{4,5},{5,4},{6,7},{7,6},{8,9},{9,8},{10,11... | collective-permute-start | bytes 6291464 | tf_op jit(solution)/shard_map/ppermute | solution.py:310
  3.0 2.0 %collective-permute-start.10 = (bf16[512,2048]{1,0:T(8,128)(2,1)}, bf16[512,2048]{1,0:T(8,128)(2,1)}, u32[]{:S(2)}, u32[]{:S(2)}) collective-permute-start(bf16[512,2048]{1,0:T(8,128)(2,1)} %features.1), channel_id=1, source_target_pairs={{1,2},{2,1},{5,6},{6,5},{9,10},{10,9},{13,14},{14,13},{17,18},{18,... | collective-permute-start | bytes 6291464 | tf_op jit(solution)/shard_map/ppermute | solution.py:311
  11.6 1.6 %copy-done.1 = bf16[32,16,2048]{2,1,0:T(8,128)(2,1)S(1)} copy-done((bf16[32,16,2048]{2,1,0:T(8,128)(2,1)S(1)}, bf16[32,16,2048]{2,1,0:T(8,128)(2,1)}, u32[]{:S(2)}) %copy-start.1) | copy-done | bytes 2097176
  13.2 1.9 %pack_blocks.3 = (bf16[8,16,2048]{2,1,0:T(8,128)(2,1)}, bf16[8,16,2048]{2,1,0:T(8,128)(2,1)}, bf16[8,16,2048]{2,1,0:T(8,128)(2,1)}) custom-call(s32[8]{0:T(128)S(1)} %collective-permute-done.1.refs_0_, s32[8]{0:T(128)S(1)} %collective-permute-done.2.refs_1_, s32[8]{0:T(128)S(1)} %collective-permute-done.3.refs_2_, bf16[32,16,2048]{2,1,0:T(8,128)(2,1)S(1)} %copy-done.1), custom_call_target="tpu_custom_call" | custom-call | bytes 3145728 | tf_op jit(solution)/shard_map/pack_blocks/pallas_call | solution.py:71
  17.7 1.6 %copy-done.4 = bf16[512,2048]{1,0:T(8,128)(2,1)S(1)} copy-done((bf16[512,2048]{1,0:T(8,128)(2,1)S(1)}, bf16[512,2048]{1,0:T(8,128)(2,1)}, u32[]{:S(2)}) %copy-start.4) | copy-done | bytes 2097176
  19.3 8.0 %add_part.5.refs_3_ = f32[512,2048]{1,0:T(8,128)S(1)} custom-call(s32[8]{0:T(128)S(1)} %dynamic-slice_bitcast_fusion.refs_0_.info, bf16[512,2048]{1,0:T(8,128)(2,1)S(1)} %copy-done.4, bf16[8192,2048]{1,0:T(8,128)(2,1)} %refs_3_.5), custom_call_target="tpu_custom_call" | custom-call | flops 4294967296 | bytes 16777216 | tf_op jit(solution)/shard_map/add_part/pallas_call | solution.py:232
  27.3 3.0 %pack_blocks.2 = (bf16[8,16,2048]{2,1,0:T(8,128)(2,1)S(1)}, bf16[8,16,2048]{2,1,0:T(8,128)(2,1)S(1)}, bf16[8,16,2048]{2,1,0:T(8,128)(2,1)S(1)}) custom-call(s32[8]{0:T(128)S(1)} %collective-permute-done.1.refs_0_, s32[8]{0:T(128)S(1)} %collective-permute-done.2.refs_1_, s32[8]{0:T(128)S(1)} %collective-permute-done.3.refs_2_, bf16[32,16,2048]{2,1,0:T(8,128)(2,1)S(1)} %copy-done.3), custom_call_target="tpu_custom_call" | custom-call | bytes 3145728 | tf_op jit(solution)/shard_map/pack_blocks/pallas_call | solution.py:71
  30.4 10.2 %collective-permute-done.6.refs_2_ = bf16[8,16,2048]{2,1,0:T(8,128)(2,1)} collective-permute-done((bf16[8,16,2048]{2,1,0:T(8,128)(2,1)}, bf16[8,16,2048]{2,1,0:T(8,128)(2,1)}, u32[]{:S(2)}, u32[]{:S(2)}) %collective-permute-start.6) | collective-permute-done | bytes 524320 | tf_op jit(solution)/shard_map/ppermute | solution.py:41
  40.6 3.5 %shrink.1 = f32[16,512]{1,0:T(8,128)S(1)} custom-call(s32[16]{0:T(128)S(1)} %get-tuple-element.33.source, s32[16]{0:T(128)S(1)} %get-tuple-element.39.place, bf16[512,2048]{1,0:T(8,128)(2,1)S(1)} %copy-done.4, bf16[32,16,2048]{2,1,0:T(8,128)(2,1)S(1)} %copy-done.2, bf16[8,16,2048]{2,1,0:T(8,128)(2,1)S(1)} %collective-permute-done.4.refs_0_, ...), custom_call_target="tpu_custom_call" | custom-call | flops 536870912 | bytes 2097152 | tf_op jit(solution)/shard_map/shrink/pallas_call | solution.py:133
  44.1 2.5 %collective-permute-start.7 = (f32[16,512]{1,0:T(8,128)S(1)}, f32[16,512]{1,0:T(8,128)S(1)}, u32[]{:S(2)}, u32[]{:S(2)}) collective-permute-start(f32[16,512]{1,0:T(8,128)S(1)} %shrink.1), channel_id=1, source_target_pairs={{0,1},{1,0},{2,3},{3,2},{4,5},{5,4},{6,7},{7,6},{8,9},{9,8},{10,11... | collective-permute-start | bytes 98312 | tf_op jit(solution)/shard_map/ppermute | solution.py:317
  46.6 3.0 %collective-permute-done.7 = f32[16,512]{1,0:T(8,128)S(1)} collective-permute-done((f32[16,512]{1,0:T(8,128)S(1)}, f32[16,512]{1,0:T(8,128)S(1)}, u32[]{:S(2)}, u32[]{:S(2)}) %collective-permute-start.7) | collective-permute-done | bytes 32800 | tf_op jit(solution)/shard_map/ppermute | solution.py:317
  50.5 1.3 collective-permute-start.11
  51.9 1.3 collective-permute-start.17
  53.7 1.7 %collective-permute-start.14 = (bf16[8,16,2048]{2,1,0:T(8,128)(2,1)S(1)}, bf16[8,16,2048]{2,1,0:T(8,128)(2,1)S(1)}, u32[]{:S(2)}, u32[]{:S(2)}) collective-permute-start(bf16[8,16,2048]{2,1,0:T(8,128)(2,1)S(1)} %get-tuple-element.36), channel_id=1, source_target_pairs={{0,8},{4,12},{8,0},{12,4},{1,9},{5,13},{9,1},{13,5},{2,10},{6,14},... | collective-permute-start | bytes 1572872 | tf_op jit(solution)/shard_map/ppermute | solution.py:41
  55.4 12.3 %collective-permute-done.14.refs_1_ = bf16[8,16,2048]{2,1,0:T(8,128)(2,1)S(1)} collective-permute-done((bf16[8,16,2048]{2,1,0:T(8,128)(2,1)S(1)}, bf16[8,16,2048]{2,1,0:T(8,128)(2,1)S(1)}, u32[]{:S(2)}, u32[]{:S(2)}) %collective-permute-start.14) | collective-permute-done | bytes 524320 | tf_op jit(solution)/shard_map/ppermute | solution.py:41
  69.0 37.7 %collective-permute-start.12 = (f32[16,512]{1,0:T(8,128)S(1)}, f32[16,512]{1,0:T(8,128)S(1)}, u32[]{:S(2)}, u32[]{:S(2)}) collective-permute-start(f32[16,512]{1,0:T(8,128)S(1)} %add.16.refs_5_), channel_id=1, source_target_pairs={{0,2},{1,3},{2,0},{3,1},{4,6},{5,7},{6,4},{7,5},{8,10},{9,11},{10,... | collective-permute-start | bytes 98312 | tf_op jit(solution)/shard_map/ppermute | solution.py:318
  106.8 8.0 %add_part.6.refs_4_ = f32[512,2048]{1,0:T(8,128)S(1)} custom-call(s32[8]{0:T(128)S(1)} %dynamic-slice_bitcast_fusion.refs_0_.info, bf16[512,2048]{1,0:T(8,128)(2,1)S(1)} %collective-permute-done.refs_1_, bf16[8192,2048]{1,0:T(8,128)(2,1)} %refs_3_.5, f32[512,2048]{1,0:T(8,128)S(1)} %add_part.5.refs_3_), custom_call_target="tpu_custom_call", output_to_operand_aliasing={{}: (3, {})} | custom-call | flops 4294967296 | bytes 16777216 | tf_op jit(solution)/shard_map/add_part/pallas_call | solution.py:232
  114.8 10.5 %copy-done = bf16[8192,2048]{1,0:T(8,128)(2,1)S(1)} copy-done((bf16[8192,2048]{1,0:T(8,128)(2,1)S(1)}, bf16[8192,2048]{1,0:T(8,128)(2,1)}, u32[]{:S(2)}) %copy-start) | copy-done | bytes 33554456
  126.5 2.8 %choose_blocks.1.refs_7_ = bf16[256,2048]{1,0:T(8,128)(2,1)S(1)} custom-call(s32[16]{0:T(128)S(1)} %get-tuple-element.33.source, s32[16]{0:T(128)S(1)} %get-tuple-element.39.place, bf16[32,16,2048]{2,1,0:T(8,128)(2,1)S(1)} %copy-done.3, bf16[8,16,2048]{2,1,0:T(8,128)(2,1)S(1)} %collective-permute-done.13.refs_0_, ...), custom_call_target="tpu_custom_call" | custom-call | bytes 2097152 | tf_op jit(solution)/shard_map/choose_blocks/pallas_call | solution.py:106
  129.3 1.3 collective-permute-start.9
  130.6 8.4 %add_part.7.refs_4_ = f32[512,2048]{1,0:T(8,128)S(1)} custom-call(s32[8]{0:T(128)S(1)} %dynamic-slice_bitcast_fusion.refs_0_.info, bf16[512,2048]{1,0:T(8,128)(2,1)} %collective-permute-done.10.refs_1_, bf16[512,2048]{1,0:T(8,128)(2,1)S(1)} %collective-permute-done.11.refs_2_, bf16[8192,2048]{1,0:T(8,128)(2,1)} %refs_3_.5, ...), custom_call_target="tpu_custom_call", output_to_operand_aliasing={{}: (4, {})} | custom-call | flops 4294967296 | bytes 16777216 | tf_op jit(solution)/shard_map/add_part/pallas_call | solution.py:232
  139.1 5.4 %add_part.8.refs_5_ = bf16[512,2048]{1,0:T(8,128)(2,1)} custom-call(s32[8]{0:T(128)S(1)} %dynamic-slice_bitcast_fusion.refs_0_.info, bf16[384,2048]{1,0:T(8,128)(2,1)S(1)} %collective-permute-done.16.refs_1_, bf16[384,2048]{1,0:T(8,128)(2,1)S(1)} %collective-permute-done.17.refs_2_, bf16[2048,2048]{1,0:T(8,128)(2,1)S(1)} %fetch_part.1.refs_3_, ...), custom_call_target="tpu_custom_call" | custom-call | flops 3221225472 | bytes 14680064 | tf_op jit(solution)/shard_map/add_part/pallas_call | solution.py:232
  144.5 2.1 %collective-permute-done.9.refs_2_ = bf16[128,2048]{1,0:T(8,128)(2,1)S(1)} collective-permute-done((bf16[128,2048]{1,0:T(8,128)(2,1)S(1)}, bf16[128,2048]{1,0:T(8,128)(2,1)S(1)}, u32[]{:S(2)}, u32[]{:S(2)}) %collective-permute-start.9) | collective-permute-done | bytes 524320 | tf_op jit(solution)/shard_map/ppermute | solution.py:323
  146.6 2.9 %add_part.9 = bf16[512,2048]{1,0:T(8,128)(2,1)} custom-call(s32[8]{0:T(128)S(1)} %dynamic-slice_bitcast_fusion.refs_0_.info, bf16[128,2048]{1,0:T(8,128)(2,1)S(1)} %collective-permute-done.8.refs_1_, bf16[128,2048]{1,0:T(8,128)(2,1)S(1)} %collective-permute-done.9.refs_2_, bf16[2048,2048]{1,0:T(8,128)(2,1)S(1)} %fetch_part.1.refs_3_, ...), custom_call_target="tpu_custom_call", output_to_operand_aliasing={{}: (5, {})} | custom-call | flops 1073741824 | bytes 10485760 | tf_op jit(solution)/shard_map/add_part/pallas_call | solution.py:232
  (41 shorter events, 13.2 us)
Async XLA Ops:
  0.0 49.6 %collective-permute-start = (bf16[512,2048]{1,0:T(8,128)(2,1)}, bf16[512,2048]{1,0:T(8,128)(2,1)S(1)}, u32[]{:S(2)}, u32[]{:S(2)}) collective-permute-start(bf16[512,2048]{1,0:T(8,128)(2,1)} %features.1), channel_id=1, source_target_pairs={{0,1},{1,0},{2,3},{3,2},{4,5},{5,4},{6,7},{7,6},{8,9},{9,8},{10,11... | collective-permute-start | bytes 6291464 | tf_op jit(solution)/shard_map/ppermute | solution.py:310
  3.0 47.4 %collective-permute-start.10 = (bf16[512,2048]{1,0:T(8,128)(2,1)}, bf16[512,2048]{1,0:T(8,128)(2,1)}, u32[]{:S(2)}, u32[]{:S(2)}) collective-permute-start(bf16[512,2048]{1,0:T(8,128)(2,1)} %features.1), channel_id=1, source_target_pairs={{1,2},{2,1},{5,6},{6,5},{9,10},{10,9},{13,14},{14,13},{17,18},{18,... | collective-permute-start | bytes 6291464 | tf_op jit(solution)/shard_map/ppermute | solution.py:311
  7.4 3.0 %collective-permute-start.3 = (s32[8]{0:T(128)S(1)}, s32[8]{0:T(128)S(1)}, u32[]{:S(2)}, u32[]{:S(2)}) collective-permute-start(s32[8]{0:T(128)S(1)} %get-tuple-element.41), channel_id=1, source_target_pairs={{0,12},{4,8},{8,4},{12,0},{1,13},{5,9},{9,5},{13,1},{2,14},{6,10},... | collective-permute-start | bytes 104 | tf_op jit(solution)/shard_map/ppermute | solution.py:41
  8.1 3.5 %collective-permute-start.2 = (s32[8]{0:T(128)S(1)}, s32[8]{0:T(128)S(1)}, u32[]{:S(2)}, u32[]{:S(2)}) collective-permute-start(s32[8]{0:T(128)S(1)} %get-tuple-element.42), channel_id=1, source_target_pairs={{0,8},{4,12},{8,0},{12,4},{1,9},{5,13},{9,1},{13,5},{2,10},{6,14},... | collective-permute-start | bytes 104 | tf_op jit(solution)/shard_map/ppermute | solution.py:41
  9.0 2.6 %collective-permute-start.1 = (s32[8]{0:T(128)S(1)}, s32[8]{0:T(128)S(1)}, u32[]{:S(2)}, u32[]{:S(2)}) collective-permute-start(s32[8]{0:T(128)S(1)} %get-tuple-element.43), channel_id=1, source_target_pairs={{0,4},{4,0},{8,12},{12,8},{1,5},{5,1},{9,13},{13,9},{2,6},{6,2},{1... | collective-permute-start | bytes 104 | tf_op jit(solution)/shard_map/ppermute | solution.py:41
  11.6 1.6 %copy-start.1 = (bf16[32,16,2048]{2,1,0:T(8,128)(2,1)S(1)}, bf16[32,16,2048]{2,1,0:T(8,128)(2,1)}, u32[]{:S(2)}) copy-start(bf16[32,16,2048]{2,1,0:T(8,128)(2,1)} %pool.2) | copy-start | bytes 6291460
  15.1 15.3 %collective-permute-start.4 = (bf16[8,16,2048]{2,1,0:T(8,128)(2,1)}, bf16[8,16,2048]{2,1,0:T(8,128)(2,1)S(1)}, u32[]{:S(2)}, u32[]{:S(2)}) collective-permute-start(bf16[8,16,2048]{2,1,0:T(8,128)(2,1)} %get-tuple-element.26), channel_id=1, source_target_pairs={{0,4},{4,0},{8,12},{12,8},{1,5},{5,1},{9,13},{13,9},{2,6},{6,2},{1... | collective-permute-start | bytes 1572872 | tf_op jit(solution)/shard_map/ppermute | solution.py:41
  15.3 15.1 %collective-permute-start.5 = (bf16[8,16,2048]{2,1,0:T(8,128)(2,1)}, bf16[8,16,2048]{2,1,0:T(8,128)(2,1)S(1)}, u32[]{:S(2)}, u32[]{:S(2)}) collective-permute-start(bf16[8,16,2048]{2,1,0:T(8,128)(2,1)} %get-tuple-element.27), channel_id=1, source_target_pairs={{0,8},{4,12},{8,0},{12,4},{1,9},{5,13},{9,1},{13,5},{2,10},{6,14},... | collective-permute-start | bytes 1572872 | tf_op jit(solution)/shard_map/ppermute | solution.py:41
  16.2 24.4 %collective-permute-start.6 = (bf16[8,16,2048]{2,1,0:T(8,128)(2,1)}, bf16[8,16,2048]{2,1,0:T(8,128)(2,1)}, u32[]{:S(2)}, u32[]{:S(2)}) collective-permute-start(bf16[8,16,2048]{2,1,0:T(8,128)(2,1)} %get-tuple-element.28), channel_id=1, source_target_pairs={{0,12},{4,8},{8,4},{12,0},{1,13},{5,9},{9,5},{13,1},{2,14},{6,10},... | collective-permute-start | bytes 1572872 | tf_op jit(solution)/shard_map/ppermute | solution.py:41
  17.7 1.6 %copy-start.4 = (bf16[512,2048]{1,0:T(8,128)(2,1)S(1)}, bf16[512,2048]{1,0:T(8,128)(2,1)}, u32[]{:S(2)}) copy-start(bf16[512,2048]{1,0:T(8,128)(2,1)} %features.1) | copy-start | bytes 6291460
  19.3 8.0 %copy-start.3 = (bf16[32,16,2048]{2,1,0:T(8,128)(2,1)S(1)}, bf16[32,16,2048]{2,1,0:T(8,128)(2,1)}, u32[]{:S(2)}) copy-start(bf16[32,16,2048]{2,1,0:T(8,128)(2,1)} %pool.3) | copy-start | bytes 6291460
  27.3 13.3 %copy-start.2 = (bf16[32,16,2048]{2,1,0:T(8,128)(2,1)S(1)}, bf16[32,16,2048]{2,1,0:T(8,128)(2,1)}, u32[]{:S(2)}) copy-start(bf16[32,16,2048]{2,1,0:T(8,128)(2,1)} %pool.2) | copy-start | bytes 6291460
  44.1 5.5 %collective-permute-start.7 = (f32[16,512]{1,0:T(8,128)S(1)}, f32[16,512]{1,0:T(8,128)S(1)}, u32[]{:S(2)}, u32[]{:S(2)}) collective-permute-start(f32[16,512]{1,0:T(8,128)S(1)} %shrink.1), channel_id=1, source_target_pairs={{0,1},{1,0},{2,3},{3,2},{4,5},{5,4},{6,7},{7,6},{8,9},{9,8},{10,11... | collective-permute-start | bytes 98312 | tf_op jit(solution)/shard_map/ppermute | solution.py:317
  49.7 2.2 %collective-permute-start.16 = (bf16[384,2048]{1,0:T(8,128)(2,1)S(1)}, bf16[384,2048]{1,0:T(8,128)(2,1)S(1)}, u32[]{:S(2)}, u32[]{:S(2)}) collective-permute-start(bf16[384,2048]{1,0:T(8,128)(2,1)S(1)} %slice.22), channel_id=1, source_target_pairs={{1,2},{2,1},{5,6},{6,5},{9,10},{10,9},{13,14},{14,13},{17,18},{18,... | collective-permute-start | bytes 4718600 | tf_op jit(solution)/shard_map/ppermute | solution.py:322
  50.5 80.2 %collective-permute-start.11 = (bf16[512,2048]{1,0:T(8,128)(2,1)}, bf16[512,2048]{1,0:T(8,128)(2,1)S(1)}, u32[]{:S(2)}, u32[]{:S(2)}) collective-permute-start(bf16[512,2048]{1,0:T(8,128)(2,1)} %collective-permute-done.10.refs_1_), channel_id=1, source_target_pairs={{1,0},{2,3},{5,4},{6,7},{9,8},{10,11},{13,12},{14,15},{17,16},{18,... | collective-permute-start | bytes 6291464 | tf_op jit(solution)/shard_map/ppermute | solution.py:321
  51.8 2.0 %collective-permute-start.13 = (bf16[8,16,2048]{2,1,0:T(8,128)(2,1)S(1)}, bf16[8,16,2048]{2,1,0:T(8,128)(2,1)S(1)}, u32[]{:S(2)}, u32[]{:S(2)}) collective-permute-start(bf16[8,16,2048]{2,1,0:T(8,128)(2,1)S(1)} %get-tuple-element.34), channel_id=1, source_target_pairs={{0,4},{4,0},{8,12},{12,8},{1,5},{5,1},{9,13},{13,9},{2,6},{6,2},{1... | collective-permute-start | bytes 1572872 | tf_op jit(solution)/shard_map/ppermute | solution.py:41
  51.9 87.2 %collective-permute-start.17 = (bf16[384,2048]{1,0:T(8,128)(2,1)S(1)}, bf16[384,2048]{1,0:T(8,128)(2,1)S(1)}, u32[]{:S(2)}, u32[]{:S(2)}) collective-permute-start(bf16[384,2048]{1,0:T(8,128)(2,1)S(1)} %collective-permute-done.16.refs_1_), channel_id=1, source_target_pairs={{1,0},{2,3},{5,4},{6,7},{9,8},{10,11},{13,12},{14,15},{17,16},{18,... | collective-permute-start | bytes 4718600 | tf_op jit(solution)/shard_map/ppermute | solution.py:323
  53.7 14.0 %collective-permute-start.14 = (bf16[8,16,2048]{2,1,0:T(8,128)(2,1)S(1)}, bf16[8,16,2048]{2,1,0:T(8,128)(2,1)S(1)}, u32[]{:S(2)}, u32[]{:S(2)}) collective-permute-start(bf16[8,16,2048]{2,1,0:T(8,128)(2,1)S(1)} %get-tuple-element.36), channel_id=1, source_target_pairs={{0,8},{4,12},{8,0},{12,4},{1,9},{5,13},{9,1},{13,5},{2,10},{6,14},... | collective-permute-start | bytes 1572872 | tf_op jit(solution)/shard_map/ppermute | solution.py:41
  67.7 58.7 %collective-permute-start.15 = (bf16[8,16,2048]{2,1,0:T(8,128)(2,1)S(1)}, bf16[8,16,2048]{2,1,0:T(8,128)(2,1)S(1)}, u32[]{:S(2)}, u32[]{:S(2)}) collective-permute-start(bf16[8,16,2048]{2,1,0:T(8,128)(2,1)S(1)} %get-tuple-element.38), channel_id=1, source_target_pairs={{0,12},{4,8},{8,4},{12,0},{1,13},{5,9},{9,5},{13,1},{2,14},{6,10},... | collective-permute-start | bytes 1572872 | tf_op jit(solution)/shard_map/ppermute | solution.py:41
  68.3 61.0 %collective-permute-start.8 = (bf16[128,2048]{1,0:T(8,128)(2,1)S(1)}, bf16[128,2048]{1,0:T(8,128)(2,1)S(1)}, u32[]{:S(2)}, u32[]{:S(2)}) collective-permute-start(bf16[128,2048]{1,0:T(8,128)(2,1)S(1)} %slice.21), channel_id=1, source_target_pairs={{1,2},{2,1},{5,6},{6,5},{9,10},{10,9},{13,14},{14,13},{17,18},{18,... | collective-permute-start | bytes 1572872 | tf_op jit(solution)/shard_map/ppermute | solution.py:322
  69.0 61.6 %collective-permute-start.12 = (f32[16,512]{1,0:T(8,128)S(1)}, f32[16,512]{1,0:T(8,128)S(1)}, u32[]{:S(2)}, u32[]{:S(2)}) collective-permute-start(f32[16,512]{1,0:T(8,128)S(1)} %add.16.refs_5_), channel_id=1, source_target_pairs={{0,2},{1,3},{2,0},{3,1},{4,6},{5,7},{6,4},{7,5},{8,10},{9,11},{10,... | collective-permute-start | bytes 98312 | tf_op jit(solution)/shard_map/ppermute | solution.py:318
  114.8 10.5 %copy-start = (bf16[8192,2048]{1,0:T(8,128)(2,1)S(1)}, bf16[8192,2048]{1,0:T(8,128)(2,1)}, u32[]{:S(2)}) copy-start(bf16[8192,2048]{1,0:T(8,128)(2,1)} %refs_3_.5) | copy-start | bytes 100663296
  129.3 17.3 %collective-permute-start.9 = (bf16[128,2048]{1,0:T(8,128)(2,1)S(1)}, bf16[128,2048]{1,0:T(8,128)(2,1)S(1)}, u32[]{:S(2)}, u32[]{:S(2)}) collective-permute-start(bf16[128,2048]{1,0:T(8,128)(2,1)S(1)} %collective-permute-done.8.refs_1_), channel_id=1, source_target_pairs={{1,0},{2,3},{5,4},{6,7},{9,8},{10,11},{13,12},{14,15},{17,16},{18,... | collective-permute-start | bytes 1572872 | tf_op jit(solution)/shard_map/ppermute | solution.py:323

commit v6 on v5

--- a/solution.py
+++ b/solution.py
@@ -320,11 +320,10 @@
     halves = held[:cut], held[cut:]
     passed = lax.ppermute(after(across, *shares[:1]), "tp", outward)
     inner = [lax.ppermute(p, "tp", middle) for p in halves]
-    last = [lax.ppermute(p, "tp", outward) for p in inner]
-
     ups = in_turn([after(packed[0], *shares[:1]), *packed[1:]], rep)
     acc = add_part(after(info, *shares[:1]), 2, [[near]], query_weight, acc)
     base = acc
+    last = [lax.ppermute(p, "tp", outward) for p in (after(inner[0], acc), inner[1])]
     up = chosen_blocks(after(source, acc), place, adapter_up, ups)
     acc = add_part(info, 4, [[across], [passed]], query_weight, acc, shares, up, blocks)
     weight = fetch_part(after(info, base), 7, query_weight, features.shape[1])

time: 150 us -> 150 us (level)
  starting transfers between devices: 56.7 us -> 49 us
  waiting for transfers between devices: 30.6 us -> 38.2 us
    ppermute x1, starting transfers between devices: 37.7 us -> 29.6 us  [on_line_of_four(): shares = [pair, lax.ppermute(pair, 'tp', [(i, i ^ 2) for i in range(4)])]]
    ppermute x2, waiting for transfers between devices: 2.12 us -> 10.1 us  [on_line_of_four(): lax.ppermute(p, 'tp', outward)]
where the time goes in v6:
time: 150 us
  starting transfers between devices  49 us (33%)
  Pallas kernels  45.2 us (30%)
  waiting for transfers between devices  38.2 us (25%)
  local copies, waits for them, and re-layouts  14.6 us (10%)
  other arithmetic  2.34 us (2%)
    pallas_call x5, Pallas kernels, add_part(): pl.pallas_call(functools.partial(add_kernel, tail), out_shape=jax.ShapeDt...  32.8 us
    ppermute x1, starting transfers between devices, on_line_of_four(): shares = [pair, lax.ppermute(pair, 'tp', [(i, i ^ 2) for i in range(4)])]  29.6 us
    ppermute x9, waiting for transfers between devices, swap(): return lax.ppermute(x, 'rep', [(r, r ^ distance) for r in range(rep)])  25.2 us
    unnamed x10, local copies, waits for them, and re-layouts  13.7 us
    ppermute x2, waiting for transfers between devices, on_line_of_four(): lax.ppermute(p, 'tp', outward)  10.1 us
    ppermute x9, starting transfers between devices, swap(): return lax.ppermute(x, 'rep', [(r, r ^ distance) for r in range(rep)])  6.58 us
    pallas_call x2, Pallas kernels, pack(): pl.pallas_call(functools.partial(pack_kernel, count, cap), out_shape=[sha...  4.9 us
    pallas_call x1, Pallas kernels, shrink(): pl.pallas_call(shrink_kernel, out_shape=jax.ShapeDtypeStruct((rank, rows)...  3.54 us
  transfers between devices with their start and end apart: 18, of which 7 were waited for; matrix products, arithmetic and copies ran while one was open for 2% of the time, Pallas kernels for 28%

profile of v6, /device:TPU:0, one launch (start us, length us, event | category | flops | bytes accessed | tf_op | source)
XLA Modules:
  0.0 149.6 jit_solution(1222961239220193994)
XLA Ops:
  0.0 3.0 %collective-permute-start = (bf16[512,2048]{1,0:T(8,128)(2,1)}, bf16[512,2048]{1,0:T(8,128)(2,1)S(1)}, u32[]{:S(2)}, u32[]{:S(2)}) collective-permute-start(bf16[512,2048]{1,0:T(8,128)(2,1)} %features.1), channel_id=1, source_target_pairs={{0,1},{1,0},{2,3},{3,2},{4,5},{5,4},{6,7},{7,6},{8,9},{9,8},{10,11... | collective-permute-start | bytes 6291464 | tf_op jit(solution)/shard_map/ppermute | solution.py:310
  3.0 2.0 %collective-permute-start.10 = (bf16[512,2048]{1,0:T(8,128)(2,1)}, bf16[512,2048]{1,0:T(8,128)(2,1)}, u32[]{:S(2)}, u32[]{:S(2)}) collective-permute-start(bf16[512,2048]{1,0:T(8,128)(2,1)} %features.1), channel_id=1, source_target_pairs={{1,2},{2,1},{5,6},{6,5},{9,10},{10,9},{13,14},{14,13},{17,18},{18,... | collective-permute-start | bytes 6291464 | tf_op jit(solution)/shard_map/ppermute | solution.py:311
  11.6 1.6 %copy-done.1 = bf16[32,16,2048]{2,1,0:T(8,128)(2,1)S(1)} copy-done((bf16[32,16,2048]{2,1,0:T(8,128)(2,1)S(1)}, bf16[32,16,2048]{2,1,0:T(8,128)(2,1)}, u32[]{:S(2)}) %copy-start.1) | copy-done | bytes 2097176
  13.2 1.9 %pack_blocks.3 = (bf16[8,16,2048]{2,1,0:T(8,128)(2,1)}, bf16[8,16,2048]{2,1,0:T(8,128)(2,1)}, bf16[8,16,2048]{2,1,0:T(8,128)(2,1)}) custom-call(s32[8]{0:T(128)S(1)} %collective-permute-done.1.refs_0_, s32[8]{0:T(128)S(1)} %collective-permute-done.2.refs_1_, s32[8]{0:T(128)S(1)} %collective-permute-done.3.refs_2_, bf16[32,16,2048]{2,1,0:T(8,128)(2,1)S(1)} %copy-done.1), custom_call_target="tpu_custom_call" | custom-call | bytes 3145728 | tf_op jit(solution)/shard_map/pack_blocks/pallas_call | solution.py:71
  17.7 1.6 %copy-done.4 = bf16[512,2048]{1,0:T(8,128)(2,1)S(1)} copy-done((bf16[512,2048]{1,0:T(8,128)(2,1)S(1)}, bf16[512,2048]{1,0:T(8,128)(2,1)}, u32[]{:S(2)}) %copy-start.4) | copy-done | bytes 2097176
  19.3 8.0 %add_part.5.refs_3_ = f32[512,2048]{1,0:T(8,128)S(1)} custom-call(s32[8]{0:T(128)S(1)} %dynamic-slice_bitcast_fusion.refs_0_.info, bf16[512,2048]{1,0:T(8,128)(2,1)S(1)} %copy-done.4, bf16[8192,2048]{1,0:T(8,128)(2,1)} %refs_3_.5), custom_call_target="tpu_custom_call" | custom-call | flops 4294967296 | bytes 16777216 | tf_op jit(solution)/shard_map/add_part/pallas_call | solution.py:232
  27.3 3.0 %pack_blocks.2 = (bf16[8,16,2048]{2,1,0:T(8,128)(2,1)S(1)}, bf16[8,16,2048]{2,1,0:T(8,128)(2,1)S(1)}, bf16[8,16,2048]{2,1,0:T(8,128)(2,1)S(1)}) custom-call(s32[8]{0:T(128)S(1)} %collective-permute-done.1.refs_0_, s32[8]{0:T(128)S(1)} %collective-permute-done.2.refs_1_, s32[8]{0:T(128)S(1)} %collective-permute-done.3.refs_2_, bf16[32,16,2048]{2,1,0:T(8,128)(2,1)S(1)} %copy-done.3), custom_call_target="tpu_custom_call" | custom-call | bytes 3145728 | tf_op jit(solution)/shard_map/pack_blocks/pallas_call | solution.py:71
  30.4 10.2 %collective-permute-done.6.refs_2_ = bf16[8,16,2048]{2,1,0:T(8,128)(2,1)} collective-permute-done((bf16[8,16,2048]{2,1,0:T(8,128)(2,1)}, bf16[8,16,2048]{2,1,0:T(8,128)(2,1)}, u32[]{:S(2)}, u32[]{:S(2)}) %collective-permute-start.6) | collective-permute-done | bytes 524320 | tf_op jit(solution)/shard_map/ppermute | solution.py:41
  40.6 3.5 %shrink.1 = f32[16,512]{1,0:T(8,128)S(1)} custom-call(s32[16]{0:T(128)S(1)} %get-tuple-element.34.source, s32[16]{0:T(128)S(1)} %get-tuple-element.41.place, bf16[512,2048]{1,0:T(8,128)(2,1)S(1)} %copy-done.4, bf16[32,16,2048]{2,1,0:T(8,128)(2,1)S(1)} %copy-done.2, bf16[8,16,2048]{2,1,0:T(8,128)(2,1)S(1)} %collective-permute-done.4.refs_0_, ...), custom_call_target="tpu_custom_call" | custom-call | flops 536870912 | bytes 2097152 | tf_op jit(solution)/shard_map/shrink/pallas_call | solution.py:133
  44.2 2.5 %collective-permute-start.7 = (f32[16,512]{1,0:T(8,128)S(1)}, f32[16,512]{1,0:T(8,128)S(1)}, u32[]{:S(2)}, u32[]{:S(2)}) collective-permute-start(f32[16,512]{1,0:T(8,128)S(1)} %shrink.1), channel_id=1, source_target_pairs={{0,1},{1,0},{2,3},{3,2},{4,5},{5,4},{6,7},{7,6},{8,9},{9,8},{10,11... | collective-permute-start | bytes 98312 | tf_op jit(solution)/shard_map/ppermute | solution.py:317
  46.6 2.9 %collective-permute-done.7 = f32[16,512]{1,0:T(8,128)S(1)} collective-permute-done((f32[16,512]{1,0:T(8,128)S(1)}, f32[16,512]{1,0:T(8,128)S(1)}, u32[]{:S(2)}, u32[]{:S(2)}) %collective-permute-start.7) | collective-permute-done | bytes 32800 | tf_op jit(solution)/shard_map/ppermute | solution.py:317
  50.5 1.3 collective-permute-start.11
  51.8 8.0 %add_part.6.refs_4_ = f32[512,2048]{1,0:T(8,128)S(1)} custom-call(s32[8]{0:T(128)S(1)} %dynamic-slice_bitcast_fusion.refs_0_.info, bf16[512,2048]{1,0:T(8,128)(2,1)S(1)} %collective-permute-done.refs_1_, bf16[8192,2048]{1,0:T(8,128)(2,1)} %refs_3_.5, f32[512,2048]{1,0:T(8,128)S(1)} %add_part.5.refs_3_), custom_call_target="tpu_custom_call", output_to_operand_aliasing={{}: (3, {})} | custom-call | flops 4294967296 | bytes 16777216 | tf_op jit(solution)/shard_map/add_part/pallas_call | solution.py:232
  59.9 1.3 collective-permute-start.17
  61.2 1.7 %collective-permute-start.14 = (bf16[8,16,2048]{2,1,0:T(8,128)(2,1)S(1)}, bf16[8,16,2048]{2,1,0:T(8,128)(2,1)S(1)}, u32[]{:S(2)}, u32[]{:S(2)}) collective-permute-start(bf16[8,16,2048]{2,1,0:T(8,128)(2,1)S(1)} %get-tuple-element.37), channel_id=1, source_target_pairs={{0,8},{4,12},{8,0},{12,4},{1,9},{5,13},{9,1},{13,5},{2,10},{6,14},... | collective-permute-start | bytes 1572872 | tf_op jit(solution)/shard_map/ppermute | solution.py:41
  62.9 12.7 %collective-permute-done.14.refs_1_ = bf16[8,16,2048]{2,1,0:T(8,128)(2,1)S(1)} collective-permute-done((bf16[8,16,2048]{2,1,0:T(8,128)(2,1)S(1)}, bf16[8,16,2048]{2,1,0:T(8,128)(2,1)S(1)}, u32[]{:S(2)}, u32[]{:S(2)}) %collective-permute-start.14) | collective-permute-done | bytes 524320 | tf_op jit(solution)/shard_map/ppermute | solution.py:41
  77.3 29.6 %collective-permute-start.12 = (f32[16,512]{1,0:T(8,128)S(1)}, f32[16,512]{1,0:T(8,128)S(1)}, u32[]{:S(2)}, u32[]{:S(2)}) collective-permute-start(f32[16,512]{1,0:T(8,128)S(1)} %add.16.refs_5_), channel_id=1, source_target_pairs={{0,2},{1,3},{2,0},{3,1},{4,6},{5,7},{6,4},{7,5},{8,10},{9,11},{10,... | collective-permute-start | bytes 98312 | tf_op jit(solution)/shard_map/ppermute | solution.py:318
  106.8 10.5 %copy-done = bf16[8192,2048]{1,0:T(8,128)(2,1)S(1)} copy-done((bf16[8192,2048]{1,0:T(8,128)(2,1)S(1)}, bf16[8192,2048]{1,0:T(8,128)(2,1)}, u32[]{:S(2)}) %copy-start) | copy-done | bytes 33554456
  118.5 2.8 %choose_blocks.1.refs_7_ = bf16[256,2048]{1,0:T(8,128)(2,1)S(1)} custom-call(s32[16]{0:T(128)S(1)} %get-tuple-element.34.source, s32[16]{0:T(128)S(1)} %get-tuple-element.41.place, bf16[32,16,2048]{2,1,0:T(8,128)(2,1)S(1)} %copy-done.3, bf16[8,16,2048]{2,1,0:T(8,128)(2,1)S(1)} %collective-permute-done.13.refs_0_, ...), custom_call_target="tpu_custom_call" | custom-call | bytes 2097152 | tf_op jit(solution)/shard_map/choose_blocks/pallas_call | solution.py:106
  122.7 8.4 %add_part.7.refs_4_ = f32[512,2048]{1,0:T(8,128)S(1)} custom-call(s32[8]{0:T(128)S(1)} %dynamic-slice_bitcast_fusion.refs_0_.info, bf16[512,2048]{1,0:T(8,128)(2,1)} %collective-permute-done.10.refs_1_, bf16[512,2048]{1,0:T(8,128)(2,1)S(1)} %collective-permute-done.11.refs_2_, bf16[8192,2048]{1,0:T(8,128)(2,1)} %refs_3_.5, ...), custom_call_target="tpu_custom_call", output_to_operand_aliasing={{}: (4, {})} | custom-call | flops 4294967296 | bytes 16777216 | tf_op jit(solution)/shard_map/add_part/pallas_call | solution.py:232
  131.1 6.2 %collective-permute-done.17.refs_2_ = bf16[384,2048]{1,0:T(8,128)(2,1)S(1)} collective-permute-done((bf16[384,2048]{1,0:T(8,128)(2,1)S(1)}, bf16[384,2048]{1,0:T(8,128)(2,1)S(1)}, u32[]{:S(2)}, u32[]{:S(2)}) %collective-permute-start.17) | collective-permute-done | bytes 1572896 | tf_op jit(solution)/shard_map/ppermute | solution.py:326
  137.4 5.4 %add_part.8.refs_5_ = bf16[512,2048]{1,0:T(8,128)(2,1)} custom-call(s32[8]{0:T(128)S(1)} %dynamic-slice_bitcast_fusion.refs_0_.info, bf16[384,2048]{1,0:T(8,128)(2,1)S(1)} %collective-permute-done.16.refs_1_, bf16[384,2048]{1,0:T(8,128)(2,1)S(1)} %collective-permute-done.17.refs_2_, bf16[2048,2048]{1,0:T(8,128)(2,1)S(1)} %fetch_part.1.refs_3_, ...), custom_call_target="tpu_custom_call" | custom-call | flops 3221225472 | bytes 14680064 | tf_op jit(solution)/shard_map/add_part/pallas_call | solution.py:232
  142.8 3.8 %collective-permute-done.9.refs_2_ = bf16[128,2048]{1,0:T(8,128)(2,1)S(1)} collective-permute-done((bf16[128,2048]{1,0:T(8,128)(2,1)S(1)}, bf16[128,2048]{1,0:T(8,128)(2,1)S(1)}, u32[]{:S(2)}, u32[]{:S(2)}) %collective-permute-start.9) | collective-permute-done | bytes 524320 | tf_op jit(solution)/shard_map/ppermute | solution.py:326
  146.6 2.9 %add_part.9 = bf16[512,2048]{1,0:T(8,128)(2,1)} custom-call(s32[8]{0:T(128)S(1)} %dynamic-slice_bitcast_fusion.refs_0_.info, bf16[128,2048]{1,0:T(8,128)(2,1)S(1)} %collective-permute-done.8.refs_1_, bf16[128,2048]{1,0:T(8,128)(2,1)S(1)} %collective-permute-done.9.refs_2_, bf16[2048,2048]{1,0:T(8,128)(2,1)S(1)} %fetch_part.1.refs_3_, ...), custom_call_target="tpu_custom_call", output_to_operand_aliasing={{}: (5, {})} | custom-call | flops 1073741824 | bytes 10485760 | tf_op jit(solution)/shard_map/add_part/pallas_call | solution.py:232
  (41 shorter events, 14.3 us)
Async XLA Ops:
  0.0 49.6 %collective-permute-start = (bf16[512,2048]{1,0:T(8,128)(2,1)}, bf16[512,2048]{1,0:T(8,128)(2,1)S(1)}, u32[]{:S(2)}, u32[]{:S(2)}) collective-permute-start(bf16[512,2048]{1,0:T(8,128)(2,1)} %features.1), channel_id=1, source_target_pairs={{0,1},{1,0},{2,3},{3,2},{4,5},{5,4},{6,7},{7,6},{8,9},{9,8},{10,11... | collective-permute-start | bytes 6291464 | tf_op jit(solution)/shard_map/ppermute | solution.py:310
  3.0 47.4 %collective-permute-start.10 = (bf16[512,2048]{1,0:T(8,128)(2,1)}, bf16[512,2048]{1,0:T(8,128)(2,1)}, u32[]{:S(2)}, u32[]{:S(2)}) collective-permute-start(bf16[512,2048]{1,0:T(8,128)(2,1)} %features.1), channel_id=1, source_target_pairs={{1,2},{2,1},{5,6},{6,5},{9,10},{10,9},{13,14},{14,13},{17,18},{18,... | collective-permute-start | bytes 6291464 | tf_op jit(solution)/shard_map/ppermute | solution.py:311
  7.4 3.0 %collective-permute-start.3 = (s32[8]{0:T(128)S(1)}, s32[8]{0:T(128)S(1)}, u32[]{:S(2)}, u32[]{:S(2)}) collective-permute-start(s32[8]{0:T(128)S(1)} %get-tuple-element.43), channel_id=1, source_target_pairs={{0,12},{4,8},{8,4},{12,0},{1,13},{5,9},{9,5},{13,1},{2,14},{6,10},... | collective-permute-start | bytes 104 | tf_op jit(solution)/shard_map/ppermute | solution.py:41
  8.1 3.5 %collective-permute-start.2 = (s32[8]{0:T(128)S(1)}, s32[8]{0:T(128)S(1)}, u32[]{:S(2)}, u32[]{:S(2)}) collective-permute-start(s32[8]{0:T(128)S(1)} %get-tuple-element.44), channel_id=1, source_target_pairs={{0,8},{4,12},{8,0},{12,4},{1,9},{5,13},{9,1},{13,5},{2,10},{6,14},... | collective-permute-start | bytes 104 | tf_op jit(solution)/shard_map/ppermute | solution.py:41
  9.0 2.6 %collective-permute-start.1 = (s32[8]{0:T(128)S(1)}, s32[8]{0:T(128)S(1)}, u32[]{:S(2)}, u32[]{:S(2)}) collective-permute-start(s32[8]{0:T(128)S(1)} %get-tuple-element.45), channel_id=1, source_target_pairs={{0,4},{4,0},{8,12},{12,8},{1,5},{5,1},{9,13},{13,9},{2,6},{6,2},{1... | collective-permute-start | bytes 104 | tf_op jit(solution)/shard_map/ppermute | solution.py:41
  11.6 1.6 %copy-start.1 = (bf16[32,16,2048]{2,1,0:T(8,128)(2,1)S(1)}, bf16[32,16,2048]{2,1,0:T(8,128)(2,1)}, u32[]{:S(2)}) copy-start(bf16[32,16,2048]{2,1,0:T(8,128)(2,1)} %pool.2) | copy-start | bytes 6291460
  15.1 15.3 %collective-permute-start.4 = (bf16[8,16,2048]{2,1,0:T(8,128)(2,1)}, bf16[8,16,2048]{2,1,0:T(8,128)(2,1)S(1)}, u32[]{:S(2)}, u32[]{:S(2)}) collective-permute-start(bf16[8,16,2048]{2,1,0:T(8,128)(2,1)} %get-tuple-element.27), channel_id=1, source_target_pairs={{0,4},{4,0},{8,12},{12,8},{1,5},{5,1},{9,13},{13,9},{2,6},{6,2},{1... | collective-permute-start | bytes 1572872 | tf_op jit(solution)/shard_map/ppermute | solution.py:41
  15.3 15.1 %collective-permute-start.5 = (bf16[8,16,2048]{2,1,0:T(8,128)(2,1)}, bf16[8,16,2048]{2,1,0:T(8,128)(2,1)S(1)}, u32[]{:S(2)}, u32[]{:S(2)}) collective-permute-start(bf16[8,16,2048]{2,1,0:T(8,128)(2,1)} %get-tuple-element.28), channel_id=1, source_target_pairs={{0,8},{4,12},{8,0},{12,4},{1,9},{5,13},{9,1},{13,5},{2,10},{6,14},... | collective-permute-start | bytes 1572872 | tf_op jit(solution)/shard_map/ppermute | solution.py:41
  16.2 24.4 %collective-permute-start.6 = (bf16[8,16,2048]{2,1,0:T(8,128)(2,1)}, bf16[8,16,2048]{2,1,0:T(8,128)(2,1)}, u32[]{:S(2)}, u32[]{:S(2)}) collective-permute-start(bf16[8,16,2048]{2,1,0:T(8,128)(2,1)} %get-tuple-element.29), channel_id=1, source_target_pairs={{0,12},{4,8},{8,4},{12,0},{1,13},{5,9},{9,5},{13,1},{2,14},{6,10},... | collective-permute-start | bytes 1572872 | tf_op jit(solution)/shard_map/ppermute | solution.py:41
  17.7 1.6 %copy-start.4 = (bf16[512,2048]{1,0:T(8,128)(2,1)S(1)}, bf16[512,2048]{1,0:T(8,128)(2,1)}, u32[]{:S(2)}) copy-start(bf16[512,2048]{1,0:T(8,128)(2,1)} %features.1) | copy-start | bytes 6291460
  19.3 8.0 %copy-start.3 = (bf16[32,16,2048]{2,1,0:T(8,128)(2,1)S(1)}, bf16[32,16,2048]{2,1,0:T(8,128)(2,1)}, u32[]{:S(2)}) copy-start(bf16[32,16,2048]{2,1,0:T(8,128)(2,1)} %pool.3) | copy-start | bytes 6291460
  27.3 13.3 %copy-start.2 = (bf16[32,16,2048]{2,1,0:T(8,128)(2,1)S(1)}, bf16[32,16,2048]{2,1,0:T(8,128)(2,1)}, u32[]{:S(2)}) copy-start(bf16[32,16,2048]{2,1,0:T(8,128)(2,1)} %pool.2) | copy-start | bytes 6291460
  44.2 5.4 %collective-permute-start.7 = (f32[16,512]{1,0:T(8,128)S(1)}, f32[16,512]{1,0:T(8,128)S(1)}, u32[]{:S(2)}, u32[]{:S(2)}) collective-permute-start(f32[16,512]{1,0:T(8,128)S(1)} %shrink.1), channel_id=1, source_target_pairs={{0,1},{1,0},{2,3},{3,2},{4,5},{5,4},{6,7},{7,6},{8,9},{9,8},{10,11... | collective-permute-start | bytes 98312 | tf_op jit(solution)/shard_map/ppermute | solution.py:317
  49.7 10.2 %collective-permute-start.16 = (bf16[384,2048]{1,0:T(8,128)(2,1)S(1)}, bf16[384,2048]{1,0:T(8,128)(2,1)S(1)}, u32[]{:S(2)}, u32[]{:S(2)}) collective-permute-start(bf16[384,2048]{1,0:T(8,128)(2,1)S(1)} %slice.22), channel_id=1, source_target_pairs={{1,2},{2,1},{5,6},{6,5},{9,10},{10,9},{13,14},{14,13},{17,18},{18,... | collective-permute-start | bytes 4718600 | tf_op jit(solution)/shard_map/ppermute | solution.py:322
  50.5 72.2 %collective-permute-start.11 = (bf16[512,2048]{1,0:T(8,128)(2,1)}, bf16[512,2048]{1,0:T(8,128)(2,1)S(1)}, u32[]{:S(2)}, u32[]{:S(2)}) collective-permute-start(bf16[512,2048]{1,0:T(8,128)(2,1)} %collective-permute-done.10.refs_1_), channel_id=1, source_target_pairs={{1,0},{2,3},{5,4},{6,7},{9,8},{10,11},{13,12},{14,15},{17,16},{18,... | collective-permute-start | bytes 6291464 | tf_op jit(solution)/shard_map/ppermute | solution.py:321
  51.8 9.4 %collective-permute-start.13 = (bf16[8,16,2048]{2,1,0:T(8,128)(2,1)S(1)}, bf16[8,16,2048]{2,1,0:T(8,128)(2,1)S(1)}, u32[]{:S(2)}, u32[]{:S(2)}) collective-permute-start(bf16[8,16,2048]{2,1,0:T(8,128)(2,1)S(1)} %get-tuple-element.35), channel_id=1, source_target_pairs={{0,4},{4,0},{8,12},{12,8},{1,5},{5,1},{9,13},{13,9},{2,6},{6,2},{1... | collective-permute-start | bytes 1572872 | tf_op jit(solution)/shard_map/ppermute | solution.py:41
  59.9 77.5 %collective-permute-start.17 = (bf16[384,2048]{1,0:T(8,128)(2,1)S(1)}, bf16[384,2048]{1,0:T(8,128)(2,1)S(1)}, u32[]{:S(2)}, u32[]{:S(2)}) collective-permute-start(bf16[384,2048]{1,0:T(8,128)(2,1)S(1)} %collective-permute-done.16.refs_1_), channel_id=1, source_target_pairs={{1,0},{2,3},{5,4},{6,7},{9,8},{10,11},{13,12},{14,15},{17,16},{18,... | collective-permute-start | bytes 4718600 | tf_op jit(solution)/shard_map/ppermute | solution.py:326
  61.2 14.4 %collective-permute-start.14 = (bf16[8,16,2048]{2,1,0:T(8,128)(2,1)S(1)}, bf16[8,16,2048]{2,1,0:T(8,128)(2,1)S(1)}, u32[]{:S(2)}, u32[]{:S(2)}) collective-permute-start(bf16[8,16,2048]{2,1,0:T(8,128)(2,1)S(1)} %get-tuple-element.37), channel_id=1, source_target_pairs={{0,8},{4,12},{8,0},{12,4},{1,9},{5,13},{9,1},{13,5},{2,10},{6,14},... | collective-permute-start | bytes 1572872 | tf_op jit(solution)/shard_map/ppermute | solution.py:41
  75.6 43.0 %collective-permute-start.15 = (bf16[8,16,2048]{2,1,0:T(8,128)(2,1)S(1)}, bf16[8,16,2048]{2,1,0:T(8,128)(2,1)S(1)}, u32[]{:S(2)}, u32[]{:S(2)}) collective-permute-start(bf16[8,16,2048]{2,1,0:T(8,128)(2,1)S(1)} %get-tuple-element.39), channel_id=1, source_target_pairs={{0,12},{4,8},{8,4},{12,0},{1,13},{5,9},{9,5},{13,1},{2,14},{6,10},... | collective-permute-start | bytes 1572872 | tf_op jit(solution)/shard_map/ppermute | solution.py:41
  76.6 44.8 %collective-permute-start.8 = (bf16[128,2048]{1,0:T(8,128)(2,1)S(1)}, bf16[128,2048]{1,0:T(8,128)(2,1)S(1)}, u32[]{:S(2)}, u32[]{:S(2)}) collective-permute-start(bf16[128,2048]{1,0:T(8,128)(2,1)S(1)} %slice.21), channel_id=1, source_target_pairs={{1,2},{2,1},{5,6},{6,5},{9,10},{10,9},{13,14},{14,13},{17,18},{18,... | collective-permute-start | bytes 1572872 | tf_op jit(solution)/shard_map/ppermute | solution.py:322
  77.3 45.4 %collective-permute-start.12 = (f32[16,512]{1,0:T(8,128)S(1)}, f32[16,512]{1,0:T(8,128)S(1)}, u32[]{:S(2)}, u32[]{:S(2)}) collective-permute-start(f32[16,512]{1,0:T(8,128)S(1)} %add.16.refs_5_), channel_id=1, source_target_pairs={{0,2},{1,3},{2,0},{3,1},{4,6},{5,7},{6,4},{7,5},{8,10},{9,11},{10,... | collective-permute-start | bytes 98312 | tf_op jit(solution)/shard_map/ppermute | solution.py:318
  106.8 10.5 %copy-start = (bf16[8192,2048]{1,0:T(8,128)(2,1)S(1)}, bf16[8192,2048]{1,0:T(8,128)(2,1)}, u32[]{:S(2)}) copy-start(bf16[8192,2048]{1,0:T(8,128)(2,1)} %refs_3_.5) | copy-start | bytes 100663296
  121.4 25.3 %collective-permute-start.9 = (bf16[128,2048]{1,0:T(8,128)(2,1)S(1)}, bf16[128,2048]{1,0:T(8,128)(2,1)S(1)}, u32[]{:S(2)}, u32[]{:S(2)}) collective-permute-start(bf16[128,2048]{1,0:T(8,128)(2,1)S(1)} %collective-permute-done.8.refs_1_), channel_id=1, source_target_pairs={{1,0},{2,3},{5,4},{6,7},{9,8},{10,11},{13,12},{14,15},{17,16},{18,... | collective-permute-start | bytes 1572872 | tf_op jit(solution)/shard_map/ppermute | solution.py:326

commit v7 on v6

--- a/solution.py
+++ b/solution.py
@@ -322,13 +322,12 @@
     inner = [lax.ppermute(p, "tp", middle) for p in halves]
     ups = in_turn([after(packed[0], *shares[:1]), *packed[1:]], rep)
     acc = add_part(after(info, *shares[:1]), 2, [[near]], query_weight, acc)
-    base = acc
-    last = [lax.ppermute(p, "tp", outward) for p in (after(inner[0], acc), inner[1])]
+    weight = fetch_part(after(info, acc), 7, query_weight, features.shape[1])
+    last = [lax.ppermute(p, "tp", outward) for p in (after(inner[0], weight), inner[1])]
     up = chosen_blocks(after(source, acc), place, adapter_up, ups)
     acc = add_part(info, 4, [[across], [passed]], query_weight, acc, shares, up, blocks)
-    weight = fetch_part(after(info, base), 7, query_weight, features.shape[1])
-    out = add_part(info, 6, [inner[:1], last[:1]], weight, acc, final=(0, None), tile=1024)
-    return add_part(info, 6, [inner[1:], last[1:]], weight, acc, final=(cut, out), tile=1024)
+    out = add_part(info, 6, [inner[:1], last[:1]], weight, acc, final=(0, None), tile=2048)
+    return add_part(info, 6, [inner[1:], last[1:]], weight, acc, final=(cut, out), tile=2048)
 
 
 def anywhere(features, query_weight, adapter_down, adapter_up, block_owner, block_slot, rep):

time: 150 us -> 150 us (level)
  starting transfers between devices: 49 us -> 37.6 us
  waiting for transfers between devices: 38.2 us -> 49.6 us
    ppermute x1, starting transfers between devices: 29.6 us -> 18.2 us  [on_line_of_four(): shares = [pair, lax.ppermute(pair, 'tp', [(i, i ^ 2) for i in range(4)])]]
    ppermute x1, waiting for transfers between devices: 0.01 us -> 9.84 us  [on_line_of_four(): shares = [pair, lax.ppermute(pair, 'tp', [(i, i ^ 2) for i in range(4)])]]
    ppermute x2, waiting for transfers between devices: 10.1 us -> 11.8 us  [on_line_of_four(): lax.ppermute(p, 'tp', outward)]
  transfers between devices with their start and end apart: 18 -> 18, of which waited for: 7 -> 8; matrix products, arithmetic and copies ran while one was open for 2% -> 2% of each run, Pallas kernels for 28% -> 28%
where the time goes in v7:
time: 150 us; the launch traced here: 149 us
  waiting for transfers between devices  49.6 us (33%)
  Pallas kernels  44.9 us (30%)
  starting transfers between devices  37.6 us (25%)
  local copies, waits for them, and re-layouts  14.6 us (10%)
  other arithmetic  2.34 us (2%)
    pallas_call x5, Pallas kernels, add_part(): pl.pallas_call(functools.partial(add_kernel, tail), out_shape=jax.ShapeDt...  32.4 us
    ppermute x9, waiting for transfers between devices, swap(): return lax.ppermute(x, 'rep', [(r, r ^ distance) for r in range(rep)])  25.2 us
    ppermute x1, starting transfers between devices, on_line_of_four(): shares = [pair, lax.ppermute(pair, 'tp', [(i, i ^ 2) for i in range(4)])]  18.2 us
    unnamed x10, local copies, waits for them, and re-layouts  13.7 us
    ppermute x2, waiting for transfers between devices, on_line_of_four(): lax.ppermute(p, 'tp', outward)  11.8 us
    ppermute x1, waiting for transfers between devices, on_line_of_four(): shares = [pair, lax.ppermute(pair, 'tp', [(i, i ^ 2) for i in range(4)])]  9.84 us
    ppermute x9, starting transfers between devices, swap(): return lax.ppermute(x, 'rep', [(r, r ^ distance) for r in range(rep)])  6.58 us
    pallas_call x2, Pallas kernels, pack(): pl.pallas_call(functools.partial(pack_kernel, count, cap), out_shape=[sha...  4.9 us
  transfers between devices with their start and end apart: 18, of which 8 were waited for; matrix products, arithmetic and copies ran while one was open for 2% of the time, Pallas kernels for 28%

profile of v7, /device:TPU:0, one launch (start us, length us, event | category | flops | bytes accessed | tf_op | source)
XLA Modules:
  0.0 149.4 jit_solution(2470213963757818238)
XLA Ops:
  0.0 3.0 %collective-permute-start = (bf16[512,2048]{1,0:T(8,128)(2,1)}, bf16[512,2048]{1,0:T(8,128)(2,1)S(1)}, u32[]{:S(2)}, u32[]{:S(2)}) collective-permute-start(bf16[512,2048]{1,0:T(8,128)(2,1)} %features.1), channel_id=1, source_target_pairs={{0,1},{1,0},{2,3},{3,2},{4,5},{5,4},{6,7},{7,6},{8,9},{9,8},{10,11... | collective-permute-start | bytes 6291464 | tf_op jit(solution)/shard_map/ppermute | solution.py:310
  3.0 2.0 %collective-permute-start.10 = (bf16[512,2048]{1,0:T(8,128)(2,1)}, bf16[512,2048]{1,0:T(8,128)(2,1)}, u32[]{:S(2)}, u32[]{:S(2)}) collective-permute-start(bf16[512,2048]{1,0:T(8,128)(2,1)} %features.1), channel_id=1, source_target_pairs={{1,2},{2,1},{5,6},{6,5},{9,10},{10,9},{13,14},{14,13},{17,18},{18,... | collective-permute-start | bytes 6291464 | tf_op jit(solution)/shard_map/ppermute | solution.py:311
  11.6 1.6 %copy-done.1 = bf16[32,16,2048]{2,1,0:T(8,128)(2,1)S(1)} copy-done((bf16[32,16,2048]{2,1,0:T(8,128)(2,1)S(1)}, bf16[32,16,2048]{2,1,0:T(8,128)(2,1)}, u32[]{:S(2)}) %copy-start.1) | copy-done | bytes 2097176
  13.2 1.9 %pack_blocks.3 = (bf16[8,16,2048]{2,1,0:T(8,128)(2,1)}, bf16[8,16,2048]{2,1,0:T(8,128)(2,1)}, bf16[8,16,2048]{2,1,0:T(8,128)(2,1)}) custom-call(s32[8]{0:T(128)S(1)} %collective-permute-done.1.refs_0_, s32[8]{0:T(128)S(1)} %collective-permute-done.2.refs_1_, s32[8]{0:T(128)S(1)} %collective-permute-done.3.refs_2_, bf16[32,16,2048]{2,1,0:T(8,128)(2,1)S(1)} %copy-done.1), custom_call_target="tpu_custom_call" | custom-call | bytes 3145728 | tf_op jit(solution)/shard_map/pack_blocks/pallas_call | solution.py:71
  17.7 1.6 %copy-done.4 = bf16[512,2048]{1,0:T(8,128)(2,1)S(1)} copy-done((bf16[512,2048]{1,0:T(8,128)(2,1)S(1)}, bf16[512,2048]{1,0:T(8,128)(2,1)}, u32[]{:S(2)}) %copy-start.4) | copy-done | bytes 2097176
  19.3 8.0 %add_part.5.refs_3_ = f32[512,2048]{1,0:T(8,128)S(1)} custom-call(s32[8]{0:T(128)S(1)} %dynamic-slice_bitcast_fusion.refs_0_.info, bf16[512,2048]{1,0:T(8,128)(2,1)S(1)} %copy-done.4, bf16[8192,2048]{1,0:T(8,128)(2,1)} %refs_3_.5), custom_call_target="tpu_custom_call" | custom-call | flops 4294967296 | bytes 16777216 | tf_op jit(solution)/shard_map/add_part/pallas_call | solution.py:232
  27.3 3.0 %pack_blocks.2 = (bf16[8,16,2048]{2,1,0:T(8,128)(2,1)S(1)}, bf16[8,16,2048]{2,1,0:T(8,128)(2,1)S(1)}, bf16[8,16,2048]{2,1,0:T(8,128)(2,1)S(1)}) custom-call(s32[8]{0:T(128)S(1)} %collective-permute-done.1.refs_0_, s32[8]{0:T(128)S(1)} %collective-permute-done.2.refs_1_, s32[8]{0:T(128)S(1)} %collective-permute-done.3.refs_2_, bf16[32,16,2048]{2,1,0:T(8,128)(2,1)S(1)} %copy-done.3), custom_call_target="tpu_custom_call" | custom-call | bytes 3145728 | tf_op jit(solution)/shard_map/pack_blocks/pallas_call | solution.py:71
  30.4 10.2 %collective-permute-done.6.refs_2_ = bf16[8,16,2048]{2,1,0:T(8,128)(2,1)} collective-permute-done((bf16[8,16,2048]{2,1,0:T(8,128)(2,1)}, bf16[8,16,2048]{2,1,0:T(8,128)(2,1)}, u32[]{:S(2)}, u32[]{:S(2)}) %collective-permute-start.6) | collective-permute-done | bytes 524320 | tf_op jit(solution)/shard_map/ppermute | solution.py:41
  40.6 3.7 %shrink.1 = f32[16,512]{1,0:T(8,128)S(1)} custom-call(s32[16]{0:T(128)S(1)} %get-tuple-element.34.source, s32[16]{0:T(128)S(1)} %get-tuple-element.41.place, bf16[512,2048]{1,0:T(8,128)(2,1)S(1)} %copy-done.4, bf16[32,16,2048]{2,1,0:T(8,128)(2,1)S(1)} %copy-done.2, bf16[8,16,2048]{2,1,0:T(8,128)(2,1)S(1)} %collective-permute-done.4.refs_0_, ...), custom_call_target="tpu_custom_call" | custom-call | flops 536870912 | bytes 2097152 | tf_op jit(solution)/shard_map/shrink/pallas_call | solution.py:133
  44.3 2.5 %collective-permute-start.7 = (f32[16,512]{1,0:T(8,128)S(1)}, f32[16,512]{1,0:T(8,128)S(1)}, u32[]{:S(2)}, u32[]{:S(2)}) collective-permute-start(f32[16,512]{1,0:T(8,128)S(1)} %shrink.1), channel_id=1, source_target_pairs={{0,1},{1,0},{2,3},{3,2},{4,5},{5,4},{6,7},{7,6},{8,9},{9,8},{10,11... | collective-permute-start | bytes 98312 | tf_op jit(solution)/shard_map/ppermute | solution.py:317
  46.8 2.8 %collective-permute-done.7 = f32[16,512]{1,0:T(8,128)S(1)} collective-permute-done((f32[16,512]{1,0:T(8,128)S(1)}, f32[16,512]{1,0:T(8,128)S(1)}, u32[]{:S(2)}, u32[]{:S(2)}) %collective-permute-start.7) | collective-permute-done | bytes 32800 | tf_op jit(solution)/shard_map/ppermute | solution.py:317
  51.8 8.0 %add_part.6.refs_4_ = f32[512,2048]{1,0:T(8,128)S(1)} custom-call(s32[8]{0:T(128)S(1)} %dynamic-slice_bitcast_fusion.refs_0_.info, bf16[512,2048]{1,0:T(8,128)(2,1)S(1)} %collective-permute-done.refs_1_, bf16[8192,2048]{1,0:T(8,128)(2,1)} %refs_3_.5, f32[512,2048]{1,0:T(8,128)S(1)} %add_part.5.refs_3_), custom_call_target="tpu_custom_call", output_to_operand_aliasing={{}: (3, {})} | custom-call | flops 4294967296 | bytes 16777216 | tf_op jit(solution)/shard_map/add_part/pallas_call | solution.py:232
  59.9 10.5 %copy-done = bf16[8192,2048]{1,0:T(8,128)(2,1)S(1)} copy-done((bf16[8192,2048]{1,0:T(8,128)(2,1)S(1)}, bf16[8192,2048]{1,0:T(8,128)(2,1)}, u32[]{:S(2)}) %copy-start) | copy-done | bytes 33554456
  72.8 1.7 %collective-permute-start.14 = (bf16[8,16,2048]{2,1,0:T(8,128)(2,1)S(1)}, bf16[8,16,2048]{2,1,0:T(8,128)(2,1)S(1)}, u32[]{:S(2)}, u32[]{:S(2)}) collective-permute-start(bf16[8,16,2048]{2,1,0:T(8,128)(2,1)S(1)} %get-tuple-element.37), channel_id=1, source_target_pairs={{0,8},{4,12},{8,0},{12,4},{1,9},{5,13},{9,1},{13,5},{2,10},{6,14},... | collective-permute-start | bytes 1572872 | tf_op jit(solution)/shard_map/ppermute | solution.py:41
  74.6 12.7 %collective-permute-done.14.refs_1_ = bf16[8,16,2048]{2,1,0:T(8,128)(2,1)S(1)} collective-permute-done((bf16[8,16,2048]{2,1,0:T(8,128)(2,1)S(1)}, bf16[8,16,2048]{2,1,0:T(8,128)(2,1)S(1)}, u32[]{:S(2)}, u32[]{:S(2)}) %collective-permute-start.14) | collective-permute-done | bytes 524320 | tf_op jit(solution)/shard_map/ppermute | solution.py:41
  88.9 18.2 %collective-permute-start.12 = (f32[16,512]{1,0:T(8,128)S(1)}, f32[16,512]{1,0:T(8,128)S(1)}, u32[]{:S(2)}, u32[]{:S(2)}) collective-permute-start(f32[16,512]{1,0:T(8,128)S(1)} %add.16.refs_5_), channel_id=1, source_target_pairs={{0,2},{1,3},{2,0},{3,1},{4,6},{5,7},{6,4},{7,5},{8,10},{9,11},{10,... | collective-permute-start | bytes 98312 | tf_op jit(solution)/shard_map/ppermute | solution.py:318
  107.1 2.8 %choose_blocks.1.refs_7_ = bf16[256,2048]{1,0:T(8,128)(2,1)S(1)} custom-call(s32[16]{0:T(128)S(1)} %get-tuple-element.34.source, s32[16]{0:T(128)S(1)} %get-tuple-element.41.place, bf16[32,16,2048]{2,1,0:T(8,128)(2,1)S(1)} %copy-done.3, bf16[8,16,2048]{2,1,0:T(8,128)(2,1)S(1)} %collective-permute-done.13.refs_0_, ...), custom_call_target="tpu_custom_call" | custom-call | bytes 2097152 | tf_op jit(solution)/shard_map/choose_blocks/pallas_call | solution.py:106
  110.0 1.3 collective-permute-start.9
  111.3 9.8 %collective-permute-done.12.refs_6_ = f32[16,512]{1,0:T(8,128)S(1)} collective-permute-done((f32[16,512]{1,0:T(8,128)S(1)}, f32[16,512]{1,0:T(8,128)S(1)}, u32[]{:S(2)}, u32[]{:S(2)}) %collective-permute-start.12) | collective-permute-done | bytes 32800 | tf_op jit(solution)/shard_map/ppermute | solution.py:318
  121.1 8.4 %add_part.7.refs_4_ = f32[512,2048]{1,0:T(8,128)S(1)} custom-call(s32[8]{0:T(128)S(1)} %dynamic-slice_bitcast_fusion.refs_0_.info, bf16[512,2048]{1,0:T(8,128)(2,1)} %collective-permute-done.10.refs_1_, bf16[512,2048]{1,0:T(8,128)(2,1)S(1)} %collective-permute-done.11.refs_2_, bf16[8192,2048]{1,0:T(8,128)(2,1)} %refs_3_.5, ...), custom_call_target="tpu_custom_call", output_to_operand_aliasing={{}: (4, {})} | custom-call | flops 4294967296 | bytes 16777216 | tf_op jit(solution)/shard_map/add_part/pallas_call | solution.py:232
  129.6 7.8 %collective-permute-done.17.refs_2_ = bf16[384,2048]{1,0:T(8,128)(2,1)S(1)} collective-permute-done((bf16[384,2048]{1,0:T(8,128)(2,1)S(1)}, bf16[384,2048]{1,0:T(8,128)(2,1)S(1)}, u32[]{:S(2)}, u32[]{:S(2)}) %collective-permute-start.17) | collective-permute-done | bytes 1572896 | tf_op jit(solution)/shard_map/ppermute | solution.py:326
  137.4 5.3 %add_part.8.refs_5_ = bf16[512,2048]{1,0:T(8,128)(2,1)} custom-call(s32[8]{0:T(128)S(1)} %dynamic-slice_bitcast_fusion.refs_0_.info, bf16[384,2048]{1,0:T(8,128)(2,1)S(1)} %collective-permute-done.16.refs_1_, bf16[384,2048]{1,0:T(8,128)(2,1)S(1)} %collective-permute-done.17.refs_2_, bf16[2048,2048]{1,0:T(8,128)(2,1)S(1)} %fetch_part.1.refs_3_, ...), custom_call_target="tpu_custom_call" | custom-call | flops 3221225472 | bytes 14680064 | tf_op jit(solution)/shard_map/add_part/pallas_call | solution.py:232
  142.7 4.0 %collective-permute-done.9.refs_2_ = bf16[128,2048]{1,0:T(8,128)(2,1)S(1)} collective-permute-done((bf16[128,2048]{1,0:T(8,128)(2,1)S(1)}, bf16[128,2048]{1,0:T(8,128)(2,1)S(1)}, u32[]{:S(2)}, u32[]{:S(2)}) %collective-permute-start.9) | collective-permute-done | bytes 524320 | tf_op jit(solution)/shard_map/ppermute | solution.py:326
  146.6 2.7 %add_part.9 = bf16[512,2048]{1,0:T(8,128)(2,1)} custom-call(s32[8]{0:T(128)S(1)} %dynamic-slice_bitcast_fusion.refs_0_.info, bf16[128,2048]{1,0:T(8,128)(2,1)S(1)} %collective-permute-done.8.refs_1_, bf16[128,2048]{1,0:T(8,128)(2,1)S(1)} %collective-permute-done.9.refs_2_, bf16[2048,2048]{1,0:T(8,128)(2,1)S(1)} %fetch_part.1.refs_3_, ...), custom_call_target="tpu_custom_call", output_to_operand_aliasing={{}: (5, {})} | custom-call | flops 1073741824 | bytes 10485760 | tf_op jit(solution)/shard_map/add_part/pallas_call | solution.py:232
  (41 shorter events, 15.6 us)
Async XLA Ops:
  0.0 49.6 %collective-permute-start = (bf16[512,2048]{1,0:T(8,128)(2,1)}, bf16[512,2048]{1,0:T(8,128)(2,1)S(1)}, u32[]{:S(2)}, u32[]{:S(2)}) collective-permute-start(bf16[512,2048]{1,0:T(8,128)(2,1)} %features.1), channel_id=1, source_target_pairs={{0,1},{1,0},{2,3},{3,2},{4,5},{5,4},{6,7},{7,6},{8,9},{9,8},{10,11... | collective-permute-start | bytes 6291464 | tf_op jit(solution)/shard_map/ppermute | solution.py:310
  3.0 47.4 %collective-permute-start.10 = (bf16[512,2048]{1,0:T(8,128)(2,1)}, bf16[512,2048]{1,0:T(8,128)(2,1)}, u32[]{:S(2)}, u32[]{:S(2)}) collective-permute-start(bf16[512,2048]{1,0:T(8,128)(2,1)} %features.1), channel_id=1, source_target_pairs={{1,2},{2,1},{5,6},{6,5},{9,10},{10,9},{13,14},{14,13},{17,18},{18,... | collective-permute-start | bytes 6291464 | tf_op jit(solution)/shard_map/ppermute | solution.py:311
  7.4 3.0 %collective-permute-start.3 = (s32[8]{0:T(128)S(1)}, s32[8]{0:T(128)S(1)}, u32[]{:S(2)}, u32[]{:S(2)}) collective-permute-start(s32[8]{0:T(128)S(1)} %get-tuple-element.43), channel_id=1, source_target_pairs={{0,12},{4,8},{8,4},{12,0},{1,13},{5,9},{9,5},{13,1},{2,14},{6,10},... | collective-permute-start | bytes 104 | tf_op jit(solution)/shard_map/ppermute | solution.py:41
  8.1 3.5 %collective-permute-start.2 = (s32[8]{0:T(128)S(1)}, s32[8]{0:T(128)S(1)}, u32[]{:S(2)}, u32[]{:S(2)}) collective-permute-start(s32[8]{0:T(128)S(1)} %get-tuple-element.44), channel_id=1, source_target_pairs={{0,8},{4,12},{8,0},{12,4},{1,9},{5,13},{9,1},{13,5},{2,10},{6,14},... | collective-permute-start | bytes 104 | tf_op jit(solution)/shard_map/ppermute | solution.py:41
  9.0 2.6 %collective-permute-start.1 = (s32[8]{0:T(128)S(1)}, s32[8]{0:T(128)S(1)}, u32[]{:S(2)}, u32[]{:S(2)}) collective-permute-start(s32[8]{0:T(128)S(1)} %get-tuple-element.45), channel_id=1, source_target_pairs={{0,4},{4,0},{8,12},{12,8},{1,5},{5,1},{9,13},{13,9},{2,6},{6,2},{1... | collective-permute-start | bytes 104 | tf_op jit(solution)/shard_map/ppermute | solution.py:41
  11.6 1.6 %copy-start.1 = (bf16[32,16,2048]{2,1,0:T(8,128)(2,1)S(1)}, bf16[32,16,2048]{2,1,0:T(8,128)(2,1)}, u32[]{:S(2)}) copy-start(bf16[32,16,2048]{2,1,0:T(8,128)(2,1)} %pool.2) | copy-start | bytes 6291460
  15.1 15.3 %collective-permute-start.4 = (bf16[8,16,2048]{2,1,0:T(8,128)(2,1)}, bf16[8,16,2048]{2,1,0:T(8,128)(2,1)S(1)}, u32[]{:S(2)}, u32[]{:S(2)}) collective-permute-start(bf16[8,16,2048]{2,1,0:T(8,128)(2,1)} %get-tuple-element.27), channel_id=1, source_target_pairs={{0,4},{4,0},{8,12},{12,8},{1,5},{5,1},{9,13},{13,9},{2,6},{6,2},{1... | collective-permute-start | bytes 1572872 | tf_op jit(solution)/shard_map/ppermute | solution.py:41
  15.3 15.1 %collective-permute-start.5 = (bf16[8,16,2048]{2,1,0:T(8,128)(2,1)}, bf16[8,16,2048]{2,1,0:T(8,128)(2,1)S(1)}, u32[]{:S(2)}, u32[]{:S(2)}) collective-permute-start(bf16[8,16,2048]{2,1,0:T(8,128)(2,1)} %get-tuple-element.28), channel_id=1, source_target_pairs={{0,8},{4,12},{8,0},{12,4},{1,9},{5,13},{9,1},{13,5},{2,10},{6,14},... | collective-permute-start | bytes 1572872 | tf_op jit(solution)/shard_map/ppermute | solution.py:41
  16.2 24.4 %collective-permute-start.6 = (bf16[8,16,2048]{2,1,0:T(8,128)(2,1)}, bf16[8,16,2048]{2,1,0:T(8,128)(2,1)}, u32[]{:S(2)}, u32[]{:S(2)}) collective-permute-start(bf16[8,16,2048]{2,1,0:T(8,128)(2,1)} %get-tuple-element.29), channel_id=1, source_target_pairs={{0,12},{4,8},{8,4},{12,0},{1,13},{5,9},{9,5},{13,1},{2,14},{6,10},... | collective-permute-start | bytes 1572872 | tf_op jit(solution)/shard_map/ppermute | solution.py:41
  17.7 1.6 %copy-start.4 = (bf16[512,2048]{1,0:T(8,128)(2,1)S(1)}, bf16[512,2048]{1,0:T(8,128)(2,1)}, u32[]{:S(2)}) copy-start(bf16[512,2048]{1,0:T(8,128)(2,1)} %features.1) | copy-start | bytes 6291460
  19.3 8.0 %copy-start.3 = (bf16[32,16,2048]{2,1,0:T(8,128)(2,1)S(1)}, bf16[32,16,2048]{2,1,0:T(8,128)(2,1)}, u32[]{:S(2)}) copy-start(bf16[32,16,2048]{2,1,0:T(8,128)(2,1)} %pool.3) | copy-start | bytes 6291460
  27.3 13.3 %copy-start.2 = (bf16[32,16,2048]{2,1,0:T(8,128)(2,1)S(1)}, bf16[32,16,2048]{2,1,0:T(8,128)(2,1)}, u32[]{:S(2)}) copy-start(bf16[32,16,2048]{2,1,0:T(8,128)(2,1)} %pool.2) | copy-start | bytes 6291460
  44.3 5.3 %collective-permute-start.7 = (f32[16,512]{1,0:T(8,128)S(1)}, f32[16,512]{1,0:T(8,128)S(1)}, u32[]{:S(2)}, u32[]{:S(2)}) collective-permute-start(f32[16,512]{1,0:T(8,128)S(1)} %shrink.1), channel_id=1, source_target_pairs={{0,1},{1,0},{2,3},{3,2},{4,5},{5,4},{6,7},{7,6},{8,9},{9,8},{10,11... | collective-permute-start | bytes 98312 | tf_op jit(solution)/shard_map/ppermute | solution.py:317
  49.7 21.8 %collective-permute-start.16 = (bf16[384,2048]{1,0:T(8,128)(2,1)S(1)}, bf16[384,2048]{1,0:T(8,128)(2,1)S(1)}, u32[]{:S(2)}, u32[]{:S(2)}) collective-permute-start(bf16[384,2048]{1,0:T(8,128)(2,1)S(1)} %slice.22), channel_id=1, source_target_pairs={{1,2},{2,1},{5,6},{6,5},{9,10},{10,9},{13,14},{14,13},{17,18},{18,... | collective-permute-start | bytes 4718600 | tf_op jit(solution)/shard_map/ppermute | solution.py:322
  50.5 70.7 %collective-permute-start.11 = (bf16[512,2048]{1,0:T(8,128)(2,1)}, bf16[512,2048]{1,0:T(8,128)(2,1)S(1)}, u32[]{:S(2)}, u32[]{:S(2)}) collective-permute-start(bf16[512,2048]{1,0:T(8,128)(2,1)} %collective-permute-done.10.refs_1_), channel_id=1, source_target_pairs={{1,0},{2,3},{5,4},{6,7},{9,8},{10,11},{13,12},{14,15},{17,16},{18,... | collective-permute-start | bytes 6291464 | tf_op jit(solution)/shard_map/ppermute | solution.py:321
  51.8 21.1 %collective-permute-start.13 = (bf16[8,16,2048]{2,1,0:T(8,128)(2,1)S(1)}, bf16[8,16,2048]{2,1,0:T(8,128)(2,1)S(1)}, u32[]{:S(2)}, u32[]{:S(2)}) collective-permute-start(bf16[8,16,2048]{2,1,0:T(8,128)(2,1)S(1)} %get-tuple-element.35), channel_id=1, source_target_pairs={{0,4},{4,0},{8,12},{12,8},{1,5},{5,1},{9,13},{13,9},{2,6},{6,2},{1... | collective-permute-start | bytes 1572872 | tf_op jit(solution)/shard_map/ppermute | solution.py:41
  59.8 10.5 %copy-start = (bf16[8192,2048]{1,0:T(8,128)(2,1)S(1)}, bf16[8192,2048]{1,0:T(8,128)(2,1)}, u32[]{:S(2)}) copy-start(bf16[8192,2048]{1,0:T(8,128)(2,1)} %refs_3_.5) | copy-start | bytes 100663296
  71.5 65.9 %collective-permute-start.17 = (bf16[384,2048]{1,0:T(8,128)(2,1)S(1)}, bf16[384,2048]{1,0:T(8,128)(2,1)S(1)}, u32[]{:S(2)}, u32[]{:S(2)}) collective-permute-start(bf16[384,2048]{1,0:T(8,128)(2,1)S(1)} %collective-permute-done.16.refs_1_), channel_id=1, source_target_pairs={{1,0},{2,3},{5,4},{6,7},{9,8},{10,11},{13,12},{14,15},{17,16},{18,... | collective-permute-start | bytes 4718600 | tf_op jit(solution)/shard_map/ppermute | solution.py:326
  72.8 14.4 %collective-permute-start.14 = (bf16[8,16,2048]{2,1,0:T(8,128)(2,1)S(1)}, bf16[8,16,2048]{2,1,0:T(8,128)(2,1)S(1)}, u32[]{:S(2)}, u32[]{:S(2)}) collective-permute-start(bf16[8,16,2048]{2,1,0:T(8,128)(2,1)S(1)} %get-tuple-element.37), channel_id=1, source_target_pairs={{0,8},{4,12},{8,0},{12,4},{1,9},{5,13},{9,1},{13,5},{2,10},{6,14},... | collective-permute-start | bytes 1572872 | tf_op jit(solution)/shard_map/ppermute | solution.py:41
  87.2 19.9 %collective-permute-start.15 = (bf16[8,16,2048]{2,1,0:T(8,128)(2,1)S(1)}, bf16[8,16,2048]{2,1,0:T(8,128)(2,1)S(1)}, u32[]{:S(2)}, u32[]{:S(2)}) collective-permute-start(bf16[8,16,2048]{2,1,0:T(8,128)(2,1)S(1)} %get-tuple-element.39), channel_id=1, source_target_pairs={{0,12},{4,8},{8,4},{12,0},{1,13},{5,9},{9,5},{13,1},{2,14},{6,10},... | collective-permute-start | bytes 1572872 | tf_op jit(solution)/shard_map/ppermute | solution.py:41
  88.2 21.8 %collective-permute-start.8 = (bf16[128,2048]{1,0:T(8,128)(2,1)S(1)}, bf16[128,2048]{1,0:T(8,128)(2,1)S(1)}, u32[]{:S(2)}, u32[]{:S(2)}) collective-permute-start(bf16[128,2048]{1,0:T(8,128)(2,1)S(1)} %slice.21), channel_id=1, source_target_pairs={{1,2},{2,1},{5,6},{6,5},{9,10},{10,9},{13,14},{14,13},{17,18},{18,... | collective-permute-start | bytes 1572872 | tf_op jit(solution)/shard_map/ppermute | solution.py:322
  88.9 32.2 %collective-permute-start.12 = (f32[16,512]{1,0:T(8,128)S(1)}, f32[16,512]{1,0:T(8,128)S(1)}, u32[]{:S(2)}, u32[]{:S(2)}) collective-permute-start(f32[16,512]{1,0:T(8,128)S(1)} %add.16.refs_5_), channel_id=1, source_target_pairs={{0,2},{1,3},{2,0},{3,1},{4,6},{5,7},{6,4},{7,5},{8,10},{9,11},{10,... | collective-permute-start | bytes 98312 | tf_op jit(solution)/shard_map/ppermute | solution.py:318
  110.0 36.6 %collective-permute-start.9 = (bf16[128,2048]{1,0:T(8,128)(2,1)S(1)}, bf16[128,2048]{1,0:T(8,128)(2,1)S(1)}, u32[]{:S(2)}, u32[]{:S(2)}) collective-permute-start(bf16[128,2048]{1,0:T(8,128)(2,1)S(1)} %collective-permute-done.8.refs_1_), channel_id=1, source_target_pairs={{1,0},{2,3},{5,4},{6,7},{9,8},{10,11},{13,12},{14,15},{17,16},{18,... | collective-permute-start | bytes 1572872 | tf_op jit(solution)/shard_map/ppermute | solution.py:326
